TPU v7x, 32 devices: a whole 2x2x4 slice. The times are simulated.
32 devices in a mesh: inst: 4 (over x, core), zone: 8 (over z, y).
Axes of the slice: x: 2, y: 2, z: 4, core: 2. Of those that a mesh axis runs over, the one named last changes fastest.
Arguments:
- state: float32 [4, 1024, 320], P('inst', 'zone'), may hold values from -6 to 6
- source: float32 [4, 1024, 320], P('inst', 'zone'), may hold values from -6 to 6
- jac_table: bfloat16 [64, 320, 320], P('zone'), may hold values from -0.3125 to 0.3125
- pattern_col: int32 [1024, 4], P('zone'), may hold values from 0 to 127
- pattern_type: int32 [1024, 4], P('zone'), may hold values from 0 to 7
- pseudo_step: float32 [4, 1024], P('inst', 'zone'), may hold values from 0.05 to 0.4
- zone_count: int32 [8], P('zone'), may hold values from 64 to 128, as said below
- link_src: int32 [4, 256], P('inst', 'zone'), may hold values from 0 to 127
- link_owner: int32 [4, 256, 1], P('inst', 'zone'), may hold values from 0 to 7; in each aligned block of 32 rows (0 to 31, 32 to 63, ..., all dimensions but the last counted through in order) at most 8 rows name the same one
- link_dest: int32 [4, 256], P('inst', 'zone'), may hold values from 0 to 127
- link_weight: int32 [4, 256], P('inst', 'zone'), may hold values from 0 to 15
- iface_table: float32 [16, 320], replicated, may hold values from 0.5 to 1.5
Outputs:
- updated: float32 [4, 1024, 320], P('inst', 'zone')
- residual: float32 [4, 1024, 320], P('inst', 'zone')
Inputs may be any that keep to these rules, and one draw needn't show every extreme that they name: `link_owner`: among the 32 links of one zone at one instance, no owner zone is named more than 8 times; in some of them one zone is named exactly 8 times. `zone_count`: some zone uses all 128 clusters.
All inputs are finite; a program needn't handle non-finite values.
Results may differ from a plain program's by a relative error of at most 0.0014.
Values sent between devices are 32-bit elements; how exact they have to be, the bound alone decides.
No kernel may reach another device: no remote copies, remote signals or barrier semaphores. Data moves between devices by JAX's collectives and lax.ppermute only.
A program may use at most 64 MiB of HBM per device.

v0:
```python
import math

import jax
import jax.numpy as jnp
from jax import lax
from jax.sharding import PartitionSpec as P

OMEGA = 0.25
NU = 0.1


def passed_along(value, axis, steps):
    count = lax.axis_size(axis)
    pairs = [(source, (source + steps) % count) for source in range(count)]
    return lax.ppermute(value, axis, pairs)


def coefficient(shift_steps, period):
    steps_f = shift_steps.astype(jnp.float32)
    parity = 1.0 - 2.0 * (shift_steps % 2).astype(jnp.float32)
    phase = math.pi * steps_f / period
    sine_safe = jnp.where(shift_steps == 0, 1.0, jnp.sin(phase))
    derive = OMEGA * parity * jnp.cos(phase) / sine_safe
    damping = NU * parity / (2.0 * sine_safe * sine_safe)
    centre = NU * (period * period + 2) / 12.0
    return jnp.where(shift_steps == 0, centre, derive + damping)


def shift_upper(moving):
    return passed_along(moving, "inst", 1)


def shift_lower(moving):
    return passed_along(moving, "inst", -1)


def on_device(
    state,
    source,
    jac_table,
    pattern_col,
    pattern_type,
    pseudo_step,
    zone_count,
    link_src,
    link_owner,
    link_dest,
    link_weight,
    iface_table,
):
    instances = lax.axis_size("inst")
    zones = lax.axis_size("zone")
    local_state = state[0]
    clusters, width = local_state.shape
    kinds = jac_table.shape[0]
    state_half = local_state.astype(jnp.bfloat16)
    table_flat = jac_table.reshape(kinds * width, width)
    products = lax.dot_general(
        state_half, table_flat, (((1,), (1,)), ((), ())), preferred_element_type=jnp.float32
    )
    products = products.reshape(clusters * kinds, width)
    entry_rows = pattern_col * kinds + pattern_type
    jac_term = jnp.sum(products[entry_rows], axis=1)
    centre_weight = coefficient(jnp.zeros((), jnp.int32), instances)

    def two_turn(steps, carry):
        accum, upper, lower = carry
        upper = shift_upper(upper)
        lower = shift_lower(lower)
        accum = (
            accum
            + coefficient(steps, instances) * upper
            + coefficient(instances - steps, instances) * lower
        )
        return (accum, upper, lower)

    accum, upper, lower = lax.fori_loop(
        1, instances // 2, two_turn, (centre_weight * local_state, local_state, local_state)
    )
    upper = shift_upper(upper)
    time_term = accum + coefficient(jnp.asarray(instances // 2, jnp.int32), instances) * upper
    links = link_src.shape[1]
    slots_per = 2 * links // zones
    link_sources = link_src[0]
    link_owners = link_owner[0, :, 0]
    link_targets = link_dest[0]
    weight_sets = iface_table.shape[0]
    choose_sets = (
        link_weight[0][:, None] == jnp.arange(weight_sets, dtype=jnp.int32)[None, :]
    ).astype(jnp.float32)
    scales = jnp.dot(choose_sets, iface_table, precision=lax.Precision.HIGHEST)
    blocks = local_state[link_sources] * scales
    cluster_ids = jnp.arange(clusters, dtype=jnp.int32)
    owner_hits = (link_owners[:, None] == jnp.arange(zones, dtype=jnp.int32)[None, :]).astype(
        jnp.int32
    )
    order_rank = jnp.sum(jnp.cumsum(owner_hits, axis=0) * owner_hits, axis=1) - 1
    slot_ids = link_owners * slots_per + order_rank
    placing = (jnp.arange(zones * slots_per, dtype=jnp.int32)[:, None] == slot_ids[None, :]).astype(
        jnp.float32
    )
    outgoing = jnp.dot(placing, blocks, precision=lax.Precision.HIGHEST)
    outgoing_targets = jnp.sum(placing * link_targets.astype(jnp.float32)[None, :], axis=1)
    incoming, incoming_targets = (
        lax.all_to_all(outgoing, "zone", split_axis=0, concat_axis=0, tiled=True),
        lax.all_to_all(outgoing_targets, "zone", split_axis=0, concat_axis=0, tiled=True),
    )
    landing = (cluster_ids[:, None] == incoming_targets.astype(jnp.int32)[None, :]).astype(
        jnp.float32
    )
    iface = jnp.dot(landing, incoming, precision=lax.Precision.HIGHEST)
    active = cluster_ids < zone_count[0]
    residual = jnp.where(
        active[:, None], source[0] + jac_term + time_term - iface, jnp.float32(0.0)
    )
    updated = local_state - pseudo_step[0][:, None] * residual
    return (updated[None], residual[None])


def solution(mesh):
    placed = (
        P("inst", "zone", None),
        P("inst", "zone", None),
        P("zone", None, None),
        P("zone", None),
        P("zone", None),
        P("inst", "zone"),
        P("zone"),
        P("inst", "zone"),
        P("inst", "zone", None),
        P("inst", "zone"),
        P("inst", "zone"),
        P(),
    )
    return jax.shard_map(
        on_device,
        mesh=mesh,
        in_specs=placed,
        out_specs=(P("inst", "zone", None), P("inst", "zone", None)),
        check_vma=False,
    )
```

profile of v0, /device:TPU:0, one launch (start us, length us, event | category | flops | bytes accessed | tf_op | source)
XLA Modules:
  0.0 40.3 jit_solution(10011502312715581987)
XLA Ops:
  0.6 0.5 %collective-permute-start = (f32[128,320]{0,1:T(8,128)}, f32[128,320]{0,1:T(8,128)}, u32[]{:S(2)}, u32[]{:S(2)}) collective-permute-start(f32[128,320]{0,1:T(8,128)} %bitcast.42), channel_id=1, source_target_pairs={{0,8},{8,16},{16,24},{24,0},{1,9},{9,17},{17,25},{25,1},{2,10},{10... | collective-permute-start | bytes 491528 | tf_op jit(solution)/shard_map/while/body/eval_jaxpr/ppermute | solution.py:15
  1.1 2.0 %collective-permute-start.1 = (f32[128,320]{0,1:T(8,128)}, f32[128,320]{0,1:T(8,128)}, u32[]{:S(2)}, u32[]{:S(2)}) collective-permute-start(f32[128,320]{0,1:T(8,128)} %bitcast.43), channel_id=1, source_target_pairs={{0,24},{8,0},{16,8},{24,16},{1,25},{9,1},{17,9},{25,17},{2,26},{10... | collective-permute-start | bytes 491528 | tf_op jit(solution)/shard_map/while/body/eval_jaxpr/ppermute | solution.py:15
  3.1 0.7 %fusion.9 = s32[32,8]{1,0:T(8,128)S(1)} fusion(s32[32]{0:T(128)} %bitcast.46), kind=kLoop, calls=%fused_computation.20 | loop fusion | flops 512 | bytes 1152 | tf_op jit(solution)/shard_map/convert_element_type | solution.py:94
  3.9 0.8 %select_reduce_fusion.1 = s32[32]{0:T(128)S(1)} fusion(s32[32,8]{1,0:T(8,128)S(1)} %reduce_window_sum.11, s32[32]{0:T(128)} %bitcast.47), kind=kLoop, calls=%fused_computation.18 | loop fusion | flops 736 | bytes 1280 | tf_op jit(solution)/shard_map/reduce_sum | solution.py:97
  4.8 0.7 %add_add_fusion = s32[32]{0:T(128)S(1)} fusion(s32[32]{0:T(128)S(1)} %select_reduce_fusion.1, s32[1,32,1]{1,2,0:T(1,128)} %param.20), kind=kLoop, calls=%fused_computation.31 | loop fusion | flops 96 | bytes 384 | tf_op jit(solution)/shard_map/add | solution.py:98
  5.4 0.7 %convert_bitcast_fusion = f32[32]{0:T(128)S(1)} fusion(s32[1,32]{1,0:T(1,128)} %param.21), kind=kLoop, calls=%fused_computation.30 | loop fusion | flops 32 | bytes 256 | tf_op jit(solution)/shard_map/mul | solution.py:103
  6.2 0.7 %all_to_all.14 = f32[8,8,1]{1,0,2:T(8,128)} reshape(f32[64]{0:T(128)S(1)} %select_reduce_fusion) | data formatting | bytes 512 | tf_op jit(solution)/shard_map/all_to_all | solution.py:106
  6.9 6.6 %all-to-all-start = ((f32[8,8,1]{1,2,0:T(1,128)}), f32[8,8,1]{1,2,0:T(1,128)S(1)}, u32[]{:S(2)}, u32[]{:S(2)}) async-start(f32[8,8,1]{1,2,0:T(1,128)} %bitcast.8), calls=%async_computation | async-start | bytes 8192 | tf_op jit(solution)/shard_map/all_to_all | solution.py:106
  13.4 1.0 %copy.24 = f32[128,320]{1,0:T(8,128)S(1)} copy(f32[128,320]{0,1:T(8,128)} %bitcast.44) | data formatting | bytes 327680 | tf_op jit(solution)/shard_map/squeeze | solution.py:53
  14.5 0.7 %fusion.12 = s32[32]{0:T(128)S(1)} fusion(s32[1,32]{1,0:T(1,128)} %param.19), kind=kLoop, calls=%fused_computation.29 | loop fusion | flops 96 | bytes 256 | tf_op jit(solution)/shard_map/select_n | solution.py:92
  15.2 0.6 %gather_fusion.1 = f32[32,320]{1,0:T(8,128)S(1)} fusion(f32[128,320]{1,0:T(8,128)S(1)} %copy.24, s32[1024]{0:T(1024)S(1)} %pad_clamp_fusion), kind=kCustom, calls=%fused_computation.1 | custom fusion | bytes 82048 | tf_op jit(solution)/shard_map/gather | solution.py:92
  15.8 1.0 %convolution_multiply_fusion = f32[32,320]{1,0:T(8,128)S(1)} fusion(f32[32,320]{1,0:T(8,128)S(1)} %gather_fusion.1, f32[16,320]{1,0:T(8,128)} %param.23, s32[32]{0:T(128)} %bitcast.49), kind=kOutput, calls=%fused_computation.3 | convolution fusion | flops 1976832 | bytes 102528 | tf_op jit(solution)/shard_map/dot_general | solution.py:91
  16.8 1.0 %convolution_bitcast_fusion = f32[8,8,320]{2,1,0:T(8,128)} fusion(f32[32,320]{1,0:T(8,128)S(1)} %convolution_multiply_fusion, s32[32]{0:T(128)S(1)} %add_add_fusion), kind=kOutput, calls=%fused_computation.2 | convolution fusion | flops 7866368 | bytes 123008 | tf_op jit(solution)/shard_map/dot_general | solution.py:102
  17.7 2.7 %fusion.5 = f32[128,2560]{1,0:T(8,128)} fusion(bf16[2560,320]{1,0:T(8,128)(2,1)S(1)} %bitcast.41, f32[1,128,320]{1,2,0:T(8,128)} %param.12), kind=kOutput, calls=%fused_computation.11 | convolution fusion | flops 209756160 | bytes 3112960 | tf_op jit(solution)/shard_map/dot_general | solution.py:58
  20.5 0.1 copy.21
  21.4 6.0 %all-to-all-start.1 = ((f32[8,8,320]{2,1,0:T(8,128)}), f32[8,8,320]{2,1,0:T(8,128)}, u32[]{:S(2)}, u32[]{:S(2)}) async-start(f32[8,8,320]{2,1,0:T(8,128)} %convolution_bitcast_fusion), calls=%async_computation.1 | async-start | bytes 196608 | tf_op jit(solution)/shard_map/all_to_all | solution.py:105
  27.4 1.7 %reshape.66 = f32[1024,320]{1,0:T(8,128)S(1)} reshape(f32[128,2560]{1,0:T(8,128)} %fusion.5) | data formatting | bytes 2621440 | tf_op jit(solution)/shard_map/reshape | solution.py:61
  29.1 2.3 %gather_fusion = f32[512,320]{1,0:T(8,128)} fusion(f32[1024,320]{1,0:T(8,128)S(1)} %reshape.66, s32[1024]{0:T(1024)S(1)} %pad_clamp_fusion.1), kind=kCustom, calls=%fused_computation | custom fusion | bytes 1312768 | tf_op jit(solution)/shard_map/gather | solution.py:63
  31.4 1.4 %reshape.72 = f32[128,4,320]{2,1,0:T(4,128)S(1)} reshape(f32[512,320]{1,0:T(8,128)} %gather_fusion) | data formatting | bytes 1310720 | tf_op jit(solution)/shard_map/gather | solution.py:63
  32.8 0.5 %reduce_sum.27 = f32[128,320]{1,0:T(8,128)S(1)} reduce(f32[128,4,320]{2,1,0:T(4,128)S(1)} %reshape.72, f32[]{:T(128)} %constant.137.clone.1), dimensions={1}, to_apply=%region_0.0 | reduce | flops 122880 | bytes 819204 | tf_op jit(solution)/shard_map/reduce_sum | solution.py:63
  33.6 1.0 %all-to-all-done.1 = f32[8,8,320]{2,1,0:T(8,128)} async-done(((f32[8,8,320]{2,1,0:T(8,128)}), f32[8,8,320]{2,1,0:T(8,128)}, u32[]{:S(2)}, u32[]{:S(2)}) %all-to-all-start.1) | async-done | bytes 81952 | tf_op jit(solution)/shard_map/all_to_all | solution.py:105
  34.6 1.2 %fusion.3 = f32[128,320]{0,1:T(8,128)S(1)} fusion(f32[8,8,320]{2,1,0:T(8,128)} %all-to-all-done.1, s32[64]{0:T(128)S(1)} %convert_element_type.41), kind=kOutput, calls=%fused_computation.9 | convolution fusion | flops 31465472 | bytes 246016 | tf_op jit(solution)/shard_map/dot_general | solution.py:111
  35.8 2.7 %collective-permute-done.2 = f32[128,320]{0,1:T(8,128)S(1)} collective-permute-done((f32[128,320]{0,1:T(8,128)}, f32[128,320]{0,1:T(8,128)S(1)}, u32[]{:S(2)}, u32[]{:S(2)}) %collective-permute-start.2) | collective-permute-done | bytes 163872 | tf_op jit(solution)/shard_map/ppermute | solution.py:15
  38.5 1.8 %subtract_bitcast_fusion = (f32[1,128,320]{1,2,0:T(8,128)}, f32[128,320]{0,1:T(8,128)}) fusion(f32[128]{0:T(128)S(1)} %bitcast.48, f32[1,128,320]{1,2,0:T(8,128)S(1)} %copy-done.1, f32[128,320]{0,1:T(8,128)S(1)} %fusion.3, f32[128,320]{0,1:T(8,128)S(1)} %collective-permute-done.2, f32[128,320]{0,1:T(8,128)} %collective-permute-done.1, ...), kind=kLoop, calls=%fused_computation.8 | loop fusion | flops 532480 | bytes 1475200 | tf_op jit(solution)/shard_map/broadcast_in_dim | solution.py:117
  (26 shorter events, 0.6 us)
Async XLA Ops:
  0.6 17.1 %copy-start = (bf16[8,320,320]{2,1,0:T(8,128)(2,1)S(1)}, bf16[8,320,320]{2,1,0:T(8,128)(2,1)}, u32[]{:S(2)}) copy-start(bf16[8,320,320]{2,1,0:T(8,128)(2,1)} %param.14) | copy-start | bytes 4915204
  0.6 32.9 %collective-permute-start = (f32[128,320]{0,1:T(8,128)}, f32[128,320]{0,1:T(8,128)}, u32[]{:S(2)}, u32[]{:S(2)}) collective-permute-start(f32[128,320]{0,1:T(8,128)} %bitcast.42), channel_id=1, source_target_pairs={{0,8},{8,16},{16,24},{24,0},{1,9},{9,17},{17,25},{25,1},{2,10},{10... | collective-permute-start | bytes 491528 | tf_op jit(solution)/shard_map/while/body/eval_jaxpr/ppermute | solution.py:15
  1.1 34.7 %collective-permute-start.1 = (f32[128,320]{0,1:T(8,128)}, f32[128,320]{0,1:T(8,128)}, u32[]{:S(2)}, u32[]{:S(2)}) collective-permute-start(f32[128,320]{0,1:T(8,128)} %bitcast.43), channel_id=1, source_target_pairs={{0,24},{8,0},{16,8},{24,16},{1,25},{9,1},{17,9},{25,17},{2,26},{10... | collective-permute-start | bytes 491528 | tf_op jit(solution)/shard_map/while/body/eval_jaxpr/ppermute | solution.py:15
  6.9 14.5 %all-to-all-start = ((f32[8,8,1]{1,2,0:T(1,128)}), f32[8,8,1]{1,2,0:T(1,128)S(1)}, u32[]{:S(2)}, u32[]{:S(2)}) async-start(f32[8,8,1]{1,2,0:T(1,128)} %bitcast.8), calls=%async_computation | async-start | bytes 8192 | tf_op jit(solution)/shard_map/all_to_all | solution.py:106
  15.8 4.7 %copy-start.3 = (s32[128,4]{0,1:T(4,128)S(1)}, s32[128,4]{0,1:T(4,128)}, u32[]{:S(2)}) copy-start(s32[128,4]{0,1:T(4,128)} %param.16) | copy-start | bytes 6148
  15.8 4.7 %copy-start.4 = (s32[128,4]{0,1:T(4,128)S(1)}, s32[128,4]{0,1:T(4,128)}, u32[]{:S(2)}) copy-start(s32[128,4]{0,1:T(4,128)} %param.15) | copy-start | bytes 6148
  21.4 13.2 %all-to-all-start.1 = ((f32[8,8,320]{2,1,0:T(8,128)}), f32[8,8,320]{2,1,0:T(8,128)}, u32[]{:S(2)}, u32[]{:S(2)}) async-start(f32[8,8,320]{2,1,0:T(8,128)} %convolution_bitcast_fusion), calls=%async_computation.1 | async-start | bytes 196608 | tf_op jit(solution)/shard_map/all_to_all | solution.py:105
  31.4 7.1 %copy-start.1 = (f32[1,128,320]{1,2,0:T(8,128)S(1)}, f32[1,128,320]{1,2,0:T(8,128)}, u32[]{:S(2)}) copy-start(f32[1,128,320]{1,2,0:T(8,128)} %param.12) | copy-start | bytes 491524
  31.4 7.1 %copy-start.2 = (f32[1,128,320]{1,2,0:T(8,128)S(1)}, f32[1,128,320]{1,2,0:T(8,128)}, u32[]{:S(2)}) copy-start(f32[1,128,320]{1,2,0:T(8,128)} %param.13) | copy-start | bytes 491524
  31.4 7.1 %copy-start.5 = (f32[1,128]{1,0:T(1,128)S(1)}, f32[1,128]{1,0:T(1,128)}, u32[]{:S(2)}) copy-start(f32[1,128]{1,0:T(1,128)} %param.17) | copy-start | bytes 1540
  33.5 5.0 %collective-permute-start.2 = (f32[128,320]{0,1:T(8,128)}, f32[128,320]{0,1:T(8,128)S(1)}, u32[]{:S(2)}, u32[]{:S(2)}) collective-permute-start(f32[128,320]{0,1:T(8,128)} %collective-permute-done), channel_id=1, source_target_pairs={{0,8},{8,16},{16,24},{24,0},{1,9},{9,17},{17,25},{25,1},{2,10},{10... | collective-permute-start | bytes 491528 | tf_op jit(solution)/shard_map/ppermute | solution.py:15
where the time goes:
time: 40.8 us; the launch traced here: 40.3 us
  starting transfers between devices  15.1 us (37%)
  local copies, waits for them, and re-layouts  8.16 us (20%)
  other arithmetic  5.99 us (15%)
  matrix products  5.89 us (14%)
  waiting for transfers between devices  3.72 us (9%)
  between operations  1.41 us (3%)
    all_to_all x1, starting transfers between devices, on_device(): lax.all_to_all(outgoing_targets, 'zone', split_axis=0, concat_axis=0, til...  6.58 us
    all_to_all x1, starting transfers between devices, on_device(): lax.all_to_all(outgoing, 'zone', split_axis=0, concat_axis=0, tiled=True)  6 us
    gather x2, local copies, waits for them, and re-layouts, on_device(): jac_term = jnp.sum(products[entry_rows], axis=1)  3.69 us
    dot_general x1, matrix products, on_device(): lax.dot_general(state_half, table_flat, (((1,), (1,)), ((), ())), preferr...  2.74 us
    ppermute x3, waiting for transfers between devices, passed_along(): return lax.ppermute(value, axis, pairs)  2.68 us
    ppermute x3, starting transfers between devices, passed_along(): return lax.ppermute(value, axis, pairs)  2.55 us
    broadcast_in_dim x1, other arithmetic, on_device(): return (updated[None], residual[None])  1.79 us
    reshape x1, local copies, waits for them, and re-layouts, on_device(): products = products.reshape(clusters * kinds, width)  1.72 us
  transfers between devices with their start and end apart: 5, of which 2 were waited for; matrix products, arithmetic and copies ran while one was open for 44% of the time, Pallas kernels for 0%

commit v1 on v0

v1 whole, which is shorter than its diff:
```python
import functools
import math

import jax
import jax.numpy as jnp
import numpy as np
from jax import lax
from jax.experimental import pallas as pl
from jax.experimental.pallas import tpu as pltpu
from jax.sharding import PartitionSpec as P

OMEGA = 0.25
NU = 0.1
LANES = 128
VMEM = pl.BlockSpec(memory_space=pltpu.VMEM)
SMEM = pl.BlockSpec(memory_space=pltpu.SMEM)


def coefficients(period):
    table = [NU * (period * period + 2) / 12.0]
    for shift in range(1, period):
        phase = math.pi * shift / period
        sign = -1.0 if shift % 2 else 1.0
        sine = math.sin(phase)
        table.append(OMEGA * sign * math.cos(phase) / sine + NU * sign / (2.0 * sine * sine))
    return [float(np.float32(entry)) for entry in table]


def chosen(table, index):
    value = jnp.float32(table[0])
    for position in range(1, len(table)):
        value = jnp.where(index == position, jnp.float32(table[position]), value)
    return value


def parts_of(value):
    high = value.astype(jnp.bfloat16)
    rest = value - high.astype(jnp.float32)
    middle = rest.astype(jnp.bfloat16)
    low = (rest - middle.astype(jnp.float32)).astype(jnp.bfloat16)
    return high, middle, low


def power_of_two(count):
    return count & (count - 1) == 0


def radices_of(zones):
    radices = []
    rest = zones
    while rest > 1:
        step = 2 if not radices or rest == 2 else 4
        radices.append(step)
        rest //= step
    return radices


def block_of(relative, radices):
    place = jnp.zeros_like(relative)
    shift = 0
    for radix in radices:
        bits = radix.bit_length() - 1
        place = place * radix + ((relative >> shift) & (radix - 1))
        shift += bits
    return place


def as_column(row):
    count = row.shape[1]
    lane = lax.broadcasted_iota(jnp.int32, (count, count), 1)
    sublane = lax.broadcasted_iota(jnp.int32, (count, count), 0)
    return jnp.sum(jnp.where(lane == sublane, row, jnp.zeros_like(row)), axis=1, keepdims=True)


def outgoing_kernel(radices, slots_per, state, source, owner, dest, weight, table, keep, send):
    width, clusters = state.shape
    links = owner.shape[1]
    sets = table.shape[0]
    slots = keep.shape[0] + send.shape[0]
    owners = owner[...].astype(jnp.float32)
    lane = lax.broadcasted_iota(jnp.int32, (links, links), 1)
    sublane = lax.broadcasted_iota(jnp.int32, (links, links), 0)
    earlier = (as_column(owners) == owners) & (sublane < lane)
    rank = jnp.sum(jnp.where(earlier, 1.0, 0.0), axis=0, keepdims=True).astype(jnp.int32)
    if radices:
        relative = owner[...] ^ lax.axis_index("zone")
        block = block_of(relative, radices)
    else:
        block = owner[...]
    slot = block * slots_per + rank
    placing = lax.broadcasted_iota(jnp.int32, (slots, links), 0) == slot

    def of_slot(row):
        return jnp.sum(
            jnp.where(placing, row[...].astype(jnp.float32) + 1.0, 0.0), axis=1, keepdims=True
        ) - 1.0

    from_cluster, to_cluster, by_set = of_slot(source), of_slot(dest), of_slot(weight)
    pick = lax.broadcasted_iota(jnp.int32, (slots, clusters), 1) == from_cluster.astype(jnp.int32)
    pick = jnp.where(pick, 1.0, 0.0).astype(jnp.bfloat16)
    parts = jnp.concatenate(parts_of(state[...]), axis=1)
    picked = lax.dot_general(
        jnp.concatenate([pick, pick, pick], axis=1),
        parts,
        (((1,), (1,)), ((), ())),
        preferred_element_type=jnp.float32,
    )
    pick = lax.broadcasted_iota(jnp.int32, (slots, sets), 1) == by_set.astype(jnp.int32)
    pick = jnp.where(pick, 1.0, 0.0).astype(jnp.bfloat16)
    scales = jnp.zeros((slots, width), jnp.float32)
    for part in parts_of(table[...]):
        scales = scales + jnp.dot(pick, part, preferred_element_type=jnp.float32)
    blocks = picked * scales
    marks = jnp.broadcast_to(to_cluster, (slots, keep.shape[1] - width))
    kept = keep.shape[0]
    keep[:, :width] = blocks[:kept]
    keep[:, width:] = marks[:kept]
    send[:, :width] = blocks[kept:]
    send[:, width:] = marks[kept:]


def jacobian_kernel(state, table, column, kind, product):
    width, clusters = state.shape
    kinds = table.shape[0]
    half = state[...].astype(jnp.bfloat16)
    codes = column[...] + clusters * kind[...]
    row = lax.broadcasted_iota(jnp.int32, (clusters, clusters), 0)
    total = jnp.zeros((width, clusters), jnp.float32)
    for which in range(kinds):
        full = jnp.dot(table[which], half, preferred_element_type=jnp.float32)
        high = full.astype(jnp.bfloat16)
        low = (full - high.astype(jnp.float32)).astype(jnp.bfloat16)
        count = jnp.zeros((clusters, clusters), jnp.float32)
        for entry in range(codes.shape[0]):
            hit = row == codes[entry : entry + 1, :] - which * clusters
            count = count + jnp.where(hit, 1.0, 0.0)
        count = count.astype(jnp.bfloat16)
        total = total + jnp.dot(
            jnp.concatenate([high, low], axis=1),
            jnp.concatenate([count, count], axis=0),
            preferred_element_type=jnp.float32,
        )
    product[...] = total


def combine_kernel(table, held_by, *refs):
    period = len(table)
    me = lax.axis_index("inst")
    *held, out = refs
    total = None
    for mask, ref in zip(held_by, held, strict=True):
        shift = ((me ^ 1) - (me ^ mask) + period) & (period - 1)
        term = chosen(table, shift) * ref[...]
        total = term if total is None else total + term
    out[...] = total


def final_kernel(table, held_by, pieces, count, step, source, product, *refs):
    period = len(table)
    held = refs[: len(held_by)]
    others = refs[len(held_by) : len(refs) - pieces - 2]
    incoming = refs[len(refs) - pieces - 2 : len(refs) - 2]
    updated, residual = refs[-2:]
    width, clusters = source.shape
    me = lax.axis_index("inst")
    total = source[...] + product[...]
    for mask, ref in zip(held_by, held, strict=True):
        shift = (me - (me ^ mask) + period) & (period - 1)
        total = total + chosen(table, shift) * ref[...]
    for ref in others:
        total = total + ref[...]
    arrived = jnp.concatenate([ref[...] for ref in incoming], axis=0)
    target = arrived[:, width : width + 1].astype(jnp.int32)
    landing = lax.broadcasted_iota(jnp.int32, (arrived.shape[0], clusters), 1) == target
    landing = jnp.where(landing, 1.0, 0.0).astype(jnp.bfloat16)
    parts = jnp.concatenate(parts_of(arrived), axis=0)
    iface = lax.dot_general(
        parts,
        jnp.concatenate([landing, landing, landing], axis=0),
        (((0,), (0,)), ((), ())),
        preferred_element_type=jnp.float32,
    )[:width]
    active = lax.broadcasted_iota(jnp.int32, (1, clusters), 1) < count[0]
    kept = jnp.where(active, total - iface, 0.0)
    residual[...] = kept
    updated[...] = held[0][...] - step[...] * kept


def moved(value, axis, mask):
    count = lax.axis_size(axis)
    return lax.ppermute(value, axis, [(place, place ^ mask) for place in range(count)])


def zone_exchange(keep, send, radices, slots_per):
    zones = math.prod(radices)
    lanes = keep.shape[-1]
    rest = zones // radices[0]
    held, shift = [], 0
    for stage, radix in enumerate(radices):
        if stage == 0:
            arrived = moved(send, "zone", 1).reshape(rest, slots_per, lanes)
            held = [keep.reshape(rest, slots_per, lanes), arrived]
            shift = 1
            continue
        bits = radix.bit_length() - 1
        rest //= radix
        cut = [piece.reshape(radix, -1, slots_per, lanes) for piece in held]
        after = [piece[0] for piece in cut]
        for digit in range(radix - 1, 0, -1):
            leaving = jnp.concatenate([piece[digit] for piece in cut], axis=0)
            leaving = leaving.reshape(-1, lanes)
            landed = moved(leaving, "zone", digit << shift)
            after.append(landed.reshape(-1, slots_per, lanes))
        if rest > 1:
            joined = []
            for piece in after:
                groups = piece.reshape(-1, rest, slots_per, lanes)
                joined.extend(groups[index] for index in range(groups.shape[0]))
            after = joined
        held = after
        shift += bits
    return [piece.reshape(-1, lanes) for piece in held]


def on_device(
    state,
    source,
    jac_table,
    pattern_col,
    pattern_type,
    pseudo_step,
    zone_count,
    link_src,
    link_owner,
    link_dest,
    link_weight,
    iface_table,
):
    instances = lax.axis_size("inst")
    zones = lax.axis_size("zone")
    state_t = state[0].T
    source_t = source[0].T
    width, clusters = state_t.shape
    links = link_src.shape[1]
    slots_per = 2 * links // zones
    slots = zones * slots_per
    padded = -(-(width + 1) // LANES) * LANES
    table = coefficients(instances)
    block = jax.ShapeDtypeStruct((width, clusters), jnp.float32)

    radices = radices_of(zones)
    half = jax.ShapeDtypeStruct((slots // 2, padded), jnp.float32)
    keep, send = pl.pallas_call(
        functools.partial(outgoing_kernel, radices, slots_per),
        out_shape=(half, half),
        in_specs=[VMEM] * 6,
        out_specs=(VMEM, VMEM),
    )(
        state_t,
        link_src,
        link_owner.reshape(1, links),
        link_dest,
        link_weight,
        iface_table,
    )
    incoming = zone_exchange(keep, send, radices, slots_per)

    held, held_by = [state_t], [0]
    mask = instances // 2
    while mask > 1:
        held = held + [moved(piece, "inst", mask) for piece in held]
        held_by = held_by + [by ^ mask for by in held_by]
        mask //= 2
    others = []
    if instances > 1:
        combined = pl.pallas_call(
            functools.partial(combine_kernel, table, held_by),
            out_shape=block,
            in_specs=[VMEM] * len(held),
            out_specs=VMEM,
        )(*held)
        others = [moved(combined, "inst", 1)]

    product = pl.pallas_call(
        jacobian_kernel,
        out_shape=block,
        in_specs=[VMEM] * 4,
        out_specs=VMEM,
    )(state_t, jac_table, pattern_col.T, pattern_type.T)

    updated, residual = pl.pallas_call(
        functools.partial(final_kernel, table, held_by, len(incoming)),
        out_shape=(block, block),
        in_specs=[SMEM] + [VMEM] * (3 + len(held) + len(others) + len(incoming)),
        out_specs=(VMEM, VMEM),
    )(zone_count, pseudo_step, source_t, product, *held, *others, *incoming)
    return updated.T[None], residual.T[None]


def solution(mesh):
    placed = (
        P("inst", "zone", None),
        P("inst", "zone", None),
        P("zone", None, None),
        P("zone", None),
        P("zone", None),
        P("inst", "zone"),
        P("zone"),
        P("inst", "zone"),
        P("inst", "zone", None),
        P("inst", "zone"),
        P("inst", "zone"),
        P(),
    )
    return jax.shard_map(
        on_device,
        mesh=mesh,
        in_specs=placed,
        out_specs=(P("inst", "zone", None), P("inst", "zone", None)),
        check_vma=False,
    )
```

time: 40.8 us -> 24.8 us (0.61)
  Pallas kernels: 0 us -> 9.5 us
  starting transfers between devices: 15.1 us -> 8.9 us
  other arithmetic: 5.99 us -> 0.01 us
  matrix products: 5.89 us -> 0 us
  local copies, waits for them, and re-layouts: 8.16 us -> 3.27 us
  waiting for transfers between devices: 3.72 us -> 1.44 us
    all_to_all x2 -> x0, starting transfers between devices: 12.6 us -> none  [the longest x1 6.58 us: on_device(): lax.all_to_all(outgoing_targets, 'zone', split_axis=0, concat_axis=0, til...]
    pallas_call x0 -> x4, Pallas kernels: none -> 9.5 us  [the longest x1 3.56 us: on_device(): pl.pallas_call(jacobian_kernel, out_shape=block, in_specs=[VMEM] * 4, out...]
    ppermute x3 -> x6, starting transfers between devices: 2.55 us -> 8.9 us  [moved(): lax.ppermute(value, axis, [(place, place ^ mask) for place in range(count)])]
    dot_general x4 -> x0, matrix products: 5.89 us -> none  [the longest x1 2.74 us: on_device(): lax.dot_general(state_half, table_flat, (((1,), (1,)), ((), ())), preferr...]
    gather x3 -> x0, local copies, waits for them, and re-layouts: 4.29 us -> none  [the longest x2 3.69 us: on_device(): jac_term = jnp.sum(products[entry_rows], axis=1)]
    broadcast_in_dim x1 -> x0, other arithmetic: 1.79 us -> none  [on_device(): return (updated[None], residual[None])]
    reshape x1 -> x0, local copies, waits for them, and re-layouts: 1.72 us -> none  [on_device(): products = products.reshape(clusters * kinds, width)]
    reduce_sum x3 -> x0, other arithmetic: 1.39 us -> none  [the longest x1 0.83 us: on_device(): jnp.sum(jnp.cumsum(owner_hits, axis=0) * owner_hits, axis=1) - 1]
  transfers between devices with their start and end apart: 5 -> 6, of which waited for: 2 -> 1; matrix products, arithmetic and copies ran while one was open for 44% -> 8% of each run, Pallas kernels for 0% -> 30%
where the time goes in v1:
time: 24.8 us; the launch traced here: 24.5 us
  Pallas kernels  9.5 us (38%)
  starting transfers between devices  8.9 us (36%)
  local copies, waits for them, and re-layouts  3.27 us (13%)
  waiting for transfers between devices  1.44 us (6%)
  between operations  1.35 us (5%)
    ppermute x6, starting transfers between devices, moved(): lax.ppermute(value, axis, [(place, place ^ mask) for place in range(count)])  8.9 us
    pallas_call x1, Pallas kernels, on_device(): pl.pallas_call(jacobian_kernel, out_shape=block, in_specs=[VMEM] * 4, out...  3.56 us
    pallas_call x1, Pallas kernels, on_device(): pl.pallas_call(functools.partial(final_kernel, table, held_by, len(incomi...  2.26 us
    pallas_call x1, Pallas kernels, on_device(): pl.pallas_call(functools.partial(outgoing_kernel, radices, slots_per), ou...  1.99 us
    squeeze x2, local copies, waits for them, and re-layouts, zone_exchange(): leaving = jnp.concatenate([piece[digit] for piece in cut], axis=0)  1.95 us
    pallas_call x1, Pallas kernels, on_device(): pl.pallas_call(functools.partial(combine_kernel, table, held_by), out_sha...  1.68 us
    ppermute x6, waiting for transfers between devices, moved(): lax.ppermute(value, axis, [(place, place ^ mask) for place in range(count)])  1.44 us
    unnamed x10, local copies, waits for them, and re-layouts  1.32 us
  transfers between devices with their start and end apart: 6, of which 1 were waited for; matrix products, arithmetic and copies ran while one was open for 8% of the time, Pallas kernels for 30%

profile of v1, /device:TPU:0, one launch (start us, length us, event | category | flops | bytes accessed | tf_op | source)
XLA Modules:
  0.0 24.5 jit_solution(14685758621104315430)
XLA Ops:
  0.6 3.0 %collective-permute-start = (f32[320,128]{1,0:T(8,128)}, f32[320,128]{1,0:T(8,128)S(1)}, u32[]{:S(2)}, u32[]{:S(2)}) collective-permute-start(f32[320,128]{1,0:T(8,128)} %bitcast.33), channel_id=1, source_target_pairs={{0,16},{8,24},{16,0},{24,8},{1,17},{9,25},{17,1},{25,9},{2,18},{10... | collective-permute-start | bytes 491528 | tf_op jit(solution)/shard_map/ppermute | solution.py:191
  3.6 2.0 %shard_map.133 = (f32[32,384]{1,0:T(8,128)}, f32[32,384]{1,0:T(8,128)}) custom-call(f32[320,128]{1,0:T(8,128)} %bitcast.34, s32[1,32]{1,0:T(1,128)} %source.1, s32[1,32]{1,0:T(1,128)} %bitcast.41, s32[1,32]{1,0:T(1,128)} %dest.1, s32[1,32]{1,0:T(1,128)} %weight.1, f32[16,320]{1,0:T(8,128)} %table.3), custom_call_target="tpu_custom_call" | custom-call | tf_op jit(solution)/shard_map/pallas_call | solution.py:253
  5.6 1.5 %collective-permute-start.2 = (f32[32,384]{1,0:T(8,128)}, f32[32,384]{1,0:T(8,128)S(1)}, u32[]{:S(2)}, u32[]{:S(2)}) collective-permute-start(f32[32,384]{1,0:T(8,128)} %get-tuple-element.7), channel_id=1, source_target_pairs={{0,1},{1,0},{2,3},{3,2},{4,5},{5,4},{6,7},{7,6},{8,9},{9,8},{10,11... | collective-permute-start | bytes 147464 | tf_op jit(solution)/shard_map/ppermute | solution.py:191
  7.1 1.4 %slice_bitcast_fusion.3 = (f32[1,8,384]{2,1,0:T(8,128)S(1)}, f32[1,8,384]{2,1,0:T(8,128)S(1)}, f32[1,8,384]{2,1,0:T(8,128)S(1)}, f32[8,384]{1,0:T(8,128)}) fusion(f32[32,384]{1,0:T(8,128)} %get-tuple-element.6), kind=kLoop, calls=%fused_computation.6 | loop fusion | bytes 98304 | tf_op jit(solution)/shard_map/squeeze | solution.py:210
  8.5 1.4 %collective-permute-done.2 = f32[32,384]{1,0:T(8,128)S(1)} collective-permute-done((f32[32,384]{1,0:T(8,128)}, f32[32,384]{1,0:T(8,128)S(1)}, u32[]{:S(2)}, u32[]{:S(2)}) %collective-permute-start.2) | collective-permute-done | bytes 49184 | tf_op jit(solution)/shard_map/ppermute | solution.py:191
  9.9 0.6 %slice_bitcast_fusion = (f32[1,8,384]{2,1,0:T(8,128)S(1)}, f32[1,8,384]{2,1,0:T(8,128)S(1)}, f32[1,8,384]{2,1,0:T(8,128)S(1)}, f32[8,384]{1,0:T(8,128)}) fusion(f32[32,384]{1,0:T(8,128)S(1)} %collective-permute-done.2), kind=kLoop, calls=%fused_computation.3 | loop fusion | bytes 98304 | tf_op jit(solution)/shard_map/squeeze | solution.py:210
  10.5 3.6 %collective-permute-start.3 = (f32[16,384]{1,0:T(8,128)S(1)}, f32[16,384]{1,0:T(8,128)S(1)}, u32[]{:S(2)}, u32[]{:S(2)}) collective-permute-start(f32[16,384]{1,0:T(8,128)S(1)} %maximum_bitcast_fusion), channel_id=1, source_target_pairs={{0,6},{1,7},{2,4},{3,5},{4,2},{5,3},{6,0},{7,1},{8,14},{9,15},{10,... | collective-permute-start | bytes 73736 | tf_op jit(solution)/shard_map/ppermute | solution.py:191
  14.1 0.0 collective-permute-done.refs_1_
  14.1 0.7 %copy-done = f32[320,128]{1,0:T(8,128)} copy-done((f32[320,128]{1,0:T(8,128)}, f32[320,128]{1,0:T(8,128)S(1)}, u32[]{:S(2)}) %copy-start) | copy-done | bytes 163864
  14.8 1.7 %shard_map.132 = f32[320,128]{1,0:T(8,128)} custom-call(f32[320,128]{1,0:T(8,128)} %bitcast.35, f32[320,128]{1,0:T(8,128)} %copy-done), custom_call_target="tpu_custom_call" | custom-call | tf_op jit(solution)/shard_map/pallas_call | solution.py:276
  16.5 0.0 collective-permute-start.1
  16.5 0.0 collective-permute-start.4
  16.5 0.8 %collective-permute-start.5 = (f32[16,384]{1,0:T(8,128)S(1)}, f32[16,384]{1,0:T(8,128)S(1)}, u32[]{:S(2)}, u32[]{:S(2)}) collective-permute-start(f32[16,384]{1,0:T(8,128)S(1)} %maximum_bitcast_fusion.2), channel_id=1, source_target_pairs={{0,2},{1,3},{2,0},{3,1},{4,6},{5,7},{6,4},{7,5},{8,10},{9,11},{10,... | collective-permute-start | bytes 73736 | tf_op jit(solution)/shard_map/ppermute | solution.py:191
  17.9 3.6 %shard_map.131.product = f32[320,128]{1,0:T(8,128)} custom-call(f32[320,128]{1,0:T(8,128)} %bitcast.36, bf16[8,320,320]{2,1,0:T(8,128)(2,1)} %table.2, s32[4,128]{1,0:T(4,128)} %bitcast.39, s32[4,128]{1,0:T(4,128)} %bitcast.40), custom_call_target="tpu_custom_call" | custom-call | tf_op jit(solution)/shard_map/pallas_call | solution.py:284
  21.5 0.0 collective-permute-done.3.refs_5_
  21.5 0.0 collective-permute-done.4.refs_6_
  21.5 0.0 collective-permute-done.5.refs_7_
  21.5 0.0 copy-start.4
  21.5 0.0 collective-permute-done.1.refs_2_
  21.6 0.5 %copy-done.2 = f32[16,384]{1,0:T(8,128)} copy-done((f32[16,384]{1,0:T(8,128)}, f32[16,384]{1,0:T(8,128)S(1)}, u32[]{:S(2)}) %copy-start.2) | copy-done | bytes 24600
  22.1 0.0 copy-done.3
  22.1 0.0 copy-done.4
  22.1 0.1 copy-done.1
  22.2 2.3 %shard_map.134 = (f32[320,128]{1,0:T(8,128)}, f32[320,128]{1,0:T(8,128)}) custom-call(s32[1]{0:T(128)S(6)} %copy.14.count, f32[1,128]{1,0:T(1,128)} %step.1, f32[320,128]{1,0:T(8,128)} %bitcast.38, f32[320,128]{1,0:T(8,128)} %shard_map.131.product, f32[320,128]{1,0:T(8,128)} %bitcast.37, f32[320,128]{1,0:T(8,128)} %copy-done, f32[320,128]{1,0:T(8,128)} %copy-done.1, ...), custom_call_target="tpu_custom_call" | custom-call | tf_op jit(solution)/shard_map/pallas_call | solution.py:291
  (7 shorter events, 0.0 us)
Async XLA Ops:
  0.6 13.5 %collective-permute-start = (f32[320,128]{1,0:T(8,128)}, f32[320,128]{1,0:T(8,128)S(1)}, u32[]{:S(2)}, u32[]{:S(2)}) collective-permute-start(f32[320,128]{1,0:T(8,128)} %bitcast.33), channel_id=1, source_target_pairs={{0,16},{8,24},{16,0},{24,8},{1,17},{9,25},{17,1},{25,9},{2,18},{10... | collective-permute-start | bytes 491528 | tf_op jit(solution)/shard_map/ppermute | solution.py:191
  5.6 4.3 %collective-permute-start.2 = (f32[32,384]{1,0:T(8,128)}, f32[32,384]{1,0:T(8,128)S(1)}, u32[]{:S(2)}, u32[]{:S(2)}) collective-permute-start(f32[32,384]{1,0:T(8,128)} %get-tuple-element.7), channel_id=1, source_target_pairs={{0,1},{1,0},{2,3},{3,2},{4,5},{5,4},{6,7},{7,6},{8,9},{9,8},{10,11... | collective-permute-start | bytes 147464 | tf_op jit(solution)/shard_map/ppermute | solution.py:191
  10.5 11.0 %collective-permute-start.3 = (f32[16,384]{1,0:T(8,128)S(1)}, f32[16,384]{1,0:T(8,128)S(1)}, u32[]{:S(2)}, u32[]{:S(2)}) collective-permute-start(f32[16,384]{1,0:T(8,128)S(1)} %maximum_bitcast_fusion), channel_id=1, source_target_pairs={{0,6},{1,7},{2,4},{3,5},{4,2},{5,3},{6,0},{7,1},{8,14},{9,15},{10,... | collective-permute-start | bytes 73736 | tf_op jit(solution)/shard_map/ppermute | solution.py:191
  14.1 0.7 %copy-start = (f32[320,128]{1,0:T(8,128)}, f32[320,128]{1,0:T(8,128)S(1)}, u32[]{:S(2)}) copy-start(f32[320,128]{1,0:T(8,128)S(1)} %collective-permute-done.refs_1_) | copy-start | bytes 491524
  16.5 5.0 %collective-permute-start.1 = (f32[320,128]{1,0:T(8,128)}, f32[320,128]{1,0:T(8,128)S(1)}, u32[]{:S(2)}, u32[]{:S(2)}) collective-permute-start(f32[320,128]{1,0:T(8,128)} %shard_map.132), channel_id=1, source_target_pairs={{0,8},{8,0},{16,24},{24,16},{1,9},{9,1},{17,25},{25,17},{2,10},{10... | collective-permute-start | bytes 491528 | tf_op jit(solution)/shard_map/ppermute | solution.py:191
  16.5 5.0 %collective-permute-start.4 = (f32[16,384]{1,0:T(8,128)S(1)}, f32[16,384]{1,0:T(8,128)S(1)}, u32[]{:S(2)}, u32[]{:S(2)}) collective-permute-start(f32[16,384]{1,0:T(8,128)S(1)} %maximum_bitcast_fusion.1), channel_id=1, source_target_pairs={{0,4},{1,5},{2,6},{3,7},{4,0},{5,1},{6,2},{7,3},{8,12},{9,13},{10,... | collective-permute-start | bytes 73736 | tf_op jit(solution)/shard_map/ppermute | solution.py:191
  16.5 5.0 %collective-permute-start.5 = (f32[16,384]{1,0:T(8,128)S(1)}, f32[16,384]{1,0:T(8,128)S(1)}, u32[]{:S(2)}, u32[]{:S(2)}) collective-permute-start(f32[16,384]{1,0:T(8,128)S(1)} %maximum_bitcast_fusion.2), channel_id=1, source_target_pairs={{0,2},{1,3},{2,0},{3,1},{4,6},{5,7},{6,4},{7,5},{8,10},{9,11},{10,... | collective-permute-start | bytes 73736 | tf_op jit(solution)/shard_map/ppermute | solution.py:191
  21.5 0.6 %copy-start.2 = (f32[16,384]{1,0:T(8,128)}, f32[16,384]{1,0:T(8,128)S(1)}, u32[]{:S(2)}) copy-start(f32[16,384]{1,0:T(8,128)S(1)} %collective-permute-done.3.refs_5_) | copy-start | bytes 73732
  21.5 0.6 %copy-start.3 = (f32[16,384]{1,0:T(8,128)}, f32[16,384]{1,0:T(8,128)S(1)}, u32[]{:S(2)}) copy-start(f32[16,384]{1,0:T(8,128)S(1)} %collective-permute-done.4.refs_6_) | copy-start | bytes 73732
  21.5 0.6 %copy-start.4 = (f32[16,384]{1,0:T(8,128)}, f32[16,384]{1,0:T(8,128)S(1)}, u32[]{:S(2)}) copy-start(f32[16,384]{1,0:T(8,128)S(1)} %collective-permute-done.5.refs_7_) | copy-start | bytes 73732
  21.5 0.7 %copy-start.1 = (f32[320,128]{1,0:T(8,128)}, f32[320,128]{1,0:T(8,128)S(1)}, u32[]{:S(2)}) copy-start(f32[320,128]{1,0:T(8,128)S(1)} %collective-permute-done.1.refs_2_) | copy-start | bytes 491524

commit v2 on v1

--- a/solution.py
+++ b/solution.py
@@ -13,7 +13,12 @@
 NU = 0.1
 LANES = 128
 VMEM = pl.BlockSpec(memory_space=pltpu.VMEM)
-SMEM = pl.BlockSpec(memory_space=pltpu.SMEM)
+HBM = pl.BlockSpec(memory_space=pltpu.HBM)
+ROOM = pltpu.CompilerParams(vmem_limit_bytes=6 << 20)
+
+
+def in_hbm(value):
+    return pltpu.with_memory_space_constraint(value, pltpu.HBM)
 
 
 def coefficients(period):
@@ -72,22 +77,58 @@
     return jnp.sum(jnp.where(lane == sublane, row, jnp.zeros_like(row)), axis=1, keepdims=True)
 
 
-def outgoing_kernel(radices, slots_per, state, source, owner, dest, weight, table, keep, send):
+def fetched(pairs, sems):
+    copies = []
+    for place, (origin, target) in enumerate(pairs):
+        copy = pltpu.make_async_copy(origin, target, sems.at[place])
+        copy.start()
+        copies.append(copy)
+    return copies
+
+
+def outgoing_kernel(
+    radices,
+    slots_per,
+    state_in,
+    source_in,
+    owner_in,
+    dest_in,
+    weight_in,
+    table_in,
+    state,
+    keep,
+    send,
+    source,
+    owner,
+    dest,
+    weight,
+    table,
+    sems,
+):
+    copies = fetched(
+        (
+            (owner_in, owner),
+            (source_in, source),
+            (weight_in, weight),
+            (dest_in, dest),
+            (state_in, state),
+            (table_in, table),
+        ),
+        sems,
+    )
     width, clusters = state.shape
     links = owner.shape[1]
     sets = table.shape[0]
     slots = keep.shape[0] + send.shape[0]
+    for copy in copies[:4]:
+        copy.wait()
     owners = owner[...].astype(jnp.float32)
     lane = lax.broadcasted_iota(jnp.int32, (links, links), 1)
     sublane = lax.broadcasted_iota(jnp.int32, (links, links), 0)
     earlier = (as_column(owners) == owners) & (sublane < lane)
     rank = jnp.sum(jnp.where(earlier, 1.0, 0.0), axis=0, keepdims=True).astype(jnp.int32)
-    if radices:
-        relative = owner[...] ^ lax.axis_index("zone")
-        block = block_of(relative, radices)
-    else:
-        block = owner[...]
-    slot = block * slots_per + rank
+    relative = owner[...] ^ lax.axis_index("zone")
+    slot = block_of(relative, radices) * slots_per + rank
     placing = lax.broadcasted_iota(jnp.int32, (slots, links), 0) == slot
 
     def of_slot(row):
@@ -98,6 +139,13 @@
     from_cluster, to_cluster, by_set = of_slot(source), of_slot(dest), of_slot(weight)
     pick = lax.broadcasted_iota(jnp.int32, (slots, clusters), 1) == from_cluster.astype(jnp.int32)
     pick = jnp.where(pick, 1.0, 0.0).astype(jnp.bfloat16)
+    choose = lax.broadcasted_iota(jnp.int32, (slots, sets), 1) == by_set.astype(jnp.int32)
+    choose = jnp.where(choose, 1.0, 0.0).astype(jnp.bfloat16)
+    copies[5].wait()
+    scales = jnp.zeros((slots, width), jnp.float32)
+    for part in parts_of(table[...]):
+        scales = scales + jnp.dot(choose, part, preferred_element_type=jnp.float32)
+    copies[4].wait()
     parts = jnp.concatenate(parts_of(state[...]), axis=1)
     picked = lax.dot_general(
         jnp.concatenate([pick, pick, pick], axis=1),
@@ -105,11 +153,6 @@
         (((1,), (1,)), ((), ())),
         preferred_element_type=jnp.float32,
     )
-    pick = lax.broadcasted_iota(jnp.int32, (slots, sets), 1) == by_set.astype(jnp.int32)
-    pick = jnp.where(pick, 1.0, 0.0).astype(jnp.bfloat16)
-    scales = jnp.zeros((slots, width), jnp.float32)
-    for part in parts_of(table[...]):
-        scales = scales + jnp.dot(pick, part, preferred_element_type=jnp.float32)
     blocks = picked * scales
     marks = jnp.broadcast_to(to_cluster, (slots, keep.shape[1] - width))
     kept = keep.shape[0]
@@ -119,52 +162,113 @@
     send[:, width:] = marks[kept:]
 
 
-def jacobian_kernel(state, table, column, kind, product):
-    width, clusters = state.shape
-    kinds = table.shape[0]
+def put_products(blocks, place, half, high, low):
+    clusters = half.shape[1]
+    full = jnp.dot(blocks, half, preferred_element_type=jnp.float32)
+    columns = slice(place * clusters, (place + 1) * clusters)
+    upper = full.astype(jnp.bfloat16)
+    high[:, columns] = upper
+    low[:, columns] = (full - upper.astype(jnp.float32)).astype(jnp.bfloat16)
+
+
+def products_kernel(blocks_in, state, high, low, blocks, sems):
+    (copy,) = fetched([(blocks_in.at[pl.ds(0, blocks.shape[0])], blocks)], sems)
     half = state[...].astype(jnp.bfloat16)
+    copy.wait()
+    for which in range(blocks.shape[0]):
+        put_products(blocks[which], which, half, high, low)
+
+
+def local_kernel(
+    table,
+    blocks_in,
+    column_in,
+    kind_in,
+    source_in,
+    step_in,
+    count,
+    state,
+    high,
+    low,
+    base,
+    rows,
+    blocks,
+    column,
+    kind,
+    source,
+    step,
+    more_high,
+    more_low,
+    sems,
+):
+    clusters = state.shape[1]
+    kinds = blocks_in.shape[0]
+    ready = kinds - blocks.shape[0]
+    copies = fetched(
+        [
+            (column_in, column),
+            (kind_in, kind),
+            (blocks_in.at[pl.ds(ready, kinds - ready)], blocks),
+            (source_in, source),
+            (step_in, step),
+        ],
+        sems,
+    )
+    half = state[...].astype(jnp.bfloat16)
+    copies[0].wait()
+    copies[1].wait()
     codes = column[...] + clusters * kind[...]
     row = lax.broadcasted_iota(jnp.int32, (clusters, clusters), 0)
-    total = jnp.zeros((width, clusters), jnp.float32)
+    counts = []
     for which in range(kinds):
-        full = jnp.dot(table[which], half, preferred_element_type=jnp.float32)
-        high = full.astype(jnp.bfloat16)
-        low = (full - high.astype(jnp.float32)).astype(jnp.bfloat16)
-        count = jnp.zeros((clusters, clusters), jnp.float32)
+        count_of = jnp.zeros((clusters, clusters), jnp.float32)
         for entry in range(codes.shape[0]):
             hit = row == codes[entry : entry + 1, :] - which * clusters
-            count = count + jnp.where(hit, 1.0, 0.0)
-        count = count.astype(jnp.bfloat16)
+            count_of = count_of + jnp.where(hit, 1.0, 0.0)
+        counts.append(count_of.astype(jnp.bfloat16))
+    counts = jnp.concatenate(counts, axis=0)
+    total = chosen(table, 0) * state[...]
+    for part in (high, low):
         total = total + jnp.dot(
-            jnp.concatenate([high, low], axis=1),
-            jnp.concatenate([count, count], axis=0),
-            preferred_element_type=jnp.float32,
+            part[...], counts[: ready * clusters], preferred_element_type=jnp.float32
         )
-    product[...] = total
-
-
-def combine_kernel(table, held_by, *refs):
+    copies[2].wait()
+    for which in range(kinds - ready):
+        put_products(blocks[which], which, half, more_high, more_low)
+    for part in (more_high, more_low):
+        total = total + jnp.dot(
+            part[...], counts[ready * clusters :], preferred_element_type=jnp.float32
+        )
+    copies[3].wait()
+    base[...] = total + source[...]
+    copies[4].wait()
+    active = lax.broadcasted_iota(jnp.int32, (1, clusters), 1) < count[0]
+    rows[0:1, :] = step[...]
+    rows[1:2, :] = jnp.where(active, 1.0, 0.0)
+
+
+def combine_kernel(table, held_by, mask, _, *refs):
     period = len(table)
     me = lax.axis_index("inst")
     *held, out = refs
     total = None
-    for mask, ref in zip(held_by, held, strict=True):
-        shift = ((me ^ 1) - (me ^ mask) + period) & (period - 1)
+    for by, ref in zip(held_by, held, strict=True):
+        shift = ((me ^ mask) - (me ^ by) + period) & (period - 1)
         term = chosen(table, shift) * ref[...]
         total = term if total is None else total + term
     out[...] = total
 
 
-def final_kernel(table, held_by, pieces, count, step, source, product, *refs):
+def final_kernel(table, held_by, pieces, base, rows, *refs):
     period = len(table)
     held = refs[: len(held_by)]
     others = refs[len(held_by) : len(refs) - pieces - 2]
     incoming = refs[len(refs) - pieces - 2 : len(refs) - 2]
     updated, residual = refs[-2:]
-    width, clusters = source.shape
+    width, clusters = base.shape
     me = lax.axis_index("inst")
-    total = source[...] + product[...]
-    for mask, ref in zip(held_by, held, strict=True):
+    total = base[...]
+    for mask, ref in zip(held_by[1:], held[1:], strict=True):
         shift = (me - (me ^ mask) + period) & (period - 1)
         total = total + chosen(table, shift) * ref[...]
     for ref in others:
@@ -180,10 +284,25 @@
         (((0,), (0,)), ((), ())),
         preferred_element_type=jnp.float32,
     )[:width]
-    active = lax.broadcasted_iota(jnp.int32, (1, clusters), 1) < count[0]
-    kept = jnp.where(active, total - iface, 0.0)
+    kept = jnp.where(rows[1:2, :] > 0.0, total - iface, 0.0)
     residual[...] = kept
-    updated[...] = held[0][...] - step[...] * kept
+    updated[...] = held[0][...] - rows[0:1, :] * kept
+
+
+def ordered_kernel(_, *refs):
+    half = len(refs) // 2
+    for origin, target in zip(refs[:half], refs[half:], strict=True):
+        target[...] = origin[...]
+
+
+def ordered(after, *values):
+    return pl.pallas_call(
+        ordered_kernel,
+        out_shape=tuple(jax.ShapeDtypeStruct(value.shape, value.dtype) for value in values),
+        in_specs=[VMEM] * (1 + len(values)),
+        out_specs=(VMEM,) * len(values),
+        compiler_params=ROOM,
+    )(after, *values)
 
 
 def moved(value, axis, mask):
@@ -191,15 +310,15 @@
     return lax.ppermute(value, axis, [(place, place ^ mask) for place in range(count)])
 
 
-def zone_exchange(keep, send, radices, slots_per):
+def zone_exchange(keep, send, radices, slots_per, after):
     zones = math.prod(radices)
     lanes = keep.shape[-1]
     rest = zones // radices[0]
     held, shift = [], 0
     for stage, radix in enumerate(radices):
         if stage == 0:
-            arrived = moved(send, "zone", 1).reshape(rest, slots_per, lanes)
-            held = [keep.reshape(rest, slots_per, lanes), arrived]
+            pieces = ordered(after, keep, moved(send, "zone", 1))
+            held = [piece.reshape(rest, slots_per, lanes) for piece in pieces]
             shift = 1
             continue
         bits = radix.bit_length() - 1
@@ -250,50 +369,102 @@
 
     radices = radices_of(zones)
     half = jax.ShapeDtypeStruct((slots // 2, padded), jnp.float32)
-    keep, send = pl.pallas_call(
+    state_t, keep, send = pl.pallas_call(
         functools.partial(outgoing_kernel, radices, slots_per),
-        out_shape=(half, half),
-        in_specs=[VMEM] * 6,
+        out_shape=(block, half, half),
+        in_specs=[HBM] * 6,
+        out_specs=(VMEM, VMEM, VMEM),
+        scratch_shapes=[pltpu.VMEM((1, links), jnp.int32)] * 4
+        + [pltpu.VMEM(iface_table.shape, jnp.float32), pltpu.SemaphoreType.DMA((6,))],
+        compiler_params=ROOM,
+    )(
+        in_hbm(state_t),
+        in_hbm(link_src),
+        in_hbm(link_owner.reshape(1, links)),
+        in_hbm(link_dest),
+        in_hbm(link_weight),
+        in_hbm(iface_table),
+    )
+    kinds = jac_table.shape[0]
+    first = kinds // 2
+    blocks_hbm = in_hbm(jac_table)
+    parts = jax.ShapeDtypeStruct((width, first * clusters), jnp.bfloat16)
+    high, low = pl.pallas_call(
+        products_kernel,
+        out_shape=(parts, parts),
+        in_specs=[HBM, VMEM],
         out_specs=(VMEM, VMEM),
-    )(
-        state_t,
-        link_src,
-        link_owner.reshape(1, links),
-        link_dest,
-        link_weight,
-        iface_table,
-    )
-    incoming = zone_exchange(keep, send, radices, slots_per)
+        scratch_shapes=[
+            pltpu.VMEM((first, *jac_table.shape[1:]), jac_table.dtype),
+            pltpu.SemaphoreType.DMA((1,)),
+        ],
+        compiler_params=ROOM,
+        cost_estimate=pl.CostEstimate(
+            flops=2 * first * width * clusters * width,
+            bytes_accessed=2 * first * width * width + 4 * parts.size,
+            transcendentals=0,
+        ),
+    )(blocks_hbm, state_t)
 
     held, held_by = [state_t], [0]
-    mask = instances // 2
-    while mask > 1:
+    mask = 1
+    while mask < instances // 2:
         held = held + [moved(piece, "inst", mask) for piece in held]
         held_by = held_by + [by ^ mask for by in held_by]
-        mask //= 2
+        mask *= 2
     others = []
     if instances > 1:
         combined = pl.pallas_call(
-            functools.partial(combine_kernel, table, held_by),
+            functools.partial(combine_kernel, table, held_by, mask),
             out_shape=block,
-            in_specs=[VMEM] * len(held),
+            in_specs=[VMEM] * (1 + len(held)),
             out_specs=VMEM,
-        )(*held)
-        others = [moved(combined, "inst", 1)]
-
-    product = pl.pallas_call(
-        jacobian_kernel,
-        out_shape=block,
-        in_specs=[VMEM] * 4,
-        out_specs=VMEM,
-    )(state_t, jac_table, pattern_col.T, pattern_type.T)
+            compiler_params=ROOM,
+        )(high, *held)
+        others = [moved(combined, "inst", mask)]
+    incoming = zone_exchange(keep, send, radices, slots_per, combined)
+
+    column, kind = pattern_col.T, pattern_type.T
+    base, rows = pl.pallas_call(
+        functools.partial(local_kernel, table),
+        out_shape=(block, jax.ShapeDtypeStruct((8, clusters), jnp.float32)),
+        in_specs=[HBM] * 5 + [VMEM] * 4,
+        out_specs=(VMEM, VMEM),
+        scratch_shapes=[
+            pltpu.VMEM((kinds - first, *jac_table.shape[1:]), jac_table.dtype),
+            pltpu.VMEM(column.shape, jnp.int32),
+            pltpu.VMEM(kind.shape, jnp.int32),
+            pltpu.VMEM((width, clusters), jnp.float32),
+            pltpu.VMEM((1, clusters), jnp.float32),
+            pltpu.VMEM((width, (kinds - first) * clusters), jnp.bfloat16),
+            pltpu.VMEM((width, (kinds - first) * clusters), jnp.bfloat16),
+            pltpu.SemaphoreType.DMA((5,)),
+        ],
+        compiler_params=ROOM,
+        cost_estimate=pl.CostEstimate(
+            flops=4 * kinds * width * clusters * clusters,
+            bytes_accessed=4 * parts.size + 8 * width * clusters,
+            transcendentals=0,
+        ),
+    )(
+        blocks_hbm,
+        in_hbm(column),
+        in_hbm(kind),
+        in_hbm(source_t),
+        in_hbm(pseudo_step),
+        zone_count,
+        state_t,
+        high,
+        low,
+    )
 
     updated, residual = pl.pallas_call(
         functools.partial(final_kernel, table, held_by, len(incoming)),
         out_shape=(block, block),
-        in_specs=[SMEM] + [VMEM] * (3 + len(held) + len(others) + len(incoming)),
+        in_specs=[VMEM] * (2 + len(held) + len(others) + len(incoming)),
         out_specs=(VMEM, VMEM),
-    )(zone_count, pseudo_step, source_t, product, *held, *others, *incoming)
+        compiler_params=ROOM,
+    )(base, rows, *held, *others, *incoming)
     return updated.T[None], residual.T[None]
 
 

time: 24.8 us -> 18 us (0.73)
  Pallas kernels: 9.5 us -> 6.04 us
  local copies, waits for them, and re-layouts: 3.27 us -> 0.01 us
    squeeze x2 -> x1, local copies, waits for them, and re-layouts: 1.95 us -> 0.01 us  [zone_exchange(): leaving = jnp.concatenate([piece[digit] for piece in cut], axis=0)]
    pallas_call x2 -> x4, Pallas kernels: 5.24 us -> 3.7 us  [the longest x1 2.04 us: on_device(): pl.pallas_call(functools.partial(local_kernel, table), out_shape=(block,...]
    unnamed x10 -> x0, local copies, waits for them, and re-layouts: 1.32 us -> none
    pallas_call x1, Pallas kernels: 2.26 us -> 1.01 us  [on_device(): pl.pallas_call(functools.partial(final_kernel, table, held_by, len(incomi...]
    pallas_call x1, Pallas kernels: 1.99 us -> 1.34 us  [on_device(): pl.pallas_call(functools.partial(outgoing_kernel, radices, slots_per), ou...]
  transfers between devices with their start and end apart: 6 -> 6, of which waited for: 1 -> 1; matrix products, arithmetic and copies ran while one was open for 8% -> 0% of each run, Pallas kernels for 30% -> 21%
where the time goes in v2:
time: 18 us; the launch traced here: 17.8 us
  starting transfers between devices  9.11 us (51%)
  Pallas kernels  6.04 us (34%)
  between operations  1.36 us (8%)
  waiting for transfers between devices  1.24 us (7%)
    ppermute x6, starting transfers between devices, moved(): lax.ppermute(value, axis, [(place, place ^ mask) for place in range(count)])  9.11 us
    pallas_call x1, Pallas kernels, on_device(): pl.pallas_call(functools.partial(local_kernel, table), out_shape=(block,...  2.04 us
    pallas_call x1, Pallas kernels, on_device(): pl.pallas_call(products_kernel, out_shape=(parts, parts), in_specs=[HBM,...  1.61 us
    pallas_call x1, Pallas kernels, on_device(): pl.pallas_call(functools.partial(outgoing_kernel, radices, slots_per), ou...  1.34 us
    ppermute x6, waiting for transfers between devices, moved(): lax.ppermute(value, axis, [(place, place ^ mask) for place in range(count)])  1.24 us
    pallas_call x1, Pallas kernels, on_device(): pl.pallas_call(functools.partial(final_kernel, table, held_by, len(incomi...  1.01 us
  transfers between devices with their start and end apart: 6, of which 1 were waited for; matrix products, arithmetic and copies ran while one was open for 0% of the time, Pallas kernels for 21%

profile of v2, /device:TPU:0, one launch (start us, length us, event | category | flops | bytes accessed | tf_op | source)
XLA Modules:
  0.0 17.8 jit_solution(1192046353210308598)
XLA Ops:
  0.6 1.3 %shard_map.131 = (f32[320,128]{1,0:T(8,128)S(1)}, f32[32,384]{1,0:T(8,128)S(1)}, f32[32,384]{1,0:T(8,128)S(1)}) custom-call(f32[320,128]{1,0:T(8,128)} %bitcast.33, s32[1,32]{1,0:T(1,128)} %source_in.1, s32[1,32]{1,0:T(1,128)} %bitcast.37, s32[1,32]{1,0:T(1,128)} %dest_in.1, s32[1,32]{1,0:T(1,128)} %weight_in.1, f32[16,320]{1,0:T(8,128)} %table_in.1), custom_call_target="tpu_custom_call" | custom-call | tf_op jit(solution)/shard_map/pallas_call | solution.py:372
  2.0 0.5 %collective-permute-start = (f32[320,128]{1,0:T(8,128)S(1)}, f32[320,128]{1,0:T(8,128)S(1)}, u32[]{:S(2)}, u32[]{:S(2)}) collective-permute-start(f32[320,128]{1,0:T(8,128)S(1)} %get-tuple-element.13.state.refs_0_), channel_id=1, source_target_pairs={{0,8},{8,0},{16,24},{24,16},{1,9},{9,1},{17,25},{25,17},{2,10},{10... | collective-permute-start | bytes 491528 | tf_op jit(solution)/shard_map/ppermute | solution.py:310
  2.5 2.6 %collective-permute-start.2 = (f32[32,384]{1,0:T(8,128)S(1)}, f32[32,384]{1,0:T(8,128)S(1)}, u32[]{:S(2)}, u32[]{:S(2)}) collective-permute-start(f32[32,384]{1,0:T(8,128)S(1)} %get-tuple-element.19), channel_id=1, source_target_pairs={{0,1},{1,0},{2,3},{3,2},{4,5},{5,4},{6,7},{7,6},{8,9},{9,8},{10,11... | collective-permute-start | bytes 147464 | tf_op jit(solution)/shard_map/ppermute | solution.py:310
  5.1 1.6 %shard_map.132 = (bf16[320,512]{1,0:T(8,128)(2,1)S(1)}, bf16[320,512]{1,0:T(8,128)(2,1)S(1)}) custom-call(bf16[8,320,320]{2,1,0:T(8,128)(2,1)} %blocks_in.3, f32[320,128]{1,0:T(8,128)S(1)} %get-tuple-element.13.state.refs_0_), custom_call_target="tpu_custom_call" | custom-call | flops 104857600 | bytes 1474560 | tf_op jit(solution)/shard_map/pallas_call | solution.py:392
  6.7 0.0 collective-permute-done.refs_1_
  6.8 1.6 %collective-permute-start.1 = (f32[320,128]{1,0:T(8,128)S(1)}, f32[320,128]{1,0:T(8,128)S(1)}, u32[]{:S(2)}, u32[]{:S(2)}) collective-permute-start(f32[320,128]{1,0:T(8,128)S(1)} %shard_map.134._), channel_id=1, source_target_pairs={{0,16},{8,24},{16,0},{24,8},{1,17},{9,25},{17,1},{25,9},{2,18},{10... | collective-permute-start | bytes 491528 | tf_op jit(solution)/shard_map/ppermute | solution.py:310
  8.3 0.0 collective-permute-done.2.refs_1_
  8.4 3.7 %collective-permute-start.3 = (f32[16,384]{1,0:T(8,128)S(1)}, f32[16,384]{1,0:T(8,128)S(1)}, u32[]{:S(2)}, u32[]{:S(2)}) collective-permute-start(f32[16,384]{1,0:T(8,128)S(1)} %maximum_bitcast_fusion), channel_id=1, source_target_pairs={{0,6},{1,7},{2,4},{3,5},{4,2},{5,3},{6,0},{7,1},{8,14},{9,15},{10,... | collective-permute-start | bytes 73736 | tf_op jit(solution)/shard_map/ppermute | solution.py:310
  12.0 0.0 collective-permute-start.4
  12.0 0.8 %collective-permute-start.5 = (f32[16,384]{1,0:T(8,128)S(1)}, f32[16,384]{1,0:T(8,128)S(1)}, u32[]{:S(2)}, u32[]{:S(2)}) collective-permute-start(f32[16,384]{1,0:T(8,128)S(1)} %maximum_bitcast_fusion.2), channel_id=1, source_target_pairs={{0,2},{1,3},{2,0},{3,1},{4,6},{5,7},{6,4},{7,5},{8,10},{9,11},{10,... | collective-permute-start | bytes 73736 | tf_op jit(solution)/shard_map/ppermute | solution.py:310
  13.5 2.0 %shard_map.133 = (f32[320,128]{1,0:T(8,128)S(1)}, f32[8,128]{1,0:T(8,128)S(1)}) custom-call(bf16[8,320,320]{2,1,0:T(8,128)(2,1)} %blocks_in.3, s32[4,128]{1,0:T(4,128)} %bitcast.35, s32[4,128]{1,0:T(4,128)} %bitcast.36, f32[320,128]{1,0:T(8,128)} %bitcast.34, f32[1,128]{1,0:T(1,128)} %step_in.1, s32[1]{0:T(128)S(6)} %copy.14.count, ...), custom_call_target="tpu_custom_call" | custom-call | flops 167772160 | bytes 983040 | tf_op jit(solution)/shard_map/pallas_call | solution.py:428
  15.5 0.0 collective-permute-done.3.refs_5_
  15.5 1.2 %collective-permute-done.4.refs_6_ = f32[16,384]{1,0:T(8,128)S(1)} collective-permute-done((f32[16,384]{1,0:T(8,128)S(1)}, f32[16,384]{1,0:T(8,128)S(1)}, u32[]{:S(2)}, u32[]{:S(2)}) %collective-permute-start.4) | collective-permute-done | bytes 24608 | tf_op jit(solution)/shard_map/ppermute | solution.py:310
  16.8 0.0 collective-permute-done.5.refs_7_
  16.8 0.0 collective-permute-done.1.refs_2_
  16.8 1.0 %shard_map.136 = (f32[320,128]{1,0:T(8,128)}, f32[320,128]{1,0:T(8,128)}) custom-call(f32[320,128]{1,0:T(8,128)S(1)} %get-tuple-element.16.base, f32[8,128]{1,0:T(8,128)S(1)} %get-tuple-element.17.rows, f32[320,128]{1,0:T(8,128)S(1)} %get-tuple-element.13.state.refs_0_, f32[320,128]{1,0:T(8,128)S(1)} %collective-permute-done.refs_1_, ...), custom_call_target="tpu_custom_call" | custom-call | tf_op jit(solution)/shard_map/pallas_call | solution.py:461
  (6 shorter events, 0.1 us)
Async XLA Ops:
  2.0 4.7 %collective-permute-start = (f32[320,128]{1,0:T(8,128)S(1)}, f32[320,128]{1,0:T(8,128)S(1)}, u32[]{:S(2)}, u32[]{:S(2)}) collective-permute-start(f32[320,128]{1,0:T(8,128)S(1)} %get-tuple-element.13.state.refs_0_), channel_id=1, source_target_pairs={{0,8},{8,0},{16,24},{24,16},{1,9},{9,1},{17,25},{25,17},{2,10},{10... | collective-permute-start | bytes 491528 | tf_op jit(solution)/shard_map/ppermute | solution.py:310
  2.5 5.8 %collective-permute-start.2 = (f32[32,384]{1,0:T(8,128)S(1)}, f32[32,384]{1,0:T(8,128)S(1)}, u32[]{:S(2)}, u32[]{:S(2)}) collective-permute-start(f32[32,384]{1,0:T(8,128)S(1)} %get-tuple-element.19), channel_id=1, source_target_pairs={{0,1},{1,0},{2,3},{3,2},{4,5},{5,4},{6,7},{7,6},{8,9},{9,8},{10,11... | collective-permute-start | bytes 147464 | tf_op jit(solution)/shard_map/ppermute | solution.py:310
  6.8 10.0 %collective-permute-start.1 = (f32[320,128]{1,0:T(8,128)S(1)}, f32[320,128]{1,0:T(8,128)S(1)}, u32[]{:S(2)}, u32[]{:S(2)}) collective-permute-start(f32[320,128]{1,0:T(8,128)S(1)} %shard_map.134._), channel_id=1, source_target_pairs={{0,16},{8,24},{16,0},{24,8},{1,17},{9,25},{17,1},{25,9},{2,18},{10... | collective-permute-start | bytes 491528 | tf_op jit(solution)/shard_map/ppermute | solution.py:310
  8.4 7.2 %collective-permute-start.3 = (f32[16,384]{1,0:T(8,128)S(1)}, f32[16,384]{1,0:T(8,128)S(1)}, u32[]{:S(2)}, u32[]{:S(2)}) collective-permute-start(f32[16,384]{1,0:T(8,128)S(1)} %maximum_bitcast_fusion), channel_id=1, source_target_pairs={{0,6},{1,7},{2,4},{3,5},{4,2},{5,3},{6,0},{7,1},{8,14},{9,15},{10,... | collective-permute-start | bytes 73736 | tf_op jit(solution)/shard_map/ppermute | solution.py:310
  12.0 4.7 %collective-permute-start.4 = (f32[16,384]{1,0:T(8,128)S(1)}, f32[16,384]{1,0:T(8,128)S(1)}, u32[]{:S(2)}, u32[]{:S(2)}) collective-permute-start(f32[16,384]{1,0:T(8,128)S(1)} %maximum_bitcast_fusion.1), channel_id=1, source_target_pairs={{0,4},{1,5},{2,6},{3,7},{4,0},{5,1},{6,2},{7,3},{8,12},{9,13},{10,... | collective-permute-start | bytes 73736 | tf_op jit(solution)/shard_map/ppermute | solution.py:310
  12.0 4.7 %collective-permute-start.5 = (f32[16,384]{1,0:T(8,128)S(1)}, f32[16,384]{1,0:T(8,128)S(1)}, u32[]{:S(2)}, u32[]{:S(2)}) collective-permute-start(f32[16,384]{1,0:T(8,128)S(1)} %maximum_bitcast_fusion.2), channel_id=1, source_target_pairs={{0,2},{1,3},{2,0},{3,1},{4,6},{5,7},{6,4},{7,5},{8,10},{9,11},{10,... | collective-permute-start | bytes 73736 | tf_op jit(solution)/shard_map/ppermute | solution.py:310

commit v3 on v2

v3 whole, which is shorter than its diff:
```python
import functools
import math

import jax
import jax.numpy as jnp
import numpy as np
from jax import lax
from jax.experimental import pallas as pl
from jax.experimental.pallas import tpu as pltpu
from jax.sharding import PartitionSpec as P

OMEGA = 0.25
NU = 0.1
LANES = 128
VMEM = pl.BlockSpec(memory_space=pltpu.VMEM)
SMEM = pl.BlockSpec(memory_space=pltpu.SMEM)
HBM = pl.BlockSpec(memory_space=pltpu.HBM)
FREE = pl.CostEstimate(flops=1, bytes_accessed=1, transcendentals=0)
ROOM = pltpu.CompilerParams(vmem_limit_bytes=6 << 20)


def in_hbm(value):
    return pltpu.with_memory_space_constraint(value, pltpu.HBM)


def coefficients(period):
    table = [NU * (period * period + 2) / 12.0]
    for shift in range(1, period):
        phase = math.pi * shift / period
        sign = -1.0 if shift % 2 else 1.0
        sine = math.sin(phase)
        table.append(OMEGA * sign * math.cos(phase) / sine + NU * sign / (2.0 * sine * sine))
    return [float(np.float32(entry)) for entry in table]


def chosen(table, index, dtype=jnp.float32):
    value = jnp.asarray(table[0], dtype)
    for position in range(1, len(table)):
        value = jnp.where(index == position, jnp.asarray(table[position], dtype), value)
    return value


def parts_of(value):
    high = value.astype(jnp.bfloat16)
    rest = value - high.astype(jnp.float32)
    middle = rest.astype(jnp.bfloat16)
    low = (rest - middle.astype(jnp.float32)).astype(jnp.bfloat16)
    return high, middle, low


def power_of_two(count):
    return count & (count - 1) == 0


def stages_of(zones):
    stages = []
    shift = zones.bit_length() - 1
    while shift:
        bits = 2 if shift > 1 else 1
        shift -= bits
        stages.append((1 << bits, shift))
    return stages


def turns_of(radix):
    if radix == 4:
        return ((0, 1, 2, 3), (2, 3, 1, 0), (3, 2, 0, 1), (1, 0, 3, 2))
    return tuple(tuple(digit ^ turn for digit in range(radix)) for turn in range(radix))


def block_of(owner, me, stages):
    place = jnp.zeros_like(owner)
    for radix, shift in stages:
        turns = turns_of(radix)
        mine = (me >> shift) & (radix - 1)
        theirs = (owner >> shift) & (radix - 1)
        turn = jnp.zeros_like(owner)
        for which in range(1, radix):
            target = chosen(turns[which], mine, jnp.int32)
            turn = jnp.where(theirs == target, which, turn)
        place = place * radix + turn
    return place


def as_column(row):
    count = row.shape[1]
    lane = lax.broadcasted_iota(jnp.int32, (count, count), 1)
    sublane = lax.broadcasted_iota(jnp.int32, (count, count), 0)
    return jnp.sum(jnp.where(lane == sublane, row, jnp.zeros_like(row)), axis=1, keepdims=True)


def fetched(pairs, sems):
    copies = []
    for place, (origin, target) in enumerate(pairs):
        copy = pltpu.make_async_copy(origin, target, sems.at[place])
        copy.start()
        copies.append(copy)
    return copies


def outgoing_kernel(
    stages,
    slots_per,
    state_in,
    source_in,
    owner_in,
    dest_in,
    weight_in,
    table_in,
    state,
    *refs,
):
    *sends, source, owner, dest, weight, table, sems = refs
    copies = fetched(
        (
            (owner_in, owner),
            (source_in, source),
            (weight_in, weight),
            (dest_in, dest),
            (state_in, state),
            (table_in, table),
        ),
        sems,
    )
    width, clusters = state.shape
    links = owner.shape[1]
    sets = table.shape[0]
    share, lanes = sends[0].shape
    slots = share * len(sends)
    for copy in copies[:4]:
        copy.wait()
    owners = owner[...].astype(jnp.float32)
    lane = lax.broadcasted_iota(jnp.int32, (links, links), 1)
    sublane = lax.broadcasted_iota(jnp.int32, (links, links), 0)
    earlier = (as_column(owners) == owners) & (sublane < lane)
    rank = jnp.sum(jnp.where(earlier, 1.0, 0.0), axis=0, keepdims=True).astype(jnp.int32)
    slot = block_of(owner[...], lax.axis_index("zone"), stages) * slots_per + rank
    placing = lax.broadcasted_iota(jnp.int32, (slots, links), 0) == slot

    def of_slot(row):
        return jnp.sum(
            jnp.where(placing, row[...].astype(jnp.float32) + 1.0, 0.0), axis=1, keepdims=True
        ) - 1.0

    from_cluster, to_cluster, by_set = of_slot(source), of_slot(dest), of_slot(weight)
    pick = lax.broadcasted_iota(jnp.int32, (slots, clusters), 1) == from_cluster.astype(jnp.int32)
    pick = jnp.where(pick, 1.0, 0.0).astype(jnp.bfloat16)
    choose = lax.broadcasted_iota(jnp.int32, (slots, sets), 1) == by_set.astype(jnp.int32)
    choose = jnp.where(choose, 1.0, 0.0).astype(jnp.bfloat16)
    copies[5].wait()
    scales = jnp.zeros((slots, width), jnp.float32)
    for part in parts_of(table[...]):
        scales = scales + jnp.dot(choose, part, preferred_element_type=jnp.float32)
    copies[4].wait()
    parts = jnp.concatenate(parts_of(state[...]), axis=1)
    picked = lax.dot_general(
        jnp.concatenate([pick, pick, pick], axis=1),
        parts,
        (((1,), (1,)), ((), ())),
        preferred_element_type=jnp.float32,
    )
    blocks = picked * scales
    marks = jnp.broadcast_to(to_cluster, (slots, lanes - width))
    for place, send in enumerate(sends):
        rows = slice(place * share, (place + 1) * share)
        send[:, :width] = blocks[rows]
        send[:, width:] = marks[rows]


def half_kernel(state, _, half):
    half[...] = state[...].astype(jnp.bfloat16)


def landed(pieces, width, clusters):
    arrived = jnp.concatenate([piece[...] for piece in pieces], axis=0)
    target = arrived[:, width : width + 1].astype(jnp.int32)
    landing = lax.broadcasted_iota(jnp.int32, (arrived.shape[0], clusters), 1) == target
    landing = jnp.where(landing, 1.0, 0.0).astype(jnp.bfloat16)
    return lax.dot_general(
        jnp.concatenate(parts_of(arrived), axis=0),
        jnp.concatenate([landing, landing, landing], axis=0),
        (((0,), (0,)), ((), ())),
        preferred_element_type=jnp.float32,
    )[:width]


def local_kernel(
    table,
    column_in,
    kind_in,
    source_in,
    step_in,
    count,
    state,
    products,
    staying,
    base,
    rows,
    column,
    kind,
    source,
    sems,
):
    width, clusters = state.shape
    kinds = products.shape[0] // width
    step = rows.at[pl.ds(0, 1), :]
    copies = fetched(
        [(column_in, column), (kind_in, kind), (source_in, source), (step_in, step)], sems
    )
    total = chosen(table, 0) * state[...] - landed([staying], width, clusters)
    high, low = [], []
    for which in range(kinds):
        full = products[pl.ds(which * width, width), :]
        upper = full.astype(jnp.bfloat16)
        high.append(upper)
        low.append((full - upper.astype(jnp.float32)).astype(jnp.bfloat16))
    copies[0].wait()
    copies[1].wait()
    codes = column[...] + clusters * kind[...]
    row = lax.broadcasted_iota(jnp.int32, (clusters, clusters), 0)
    counts = []
    for which in range(kinds):
        count_of = jnp.zeros((clusters, clusters), jnp.float32)
        for entry in range(codes.shape[0]):
            hit = row == codes[entry : entry + 1, :] - which * clusters
            count_of = count_of + jnp.where(hit, 1.0, 0.0)
        counts.append(count_of.astype(jnp.bfloat16))
    counts = jnp.concatenate(counts, axis=0)
    for part in (high, low):
        total = total + jnp.dot(
            jnp.concatenate(part, axis=1), counts, preferred_element_type=jnp.float32
        )
    copies[2].wait()
    copies[3].wait()
    base[...] = total + source[...]
    active = lax.broadcasted_iota(jnp.int32, (1, clusters), 1) < count[0]
    rows[1:2, :] = jnp.where(active, 1.0, 0.0)


def combine_kernel(table, held_by, mask, *refs):
    period = len(table)
    me = lax.axis_index("inst")
    held, rest = refs[: len(held_by)], refs[len(held_by) :]
    passing = len(rest) // 2
    out = rest[passing]
    for origin, target in zip(rest[:passing], rest[passing + 1 :], strict=True):
        target[...] = origin[...]
    total = None
    for by, ref in zip(held_by, held, strict=True):
        shift = ((me ^ mask) - (me ^ by) + period) & (period - 1)
        term = chosen(table, shift) * ref[...]
        total = term if total is None else total + term
    out[...] = total


def final_kernel(table, held_by, pieces, base, rows, *refs):
    period = len(table)
    held = refs[: len(held_by)]
    others = refs[len(held_by) : len(refs) - pieces - 2]
    incoming = refs[len(refs) - pieces - 2 : len(refs) - 2]
    updated, residual = refs[-2:]
    width, clusters = base.shape
    me = lax.axis_index("inst")
    total = base[...]
    for mask, ref in zip(held_by[1:], held[1:], strict=True):
        shift = (me - (me ^ mask) + period) & (period - 1)
        total = total + chosen(table, shift) * ref[...]
    for ref in others:
        total = total + ref[...]
    total = total - landed(incoming, width, clusters)
    kept = jnp.where(rows[1:2, :] > 0.0, total, 0.0)
    residual[...] = kept
    updated[...] = held[0][...] - rows[0:1, :] * kept


def ordered_kernel(_, *refs):
    half = len(refs) // 2
    for origin, target in zip(refs[:half], refs[half:], strict=True):
        target[...] = origin[...]


def ordered(after, *values):
    return pl.pallas_call(
        ordered_kernel,
        out_shape=tuple(jax.ShapeDtypeStruct(value.shape, value.dtype) for value in values),
        in_specs=[VMEM] * (1 + len(values)),
        out_specs=(VMEM,) * len(values),
        compiler_params=ROOM,
        cost_estimate=FREE,
    )(after, *values)


def moved(value, axis, mask):
    count = lax.axis_size(axis)
    return lax.ppermute(value, axis, [(place, place ^ mask) for place in range(count)])


def stage_sent(sends, stage):
    radix, shift = stage
    turns = turns_of(radix)
    zones = lax.axis_size("zone")
    held = [sends[0]]
    for which in range(1, radix):
        pairs = []
        for place in range(zones):
            digit = (place >> shift) & (radix - 1)
            pairs.append((place, place + ((turns[which][digit] - digit) << shift)))
        held.append(lax.ppermute(sends[which], "zone", pairs))
    return held


def regrouped(held, radix):
    lanes = held[0].shape[1]
    cut = [piece.reshape(radix, -1, lanes) for piece in held]
    return [jnp.concatenate([piece[which] for piece in cut], axis=0) for which in range(radix)]


def on_device(
    state,
    source,
    jac_table,
    pattern_col,
    pattern_type,
    pseudo_step,
    zone_count,
    link_src,
    link_owner,
    link_dest,
    link_weight,
    iface_table,
):
    instances = lax.axis_size("inst")
    zones = lax.axis_size("zone")
    state_in = state[0].T
    source_t = source[0].T
    width, clusters = state_in.shape
    links = link_src.shape[1]
    slots_per = 2 * links // zones
    slots = zones * slots_per
    padded = -(-(width + 1) // LANES) * LANES
    table = coefficients(instances)
    block = jax.ShapeDtypeStruct((width, clusters), jnp.float32)

    stages = stages_of(zones)
    first = stages[0][0]
    share = jax.ShapeDtypeStruct((slots // first, padded), jnp.float32)
    state_t, *sends = pl.pallas_call(
        functools.partial(outgoing_kernel, stages, slots_per),
        out_shape=(block, *[share] * first),
        in_specs=[HBM] * 6,
        out_specs=(VMEM,) * (1 + first),
        scratch_shapes=[pltpu.VMEM((1, links), jnp.int32)] * 4
        + [pltpu.VMEM(iface_table.shape, jnp.float32), pltpu.SemaphoreType.DMA((6,))],
        compiler_params=ROOM,
    )(
        in_hbm(state_in),
        in_hbm(link_src),
        in_hbm(link_owner.reshape(1, links)),
        in_hbm(link_dest),
        in_hbm(link_weight),
        in_hbm(iface_table),
    )

    held, held_by = [state_t], [0]
    mask = 1
    while mask < instances // 2:
        arrivals = [moved(piece, "inst", mask) for piece in held]
        held = held + arrivals
        held_by = held_by + [by ^ mask for by in held_by]
        mask *= 2
    others = []
    if instances > 1:
        (combined,) = pl.pallas_call(
            functools.partial(combine_kernel, table, held_by, mask),
            out_shape=(block,),
            in_specs=[VMEM] * len(held),
            out_specs=(VMEM,),
            compiler_params=ROOM,
            cost_estimate=FREE,
        )(*held)
        others = [moved(combined, "inst", mask)]

    kinds = jac_table.shape[0]
    half = pl.pallas_call(
        half_kernel,
        out_shape=jax.ShapeDtypeStruct((width, clusters), jnp.bfloat16),
        in_specs=[VMEM] * 2,
        out_specs=VMEM,
        compiler_params=ROOM,
    )(state_t, combined)
    products = lax.dot_general(
        jac_table.reshape(kinds * width, width),
        half,
        (((1,), (0,)), ((), ())),
        preferred_element_type=jnp.float32,
    )

    pieces = ordered(products, *stage_sent(sends, stages[0]))
    for stage in stages[1:]:
        pieces = stage_sent(regrouped(pieces, stage[0]), stage)
    staying, *incoming = pieces

    column, kind = pattern_col.T, pattern_type.T
    base, rows = pl.pallas_call(
        functools.partial(local_kernel, table),
        out_shape=(block, jax.ShapeDtypeStruct((8, clusters), jnp.float32)),
        in_specs=[HBM] * 4 + [SMEM] + [VMEM] * 3,
        out_specs=(VMEM, VMEM),
        scratch_shapes=[
            pltpu.VMEM(column.shape, jnp.int32),
            pltpu.VMEM(kind.shape, jnp.int32),
            pltpu.VMEM((width, clusters), jnp.float32),
            pltpu.SemaphoreType.DMA((4,)),
        ],
        compiler_params=ROOM,
        cost_estimate=FREE,
    )(
        in_hbm(column),
        in_hbm(kind),
        in_hbm(source_t),
        in_hbm(pseudo_step),
        zone_count,
        state_t,
        products,
        staying,
    )

    updated, residual = pl.pallas_call(
        functools.partial(final_kernel, table, held_by, len(incoming)),
        out_shape=(block, block),
        in_specs=[VMEM] * (2 + len(held) + len(others) + len(incoming)),
        out_specs=(VMEM, VMEM),
        compiler_params=ROOM,
    )(base, rows, *held, *others, *incoming)
    return updated.T[None], residual.T[None]


def solution(mesh):
    placed = (
        P("inst", "zone", None),
        P("inst", "zone", None),
        P("zone", None, None),
        P("zone", None),
        P("zone", None),
        P("inst", "zone"),
        P("zone"),
        P("inst", "zone"),
        P("inst", "zone", None),
        P("inst", "zone"),
        P("inst", "zone"),
        P(),
    )
    return jax.shard_map(
        on_device,
        mesh=mesh,
        in_specs=placed,
        out_specs=(P("inst", "zone", None), P("inst", "zone", None)),
        check_vma=False,
    )
```

time: 18 us -> 16.6 us (0.922)
  Pallas kernels: 6.04 us -> 3.91 us
  matrix products: 0 us -> 0.66 us
  waiting for transfers between devices: 1.24 us -> 1.52 us
    ppermute x6 -> x2, starting transfers between devices: 9.11 us -> 2.07 us  [moved(): lax.ppermute(value, axis, [(place, place ^ mask) for place in range(count)])]
    ppermute x0 -> x4, starting transfers between devices: none -> 6.89 us  [stage_sent(): held.append(lax.ppermute(sends[which], 'zone', pairs))]
    ppermute x0 -> x4, waiting for transfers between devices: none -> 1.51 us  [stage_sent(): held.append(lax.ppermute(sends[which], 'zone', pairs))]
    pallas_call x2, Pallas kernels: 2.95 us -> 1.49 us  [the longest x1 1.48 us: on_device(): pl.pallas_call(functools.partial(outgoing_kernel, stages, slots_per), out...]
    ppermute x6 -> x2, waiting for transfers between devices: 1.24 us -> 0.01 us  [moved(): lax.ppermute(value, axis, [(place, place ^ mask) for place in range(count)])]
    dot_general x0 -> x1, matrix products: none -> 0.66 us  [on_device(): lax.dot_general(jac_table.reshape(kinds * width, width), half, (((1,), (0...]
    pallas_call x1, Pallas kernels: 2.04 us -> 1.41 us  [on_device(): pl.pallas_call(functools.partial(local_kernel, table), out_shape=(block,...]
  transfers between devices with their start and end apart: 6 -> 6, of which waited for: 1 -> 3; matrix products, arithmetic and copies ran while one was open for 0% -> 4% of each run, Pallas kernels for 21% -> 9%
where the time goes in v3:
time: 16.6 us; the launch traced here: 16.5 us
  starting transfers between devices  8.96 us (54%)
  Pallas kernels  3.91 us (24%)
  waiting for transfers between devices  1.52 us (9%)
  between operations  1.38 us (8%)
  matrix products  0.66 us (4%)
    ppermute x4, starting transfers between devices, stage_sent(): held.append(lax.ppermute(sends[which], 'zone', pairs))  6.89 us
    ppermute x2, starting transfers between devices, moved(): lax.ppermute(value, axis, [(place, place ^ mask) for place in range(count)])  2.07 us
    ppermute x4, waiting for transfers between devices, stage_sent(): held.append(lax.ppermute(sends[which], 'zone', pairs))  1.51 us
    pallas_call x1, Pallas kernels, on_device(): pl.pallas_call(functools.partial(outgoing_kernel, stages, slots_per), out...  1.48 us
    pallas_call x1, Pallas kernels, on_device(): pl.pallas_call(functools.partial(local_kernel, table), out_shape=(block,...  1.41 us
    pallas_call x1, Pallas kernels, on_device(): pl.pallas_call(functools.partial(final_kernel, table, held_by, len(incomi...  0.96 us
    dot_general x1, matrix products, on_device(): lax.dot_general(jac_table.reshape(kinds * width, width), half, (((1,), (0...  0.66 us
  transfers between devices with their start and end apart: 6, of which 3 were waited for; matrix products, arithmetic and copies ran while one was open for 4% of the time, Pallas kernels for 9%

profile of v3, /device:TPU:0, one launch (start us, length us, event | category | flops | bytes accessed | tf_op | source)
XLA Modules:
  0.0 16.5 jit_solution(16375143395475713467)
XLA Ops:
  0.6 0.0 copy-start
  0.6 1.5 %shard_map.131 = (f32[320,128]{1,0:T(8,128)S(1)}, f32[16,384]{1,0:T(8,128)S(1)}, f32[16,384]{1,0:T(8,128)S(1)}, f32[16,384]{1,0:T(8,128)S(1)}, f32[16,384]{1,0:T(8,128)S(1)}) custom-call(f32[320,128]{1,0:T(8,128)} %bitcast.22, s32[1,32]{1,0:T(1,128)} %source_in.1, s32[1,32]{1,0:T(1,128)} %bitcast.25, s32[1,32]{1,0:T(1,128)} %dest_in.1, s32[1,32]{1,0:T(1,128)} %weight_in.1, ...), custom_call_target="tpu_custom_call" | custom-call | tf_op jit(solution)/shard_map/pallas_call | solution.py:347
  2.1 0.5 %collective-permute-start = (f32[320,128]{1,0:T(8,128)S(1)}, f32[320,128]{1,0:T(8,128)S(1)}, u32[]{:S(2)}, u32[]{:S(2)}) collective-permute-start(f32[320,128]{1,0:T(8,128)S(1)} %get-tuple-element.15.refs_0_.state), channel_id=1, source_target_pairs={{0,8},{8,0},{16,24},{24,16},{1,9},{9,1},{17,25},{25,17},{2,10},{10... | collective-permute-start | bytes 491528 | tf_op jit(solution)/shard_map/ppermute | solution.py:295
  2.7 3.6 %collective-permute-start.1 = (f32[16,384]{1,0:T(8,128)S(1)}, f32[16,384]{1,0:T(8,128)S(1)}, u32[]{:S(2)}, u32[]{:S(2)}) collective-permute-start(f32[16,384]{1,0:T(8,128)S(1)} %get-tuple-element.17), channel_id=1, source_target_pairs={{0,4},{1,5},{2,6},{3,7},{4,2},{5,3},{6,0},{7,1},{8,12},{9,13},{10,... | collective-permute-start | bytes 73736 | tf_op jit(solution)/shard_map/ppermute | solution.py:308
  6.3 1.1 %collective-permute-start.2 = (f32[16,384]{1,0:T(8,128)S(1)}, f32[16,384]{1,0:T(8,128)S(1)}, u32[]{:S(2)}, u32[]{:S(2)}) collective-permute-start(f32[16,384]{1,0:T(8,128)S(1)} %get-tuple-element.18), channel_id=1, source_target_pairs={{0,6},{1,7},{2,4},{3,5},{4,0},{5,1},{6,2},{7,3},{8,14},{9,15},{10,... | collective-permute-start | bytes 73736 | tf_op jit(solution)/shard_map/ppermute | solution.py:308
  7.4 0.5 %collective-permute-start.3 = (f32[16,384]{1,0:T(8,128)S(1)}, f32[16,384]{1,0:T(8,128)S(1)}, u32[]{:S(2)}, u32[]{:S(2)}) collective-permute-start(f32[16,384]{1,0:T(8,128)S(1)} %get-tuple-element.19), channel_id=1, source_target_pairs={{0,2},{1,3},{2,0},{3,1},{4,6},{5,7},{6,4},{7,5},{8,10},{9,11},{10,... | collective-permute-start | bytes 73736 | tf_op jit(solution)/shard_map/ppermute | solution.py:308
  8.5 0.0 collective-permute-done.refs_1_
  8.6 1.6 %collective-permute-start.4 = (f32[320,128]{1,0:T(8,128)S(1)}, f32[320,128]{1,0:T(8,128)S(1)}, u32[]{:S(2)}, u32[]{:S(2)}) collective-permute-start(f32[320,128]{1,0:T(8,128)S(1)} %shard_map.132._), channel_id=1, source_target_pairs={{0,16},{8,24},{16,0},{24,8},{1,17},{9,25},{17,1},{25,9},{2,18},{10... | collective-permute-start | bytes 491528 | tf_op jit(solution)/shard_map/ppermute | solution.py:295
  10.2 0.0 copy-done
  10.2 0.7 %convolution_bitcast_fusion._.products = f32[2560,128]{1,0:T(8,128)S(1)} fusion(bf16[2560,320]{1,0:T(8,128)(2,1)S(1)} %bitcast.20, bf16[320,128]{1,0:T(8,128)(2,1)S(1)} %shard_map.133), kind=kOutput, calls=%fused_computation | convolution fusion | flops 209715200 | bytes 3031040 | tf_op jit(solution)/shard_map/dot_general | solution.py:391
  10.8 0.0 collective-permute-done.1.refs_1_
  10.8 0.3 %collective-permute-done.2.refs_2_ = f32[16,384]{1,0:T(8,128)S(1)} collective-permute-done((f32[16,384]{1,0:T(8,128)S(1)}, f32[16,384]{1,0:T(8,128)S(1)}, u32[]{:S(2)}, u32[]{:S(2)}) %collective-permute-start.2) | collective-permute-done | bytes 24608 | tf_op jit(solution)/shard_map/ppermute | solution.py:308
  11.1 0.2 collective-permute-done.3.refs_3_
  11.3 1.7 %collective-permute-start.5 = (f32[32,384]{1,0:T(8,128)S(1)}, f32[32,384]{1,0:T(8,128)S(1)}, u32[]{:S(2)}, u32[]{:S(2)}) collective-permute-start(f32[32,384]{1,0:T(8,128)S(1)} %pad_maximum_fusion.1), channel_id=1, source_target_pairs={{0,1},{1,0},{2,3},{3,2},{4,5},{5,4},{6,7},{7,6},{8,9},{9,8},{10,11... | collective-permute-start | bytes 147464 | tf_op jit(solution)/shard_map/ppermute | solution.py:308
  13.0 1.4 %shard_map.135 = (f32[320,128]{1,0:T(8,128)S(1)}, f32[8,128]{1,0:T(8,128)S(1)}) custom-call(s32[4,128]{1,0:T(4,128)} %bitcast.23, s32[4,128]{1,0:T(4,128)} %bitcast.24, f32[320,128]{1,0:T(8,128)} %bitcast.21, f32[1,128]{1,0:T(1,128)} %step_in.1, s32[1]{0:T(128)S(6)} %copy.16.count, f32[320,128]{1,0:T(8,128)S(1)} %get-tuple-element.15.refs_0_.state, ...), custom_call_target="tpu_custom_call" | custom-call | flops 1 | bytes 1 | tf_op jit(solution)/shard_map/pallas_call | solution.py:404
  14.4 1.1 %collective-permute-done.5.refs_3_ = f32[32,384]{1,0:T(8,128)S(1)} collective-permute-done((f32[32,384]{1,0:T(8,128)S(1)}, f32[32,384]{1,0:T(8,128)S(1)}, u32[]{:S(2)}, u32[]{:S(2)}) %collective-permute-start.5) | collective-permute-done | bytes 49184 | tf_op jit(solution)/shard_map/ppermute | solution.py:308
  15.5 0.0 collective-permute-done.4.refs_2_
  15.5 1.0 %shard_map.136 = (f32[320,128]{1,0:T(8,128)}, f32[320,128]{1,0:T(8,128)}) custom-call(f32[320,128]{1,0:T(8,128)S(1)} %get-tuple-element.24.base, f32[8,128]{1,0:T(8,128)S(1)} %get-tuple-element.25.rows, f32[320,128]{1,0:T(8,128)S(1)} %get-tuple-element.15.refs_0_.state, f32[320,128]{1,0:T(8,128)S(1)} %collective-permute-done.refs_1_, ...), custom_call_target="tpu_custom_call" | custom-call | tf_op jit(solution)/shard_map/pallas_call | solution.py:428
  (7 shorter events, 0.1 us)
Async XLA Ops:
  0.6 9.5 %copy-start = (bf16[8,320,320]{2,1,0:T(8,128)(2,1)S(1)}, bf16[8,320,320]{2,1,0:T(8,128)(2,1)}, u32[]{:S(2)}) copy-start(bf16[8,320,320]{2,1,0:T(8,128)(2,1)} %param.14) | copy-start | bytes 4915204
  2.1 6.4 %collective-permute-start = (f32[320,128]{1,0:T(8,128)S(1)}, f32[320,128]{1,0:T(8,128)S(1)}, u32[]{:S(2)}, u32[]{:S(2)}) collective-permute-start(f32[320,128]{1,0:T(8,128)S(1)} %get-tuple-element.15.refs_0_.state), channel_id=1, source_target_pairs={{0,8},{8,0},{16,24},{24,16},{1,9},{9,1},{17,25},{25,17},{2,10},{10... | collective-permute-start | bytes 491528 | tf_op jit(solution)/shard_map/ppermute | solution.py:295
  2.7 8.2 %collective-permute-start.1 = (f32[16,384]{1,0:T(8,128)S(1)}, f32[16,384]{1,0:T(8,128)S(1)}, u32[]{:S(2)}, u32[]{:S(2)}) collective-permute-start(f32[16,384]{1,0:T(8,128)S(1)} %get-tuple-element.17), channel_id=1, source_target_pairs={{0,4},{1,5},{2,6},{3,7},{4,2},{5,3},{6,0},{7,1},{8,12},{9,13},{10,... | collective-permute-start | bytes 73736 | tf_op jit(solution)/shard_map/ppermute | solution.py:308
  6.3 4.8 %collective-permute-start.2 = (f32[16,384]{1,0:T(8,128)S(1)}, f32[16,384]{1,0:T(8,128)S(1)}, u32[]{:S(2)}, u32[]{:S(2)}) collective-permute-start(f32[16,384]{1,0:T(8,128)S(1)} %get-tuple-element.18), channel_id=1, source_target_pairs={{0,6},{1,7},{2,4},{3,5},{4,0},{5,1},{6,2},{7,3},{8,14},{9,15},{10,... | collective-permute-start | bytes 73736 | tf_op jit(solution)/shard_map/ppermute | solution.py:308
  7.4 3.9 %collective-permute-start.3 = (f32[16,384]{1,0:T(8,128)S(1)}, f32[16,384]{1,0:T(8,128)S(1)}, u32[]{:S(2)}, u32[]{:S(2)}) collective-permute-start(f32[16,384]{1,0:T(8,128)S(1)} %get-tuple-element.19), channel_id=1, source_target_pairs={{0,2},{1,3},{2,0},{3,1},{4,6},{5,7},{6,4},{7,5},{8,10},{9,11},{10,... | collective-permute-start | bytes 73736 | tf_op jit(solution)/shard_map/ppermute | solution.py:308
  8.6 6.9 %collective-permute-start.4 = (f32[320,128]{1,0:T(8,128)S(1)}, f32[320,128]{1,0:T(8,128)S(1)}, u32[]{:S(2)}, u32[]{:S(2)}) collective-permute-start(f32[320,128]{1,0:T(8,128)S(1)} %shard_map.132._), channel_id=1, source_target_pairs={{0,16},{8,24},{16,0},{24,8},{1,17},{9,25},{17,1},{25,9},{2,18},{10... | collective-permute-start | bytes 491528 | tf_op jit(solution)/shard_map/ppermute | solution.py:295
  11.3 4.2 %collective-permute-start.5 = (f32[32,384]{1,0:T(8,128)S(1)}, f32[32,384]{1,0:T(8,128)S(1)}, u32[]{:S(2)}, u32[]{:S(2)}) collective-permute-start(f32[32,384]{1,0:T(8,128)S(1)} %pad_maximum_fusion.1), channel_id=1, source_target_pairs={{0,1},{1,0},{2,3},{3,2},{4,5},{5,4},{6,7},{7,6},{8,9},{9,8},{10,11... | collective-permute-start | bytes 147464 | tf_op jit(solution)/shard_map/ppermute | solution.py:308

commit v4 on v3

--- a/solution.py
+++ b/solution.py
@@ -52,33 +52,33 @@
     return count & (count - 1) == 0
 
 
-def stages_of(zones):
+def turns_of(radix, first):
+    if radix == 4 and first:
+        return ((0, 1, 2, 3), (1, 3, 2, 0), (2, 1, 0, 3), (3, 0, 1, 2), (0, 2, 3, 1))
+    return tuple(tuple(digit ^ turn for digit in range(radix)) for turn in range(radix))
+
+
+def stages_of(zones, instances):
     stages = []
     shift = zones.bit_length() - 1
     while shift:
         bits = 2 if shift > 1 else 1
         shift -= bits
-        stages.append((1 << bits, shift))
+        stages.append((turns_of(1 << bits, not stages and instances > 1), shift))
     return stages
-
-
-def turns_of(radix):
-    if radix == 4:
-        return ((0, 1, 2, 3), (2, 3, 1, 0), (3, 2, 0, 1), (1, 0, 3, 2))
-    return tuple(tuple(digit ^ turn for digit in range(radix)) for turn in range(radix))
 
 
 def block_of(owner, me, stages):
     place = jnp.zeros_like(owner)
-    for radix, shift in stages:
-        turns = turns_of(radix)
+    for turns, shift in stages:
+        radix = len(turns[0])
         mine = (me >> shift) & (radix - 1)
         theirs = (owner >> shift) & (radix - 1)
         turn = jnp.zeros_like(owner)
-        for which in range(1, radix):
+        for which in range(1, len(turns)):
             target = chosen(turns[which], mine, jnp.int32)
-            turn = jnp.where(theirs == target, which, turn)
-        place = place * radix + turn
+            turn = jnp.where((theirs == target) & (theirs != mine), which, turn)
+        place = place * len(turns) + turn
     return place
 
 
@@ -273,46 +273,60 @@
     updated[...] = held[0][...] - rows[0:1, :] * kept
 
 
-def ordered_kernel(_, *refs):
-    half = len(refs) // 2
-    for origin, target in zip(refs[:half], refs[half:], strict=True):
-        target[...] = origin[...]
-
-
-def ordered(after, *values):
-    return pl.pallas_call(
-        ordered_kernel,
-        out_shape=tuple(jax.ShapeDtypeStruct(value.shape, value.dtype) for value in values),
-        in_specs=[VMEM] * (1 + len(values)),
-        out_specs=(VMEM,) * len(values),
-        compiler_params=ROOM,
-        cost_estimate=FREE,
-    )(after, *values)
-
-
 def moved(value, axis, mask):
     count = lax.axis_size(axis)
     return lax.ppermute(value, axis, [(place, place ^ mask) for place in range(count)])
 
 
 def stage_sent(sends, stage):
-    radix, shift = stage
-    turns = turns_of(radix)
-    zones = lax.axis_size("zone")
+    turns, shift = stage
+    radix = len(turns[0])
+    instances, zones = lax.axis_size("inst"), lax.axis_size("zone")
     held = [sends[0]]
-    for which in range(1, radix):
+    for which in range(1, len(turns)):
         pairs = []
-        for place in range(zones):
-            digit = (place >> shift) & (radix - 1)
-            pairs.append((place, place + ((turns[which][digit] - digit) << shift)))
-        held.append(lax.ppermute(sends[which], "zone", pairs))
+        for inst in range(instances):
+            for zone in range(zones):
+                digit = (zone >> shift) & (radix - 1)
+                step = turns[which][digit] - digit
+                place = inst * zones + zone
+                target = place + (step << shift) if step else (inst ^ 1) * zones + zone
+                pairs.append((place, target))
+        held.append(lax.ppermute(sends[which], ("inst", "zone"), pairs))
     return held
 
 
-def regrouped(held, radix):
-    lanes = held[0].shape[1]
-    cut = [piece.reshape(radix, -1, lanes) for piece in held]
-    return [jnp.concatenate([piece[which] for piece in cut], axis=0) for which in range(radix)]
+def regroup_kernel(stage, _, *refs):
+    turns, shift = stage
+    radix = len(turns[0])
+    held, outs = refs[: len(turns)], refs[len(turns) :]
+    mine = (lax.axis_index("zone") >> shift) & (radix - 1)
+    came = [[turn for turn in range(1, len(turns)) if turns[turn][d] != d] for d in range(radix)]
+    pieces = [held[0][...]]
+    for order in range(radix - 1):
+        source = [came[digit][order] for digit in range(radix)]
+        piece = held[source[0]][...]
+        for digit in range(1, radix):
+            if source[digit] != source[0]:
+                piece = jnp.where(mine == digit, held[source[digit]][...], piece)
+        pieces.append(piece)
+    rows = pieces[0].shape[0] // len(outs)
+    for which, out in enumerate(outs):
+        for place, piece in enumerate(pieces):
+            out[pl.ds(place * rows, rows), :] = piece[which * rows : (which + 1) * rows]
+
+
+def regrouped(held, stage, next_turns, after):
+    radix = len(stage[0][0])
+    rows, lanes = held[0].shape
+    out = jax.ShapeDtypeStruct((radix * rows // next_turns, lanes), jnp.float32)
+    return pl.pallas_call(
+        functools.partial(regroup_kernel, stage),
+        out_shape=(out,) * next_turns,
+        in_specs=[VMEM] * (1 + len(held)),
+        out_specs=(VMEM,) * next_turns,
+        compiler_params=ROOM,
+    )(after, *held)
 
 
 def on_device(
@@ -336,14 +350,14 @@
     width, clusters = state_in.shape
     links = link_src.shape[1]
     slots_per = 2 * links // zones
-    slots = zones * slots_per
     padded = -(-(width + 1) // LANES) * LANES
     table = coefficients(instances)
     block = jax.ShapeDtypeStruct((width, clusters), jnp.float32)
 
-    stages = stages_of(zones)
-    first = stages[0][0]
-    share = jax.ShapeDtypeStruct((slots // first, padded), jnp.float32)
+    stages = stages_of(zones, instances)
+    turns = [len(stage[0]) for stage in stages] + [1]
+    first = turns[0]
+    share = jax.ShapeDtypeStruct((math.prod(turns[1:]) * slots_per, padded), jnp.float32)
     state_t, *sends = pl.pallas_call(
         functools.partial(outgoing_kernel, stages, slots_per),
         out_shape=(block, *[share] * first),
@@ -371,14 +385,21 @@
     others = []
     if instances > 1:
         (combined,) = pl.pallas_call(
-            functools.partial(combine_kernel, table, held_by, mask),
+            functools.partial(combine_kernel, table, held_by, instances - 1),
             out_shape=(block,),
             in_specs=[VMEM] * len(held),
             out_specs=(VMEM,),
             compiler_params=ROOM,
             cost_estimate=FREE,
         )(*held)
-        others = [moved(combined, "inst", mask)]
+        others = [moved(combined, "inst", instances - 1)]
+
+    pieces = sends
+    for place, stage in enumerate(stages):
+        if place:
+            pieces = regrouped(pieces, stages[place - 1], turns[place], combined)
+        pieces = stage_sent(pieces, stage)
+    staying, *incoming = pieces
 
     kinds = jac_table.shape[0]
     half = pl.pallas_call(
@@ -387,18 +408,13 @@
         in_specs=[VMEM] * 2,
         out_specs=VMEM,
         compiler_params=ROOM,
-    )(state_t, combined)
+    )(state_t, staying)
     products = lax.dot_general(
         jac_table.reshape(kinds * width, width),
         half,
         (((1,), (0,)), ((), ())),
         preferred_element_type=jnp.float32,
     )
-
-    pieces = ordered(products, *stage_sent(sends, stages[0]))
-    for stage in stages[1:]:
-        pieces = stage_sent(regrouped(pieces, stage[0]), stage)
-    staying, *incoming = pieces
 
     column, kind = pattern_col.T, pattern_type.T
     base, rows = pl.pallas_call(

time: 16.6 us -> 15.9 us (0.958)
  waiting for transfers between devices: 1.52 us -> 0.89 us
    ppermute x4 -> x5, waiting for transfers between devices: 1.51 us -> 0.88 us  [stage_sent(): held.append(lax.ppermute(sends[which], ('inst', 'zone'), pairs))]
    ppermute x4 -> x5, starting transfers between devices: 6.89 us -> 6.7 us  [stage_sent(): held.append(lax.ppermute(sends[which], ('inst', 'zone'), pairs))]
  transfers between devices with their start and end apart: 6 -> 7, of which waited for: 3 -> 2; matrix products, arithmetic and copies ran while one was open for 4% -> 4% of each run, Pallas kernels for 9% -> 9%
where the time goes in v4:
time: 15.9 us; the launch traced here: 15.8 us
  starting transfers between devices  8.88 us (56%)
  Pallas kernels  3.97 us (25%)
  between operations  1.35 us (8%)
  waiting for transfers between devices  0.89 us (6%)
  matrix products  0.67 us (4%)
    ppermute x5, starting transfers between devices, stage_sent(): held.append(lax.ppermute(sends[which], ('inst', 'zone'), pairs))  6.7 us
    ppermute x2, starting transfers between devices, moved(): lax.ppermute(value, axis, [(place, place ^ mask) for place in range(count)])  2.18 us
    pallas_call x1, Pallas kernels, on_device(): pl.pallas_call(functools.partial(outgoing_kernel, stages, slots_per), out...  1.53 us
    pallas_call x1, Pallas kernels, on_device(): pl.pallas_call(functools.partial(local_kernel, table), out_shape=(block,...  1.42 us
    pallas_call x1, Pallas kernels, on_device(): pl.pallas_call(functools.partial(final_kernel, table, held_by, len(incomi...  0.96 us
    ppermute x5, waiting for transfers between devices, stage_sent(): held.append(lax.ppermute(sends[which], ('inst', 'zone'), pairs))  0.88 us
    dot_general x1, matrix products, on_device(): lax.dot_general(jac_table.reshape(kinds * width, width), half, (((1,), (0...  0.67 us
  transfers between devices with their start and end apart: 7, of which 2 were waited for; matrix products, arithmetic and copies ran while one was open for 4% of the time, Pallas kernels for 9%

profile of v4, /device:TPU:0, one launch (start us, length us, event | category | flops | bytes accessed | tf_op | source)
XLA Modules:
  0.0 15.8 jit_solution(13417284976129904283)
XLA Ops:
  0.6 0.0 copy-start
  0.6 1.5 %shard_map.131 = (f32[320,128]{1,0:T(8,128)S(1)}, f32[16,384]{1,0:T(8,128)S(1)}, f32[16,384]{1,0:T(8,128)S(1)}, f32[16,384]{1,0:T(8,128)S(1)}, f32[16,384]{1,0:T(8,128)S(1)}, /*index=5*/f32[16,384]{1,0:T(8,128)S(1)}) custom-call(f32[320,128]{1,0:T(8,128)} %bitcast.22, s32[1,32]{1,0:T(1,128)} %source_in.1, s32[1,32]{1,0:T(1,128)} %bitcast.25, ...), custom_call_target="tpu_custom_call" | custom-call | tf_op jit(solution)/shard_map/pallas_call | solution.py:361
  2.2 0.5 %collective-permute-start = (f32[320,128]{1,0:T(8,128)S(1)}, f32[320,128]{1,0:T(8,128)S(1)}, u32[]{:S(2)}, u32[]{:S(2)}) collective-permute-start(f32[320,128]{1,0:T(8,128)S(1)} %get-tuple-element.14.refs_0_.state), channel_id=1, source_target_pairs={{0,8},{8,0},{16,24},{24,16},{1,9},{9,1},{17,25},{25,17},{2,10},{10... | collective-permute-start | bytes 491528 | tf_op jit(solution)/shard_map/ppermute | solution.py:278
  2.7 2.6 %collective-permute-start.1 = (f32[16,384]{1,0:T(8,128)S(1)}, f32[16,384]{1,0:T(8,128)S(1)}, u32[]{:S(2)}, u32[]{:S(2)}) collective-permute-start(f32[16,384]{1,0:T(8,128)S(1)} %get-tuple-element.16), channel_id=1, source_target_pairs={{0,2},{1,3},{2,6},{3,7},{4,12},{5,13},{6,0},{7,1},{8,10},{9,11},{1... | collective-permute-start | bytes 73736 | tf_op jit(solution)/shard_map/ppermute | solution.py:295
  5.3 1.5 %collective-permute-start.2 = (f32[16,384]{1,0:T(8,128)S(1)}, f32[16,384]{1,0:T(8,128)S(1)}, u32[]{:S(2)}, u32[]{:S(2)}) collective-permute-start(f32[16,384]{1,0:T(8,128)S(1)} %get-tuple-element.17), channel_id=1, source_target_pairs={{0,4},{1,5},{2,10},{3,11},{4,0},{5,1},{6,14},{7,15},{8,12},{9,13},... | collective-permute-start | bytes 73736 | tf_op jit(solution)/shard_map/ppermute | solution.py:295
  6.8 1.0 %collective-permute-start.3 = (f32[16,384]{1,0:T(8,128)S(1)}, f32[16,384]{1,0:T(8,128)S(1)}, u32[]{:S(2)}, u32[]{:S(2)}) collective-permute-start(f32[16,384]{1,0:T(8,128)S(1)} %get-tuple-element.18), channel_id=1, source_target_pairs={{0,6},{1,7},{2,0},{3,1},{4,2},{5,3},{6,4},{7,5},{8,14},{9,15},{10,... | collective-permute-start | bytes 73736 | tf_op jit(solution)/shard_map/ppermute | solution.py:295
  7.8 0.0 collective-permute-start.4
  8.5 0.0 collective-permute-done.refs_1_
  8.5 1.7 %collective-permute-start.5 = (f32[320,128]{1,0:T(8,128)S(1)}, f32[320,128]{1,0:T(8,128)S(1)}, u32[]{:S(2)}, u32[]{:S(2)}) collective-permute-start(f32[320,128]{1,0:T(8,128)S(1)} %shard_map.132._), channel_id=1, source_target_pairs={{0,24},{8,16},{16,8},{24,0},{1,25},{9,17},{17,9},{25,1},{2,26},{10... | collective-permute-start | bytes 491528 | tf_op jit(solution)/shard_map/ppermute | solution.py:278
  10.2 0.0 collective-permute-done.1.refs_1_
  10.2 0.0 collective-permute-done.2.refs_2_
  10.2 0.4 %collective-permute-done.3.refs_3_ = f32[16,384]{1,0:T(8,128)S(1)} collective-permute-done((f32[16,384]{1,0:T(8,128)S(1)}, f32[16,384]{1,0:T(8,128)S(1)}, u32[]{:S(2)}, u32[]{:S(2)}) %collective-permute-start.3) | collective-permute-done | bytes 24608 | tf_op jit(solution)/shard_map/ppermute | solution.py:295
  10.6 0.0 collective-permute-done.4.refs_4_
  10.6 1.6 %collective-permute-start.6 = (f32[32,384]{1,0:T(8,128)S(1)}, f32[32,384]{1,0:T(8,128)S(1)}, u32[]{:S(2)}, u32[]{:S(2)}) collective-permute-start(f32[32,384]{1,0:T(8,128)S(1)} %get-tuple-element.23), channel_id=1, source_target_pairs={{0,1},{1,0},{2,3},{3,2},{4,5},{5,4},{6,7},{7,6},{8,9},{9,8},{10,11... | collective-permute-start | bytes 147464 | tf_op jit(solution)/shard_map/ppermute | solution.py:295
  12.2 0.0 copy-done
  12.3 0.7 %convolution_bitcast_fusion.products = f32[2560,128]{1,0:T(8,128)S(1)} fusion(bf16[2560,320]{1,0:T(8,128)(2,1)S(1)} %bitcast.20, bf16[320,128]{1,0:T(8,128)(2,1)S(1)} %shard_map.134), kind=kOutput, calls=%fused_computation | convolution fusion | flops 209715200 | bytes 3031040 | tf_op jit(solution)/shard_map/dot_general | solution.py:412
  12.9 1.4 %shard_map.135 = (f32[320,128]{1,0:T(8,128)S(1)}, f32[8,128]{1,0:T(8,128)S(1)}) custom-call(s32[4,128]{1,0:T(4,128)} %bitcast.23, s32[4,128]{1,0:T(4,128)} %bitcast.24, f32[320,128]{1,0:T(8,128)} %bitcast.21, f32[1,128]{1,0:T(1,128)} %step_in.1, s32[1]{0:T(128)S(6)} %copy.16.count, f32[320,128]{1,0:T(8,128)S(1)} %get-tuple-element.14.refs_0_.state, ...), custom_call_target="tpu_custom_call" | custom-call | flops 1 | bytes 1 | tf_op jit(solution)/shard_map/pallas_call | solution.py:420
  14.3 0.4 %collective-permute-done.6.refs_3_ = f32[32,384]{1,0:T(8,128)S(1)} collective-permute-done((f32[32,384]{1,0:T(8,128)S(1)}, f32[32,384]{1,0:T(8,128)S(1)}, u32[]{:S(2)}, u32[]{:S(2)}) %collective-permute-start.6) | collective-permute-done | bytes 49184 | tf_op jit(solution)/shard_map/ppermute | solution.py:295
  14.8 0.0 collective-permute-done.5.refs_2_
  14.8 1.0 %shard_map.136 = (f32[320,128]{1,0:T(8,128)}, f32[320,128]{1,0:T(8,128)}) custom-call(f32[320,128]{1,0:T(8,128)S(1)} %get-tuple-element.21.base, f32[8,128]{1,0:T(8,128)S(1)} %get-tuple-element.22.rows, f32[320,128]{1,0:T(8,128)S(1)} %get-tuple-element.14.refs_0_.state, f32[320,128]{1,0:T(8,128)S(1)} %collective-permute-done.refs_1_, ...), custom_call_target="tpu_custom_call" | custom-call | tf_op jit(solution)/shard_map/pallas_call | solution.py:444
  (3 shorter events, 0.1 us)
Async XLA Ops:
  0.6 11.6 %copy-start = (bf16[8,320,320]{2,1,0:T(8,128)(2,1)S(1)}, bf16[8,320,320]{2,1,0:T(8,128)(2,1)}, u32[]{:S(2)}) copy-start(bf16[8,320,320]{2,1,0:T(8,128)(2,1)} %param.14) | copy-start | bytes 4915204
  2.2 6.3 %collective-permute-start = (f32[320,128]{1,0:T(8,128)S(1)}, f32[320,128]{1,0:T(8,128)S(1)}, u32[]{:S(2)}, u32[]{:S(2)}) collective-permute-start(f32[320,128]{1,0:T(8,128)S(1)} %get-tuple-element.14.refs_0_.state), channel_id=1, source_target_pairs={{0,8},{8,0},{16,24},{24,16},{1,9},{9,1},{17,25},{25,17},{2,10},{10... | collective-permute-start | bytes 491528 | tf_op jit(solution)/shard_map/ppermute | solution.py:278
  2.7 7.5 %collective-permute-start.1 = (f32[16,384]{1,0:T(8,128)S(1)}, f32[16,384]{1,0:T(8,128)S(1)}, u32[]{:S(2)}, u32[]{:S(2)}) collective-permute-start(f32[16,384]{1,0:T(8,128)S(1)} %get-tuple-element.16), channel_id=1, source_target_pairs={{0,2},{1,3},{2,6},{3,7},{4,12},{5,13},{6,0},{7,1},{8,10},{9,11},{1... | collective-permute-start | bytes 73736 | tf_op jit(solution)/shard_map/ppermute | solution.py:295
  5.3 4.9 %collective-permute-start.2 = (f32[16,384]{1,0:T(8,128)S(1)}, f32[16,384]{1,0:T(8,128)S(1)}, u32[]{:S(2)}, u32[]{:S(2)}) collective-permute-start(f32[16,384]{1,0:T(8,128)S(1)} %get-tuple-element.17), channel_id=1, source_target_pairs={{0,4},{1,5},{2,10},{3,11},{4,0},{5,1},{6,14},{7,15},{8,12},{9,13},... | collective-permute-start | bytes 73736 | tf_op jit(solution)/shard_map/ppermute | solution.py:295
  6.8 3.8 %collective-permute-start.3 = (f32[16,384]{1,0:T(8,128)S(1)}, f32[16,384]{1,0:T(8,128)S(1)}, u32[]{:S(2)}, u32[]{:S(2)}) collective-permute-start(f32[16,384]{1,0:T(8,128)S(1)} %get-tuple-element.18), channel_id=1, source_target_pairs={{0,6},{1,7},{2,0},{3,1},{4,2},{5,3},{6,4},{7,5},{8,14},{9,15},{10,... | collective-permute-start | bytes 73736 | tf_op jit(solution)/shard_map/ppermute | solution.py:295
  7.8 2.8 %collective-permute-start.4 = (f32[16,384]{1,0:T(8,128)S(1)}, f32[16,384]{1,0:T(8,128)S(1)}, u32[]{:S(2)}, u32[]{:S(2)}) collective-permute-start(f32[16,384]{1,0:T(8,128)S(1)} %get-tuple-element.19), channel_id=1, source_target_pairs={{0,8},{1,9},{2,4},{3,5},{4,6},{5,7},{6,2},{7,3},{8,0},{9,1},{10,12... | collective-permute-start | bytes 73736 | tf_op jit(solution)/shard_map/ppermute | solution.py:295
  8.5 6.3 %collective-permute-start.5 = (f32[320,128]{1,0:T(8,128)S(1)}, f32[320,128]{1,0:T(8,128)S(1)}, u32[]{:S(2)}, u32[]{:S(2)}) collective-permute-start(f32[320,128]{1,0:T(8,128)S(1)} %shard_map.132._), channel_id=1, source_target_pairs={{0,24},{8,16},{16,8},{24,0},{1,25},{9,17},{17,9},{25,1},{2,26},{10... | collective-permute-start | bytes 491528 | tf_op jit(solution)/shard_map/ppermute | solution.py:278
  10.6 4.2 %collective-permute-start.6 = (f32[32,384]{1,0:T(8,128)S(1)}, f32[32,384]{1,0:T(8,128)S(1)}, u32[]{:S(2)}, u32[]{:S(2)}) collective-permute-start(f32[32,384]{1,0:T(8,128)S(1)} %get-tuple-element.23), channel_id=1, source_target_pairs={{0,1},{1,0},{2,3},{3,2},{4,5},{5,4},{6,7},{7,6},{8,9},{9,8},{10,11... | collective-permute-start | bytes 147464 | tf_op jit(solution)/shard_map/ppermute | solution.py:295

commit v5 on v4

--- a/solution.py
+++ b/solution.py
@@ -52,20 +52,24 @@
     return count & (count - 1) == 0
 
 
-def turns_of(radix, first):
-    if radix == 4 and first:
+def turns_of(radix, last):
+    if radix == 4 and last:
         return ((0, 1, 2, 3), (1, 3, 2, 0), (2, 1, 0, 3), (3, 0, 1, 2), (0, 2, 3, 1))
     return tuple(tuple(digit ^ turn for digit in range(radix)) for turn in range(radix))
 
 
 def stages_of(zones, instances):
     stages = []
-    shift = zones.bit_length() - 1
-    while shift:
-        bits = 2 if shift > 1 else 1
-        shift -= bits
-        stages.append((turns_of(1 << bits, not stages and instances > 1), shift))
+    shift, top = 0, zones.bit_length() - 1
+    while shift < top:
+        bits = 1 if (top - shift) % 2 else 2
+        stages.append((turns_of(1 << bits, shift and shift + bits == top and instances > 1), shift))
+        shift += bits
     return stages
+
+
+def used_turns(turns, digit):
+    return [turn for turn in range(1, len(turns)) if turns[turn][digit] != digit]
 
 
 def block_of(owner, me, stages):
@@ -74,11 +78,15 @@
         radix = len(turns[0])
         mine = (me >> shift) & (radix - 1)
         theirs = (owner >> shift) & (radix - 1)
-        turn = jnp.zeros_like(owner)
-        for which in range(1, len(turns)):
-            target = chosen(turns[which], mine, jnp.int32)
-            turn = jnp.where((theirs == target) & (theirs != mine), which, turn)
-        place = place * len(turns) + turn
+        order = jnp.zeros_like(owner)
+        for target in range(radix):
+            orders = [0] * radix
+            for digit in range(radix):
+                for which, turn in enumerate(used_turns(turns, digit)):
+                    if turns[turn][digit] == target:
+                        orders[digit] = which + 1
+            order = jnp.where(theirs == target, chosen(orders, mine, jnp.int32), order)
+        place = place * radix + order
     return place
 
 
@@ -296,35 +304,43 @@
     return held
 
 
-def regroup_kernel(stage, _, *refs):
+def regroup_kernel(stage, unit, _, *refs):
     turns, shift = stage
     radix = len(turns[0])
-    held, outs = refs[: len(turns)], refs[len(turns) :]
+    outs = refs[-len(turns) :]
+    block = unit // radix
     mine = (lax.axis_index("zone") >> shift) & (radix - 1)
-    came = [[turn for turn in range(1, len(turns)) if turns[turn][d] != d] for d in range(radix)]
-    pieces = [held[0][...]]
-    for order in range(radix - 1):
-        source = [came[digit][order] for digit in range(radix)]
-        piece = held[source[0]][...]
-        for digit in range(1, radix):
-            if source[digit] != source[0]:
-                piece = jnp.where(mine == digit, held[source[digit]][...], piece)
-        pieces.append(piece)
-    rows = pieces[0].shape[0] // len(outs)
-    for which, out in enumerate(outs):
-        for place, piece in enumerate(pieces):
-            out[pl.ds(place * rows, rows), :] = piece[which * rows : (which + 1) * rows]
-
-
-def regrouped(held, stage, next_turns, after):
-    radix = len(stage[0][0])
-    rows, lanes = held[0].shape
-    out = jax.ShapeDtypeStruct((radix * rows // next_turns, lanes), jnp.float32)
+    used = [used_turns(turns, digit) for digit in range(radix)]
+    place = 0
+    for ref in refs[: -len(turns)]:
+        for start in range(0, ref.shape[0], unit):
+            blocks = [ref[pl.ds(start + which * block, block), :] for which in range(radix)]
+            rows = pl.ds(place * block, block)
+            place += 1
+            outs[0][rows, :] = blocks[0]
+            for turn in range(1, len(turns)):
+                value = None
+                for which in range(radix - 1):
+                    digits = [digit for digit in range(radix) if used[digit][which] == turn]
+                    if len(digits) == radix:
+                        value = blocks[which + 1]
+                    elif digits:
+                        here = chosen([int(digit in digits) for digit in range(radix)], mine, jnp.int32)
+                        value = jnp.zeros_like(blocks[0]) if value is None else value
+                        value = jnp.where(here == 1, blocks[which + 1], value)
+                outs[turn][rows, :] = value
+
+
+def regrouped(held, stage, unit, after):
+    turns = stage[0]
+    lanes = held[0].shape[1]
+    rows = sum(piece.shape[0] for piece in held) // len(turns[0])
+    out = jax.ShapeDtypeStruct((rows, lanes), jnp.float32)
     return pl.pallas_call(
-        functools.partial(regroup_kernel, stage),
-        out_shape=(out,) * next_turns,
+        functools.partial(regroup_kernel, stage, unit),
+        out_shape=(out,) * len(turns),
         in_specs=[VMEM] * (1 + len(held)),
-        out_specs=(VMEM,) * next_turns,
+        out_specs=(VMEM,) * len(turns),
         compiler_params=ROOM,
     )(after, *held)
 
@@ -355,9 +371,11 @@
     block = jax.ShapeDtypeStruct((width, clusters), jnp.float32)
 
     stages = stages_of(zones, instances)
-    turns = [len(stage[0]) for stage in stages] + [1]
-    first = turns[0]
-    share = jax.ShapeDtypeStruct((math.prod(turns[1:]) * slots_per, padded), jnp.float32)
+    units = [zones * slots_per]
+    for turns, _ in stages:
+        units.append(units[-1] // len(turns[0]))
+    first = len(stages[0][0])
+    share = jax.ShapeDtypeStruct((units[1], padded), jnp.float32)
     state_t, *sends = pl.pallas_call(
         functools.partial(outgoing_kernel, stages, slots_per),
         out_shape=(block, *[share] * first),
@@ -397,7 +415,7 @@
     pieces = sends
     for place, stage in enumerate(stages):
         if place:
-            pieces = regrouped(pieces, stages[place - 1], turns[place], combined)
+            pieces = regrouped(pieces, stage, units[place], combined)
         pieces = stage_sent(pieces, stage)
     staying, *incoming = pieces
 

time: 15.9 us -> 15.6 us (0.981)
  starting transfers between devices: 8.88 us -> 8.63 us
    ppermute x2, starting transfers between devices: 2.18 us -> 1.85 us  [moved(): lax.ppermute(value, axis, [(place, place ^ mask) for place in range(count)])]
  transfers between devices with their start and end apart: 7 -> 7, of which waited for: 2 -> 3; matrix products, arithmetic and copies ran while one was open for 4% -> 4% of each run, Pallas kernels for 9% -> 10%
where the time goes in v5:
time: 15.6 us; the launch traced here: 15.5 us
  starting transfers between devices  8.63 us (55%)
  Pallas kernels  3.96 us (25%)
  between operations  1.36 us (9%)
  waiting for transfers between devices  0.83 us (5%)
  matrix products  0.67 us (4%)
    ppermute x5, starting transfers between devices, stage_sent(): held.append(lax.ppermute(sends[which], ('inst', 'zone'), pairs))  6.79 us
    ppermute x2, starting transfers between devices, moved(): lax.ppermute(value, axis, [(place, place ^ mask) for place in range(count)])  1.85 us
    pallas_call x1, Pallas kernels, on_device(): pl.pallas_call(functools.partial(outgoing_kernel, stages, slots_per), out...  1.48 us
    pallas_call x1, Pallas kernels, on_device(): pl.pallas_call(functools.partial(local_kernel, table), out_shape=(block,...  1.42 us
    pallas_call x1, Pallas kernels, on_device(): pl.pallas_call(functools.partial(final_kernel, table, held_by, len(incomi...  1.01 us
    ppermute x5, waiting for transfers between devices, stage_sent(): held.append(lax.ppermute(sends[which], ('inst', 'zone'), pairs))  0.82 us
    dot_general x1, matrix products, on_device(): lax.dot_general(jac_table.reshape(kinds * width, width), half, (((1,), (0...  0.67 us
  transfers between devices with their start and end apart: 7, of which 3 were waited for; matrix products, arithmetic and copies ran while one was open for 4% of the time, Pallas kernels for 10%

profile of v5, /device:TPU:0, one launch (start us, length us, event | category | flops | bytes accessed | tf_op | source)
XLA Modules:
  0.0 15.5 jit_solution(9674003530181461843)
XLA Ops:
  0.6 0.0 copy-start
  0.6 1.5 %shard_map.131 = (f32[320,128]{1,0:T(8,128)S(1)}, f32[32,384]{1,0:T(8,128)S(1)}, f32[32,384]{1,0:T(8,128)S(1)}) custom-call(f32[320,128]{1,0:T(8,128)} %bitcast.21, s32[1,32]{1,0:T(1,128)} %source_in.1, s32[1,32]{1,0:T(1,128)} %bitcast.25, s32[1,32]{1,0:T(1,128)} %dest_in.1, s32[1,32]{1,0:T(1,128)} %weight_in.1, f32[16,320]{1,0:T(8,128)} %table_in.1), custom_call_target="tpu_custom_call" | custom-call | tf_op jit(solution)/shard_map/pallas_call | solution.py:379
  2.1 0.5 %collective-permute-start = (f32[320,128]{1,0:T(8,128)S(1)}, f32[320,128]{1,0:T(8,128)S(1)}, u32[]{:S(2)}, u32[]{:S(2)}) collective-permute-start(f32[320,128]{1,0:T(8,128)S(1)} %get-tuple-element.14.refs_0_.state), channel_id=1, source_target_pairs={{0,8},{8,0},{16,24},{24,16},{1,9},{9,1},{17,25},{25,17},{2,10},{10... | collective-permute-start | bytes 491528 | tf_op jit(solution)/shard_map/ppermute | solution.py:286
  2.7 2.6 %collective-permute-start.1 = (f32[32,384]{1,0:T(8,128)S(1)}, f32[32,384]{1,0:T(8,128)S(1)}, u32[]{:S(2)}, u32[]{:S(2)}) collective-permute-start(f32[32,384]{1,0:T(8,128)S(1)} %get-tuple-element.16), channel_id=1, source_target_pairs={{0,1},{1,0},{2,3},{3,2},{4,5},{5,4},{6,7},{7,6},{8,9},{9,8},{10,11... | collective-permute-start | bytes 147464 | tf_op jit(solution)/shard_map/ppermute | solution.py:303
  5.9 0.0 collective-permute-done.refs_1_
  6.0 1.3 %collective-permute-start.2 = (f32[320,128]{1,0:T(8,128)S(1)}, f32[320,128]{1,0:T(8,128)S(1)}, u32[]{:S(2)}, u32[]{:S(2)}) collective-permute-start(f32[320,128]{1,0:T(8,128)S(1)} %shard_map.132._), channel_id=1, source_target_pairs={{0,24},{8,16},{16,8},{24,0},{1,25},{9,17},{17,9},{25,1},{2,26},{10... | collective-permute-start | bytes 491528 | tf_op jit(solution)/shard_map/ppermute | solution.py:286
  7.3 0.3 %collective-permute-done.1.refs_1_ = f32[32,384]{1,0:T(8,128)S(1)} collective-permute-done((f32[32,384]{1,0:T(8,128)S(1)}, f32[32,384]{1,0:T(8,128)S(1)}, u32[]{:S(2)}, u32[]{:S(2)}) %collective-permute-start.1) | collective-permute-done | bytes 49184 | tf_op jit(solution)/shard_map/ppermute | solution.py:303
  7.6 1.9 %collective-permute-start.3 = (f32[16,384]{1,0:T(8,128)S(1)}, f32[16,384]{1,0:T(8,128)S(1)}, u32[]{:S(2)}, u32[]{:S(2)}) collective-permute-start(f32[16,384]{1,0:T(8,128)S(1)} %get-tuple-element.20), channel_id=1, source_target_pairs={{0,2},{1,3},{2,6},{3,7},{4,12},{5,13},{6,0},{7,1},{8,10},{9,11},{1... | collective-permute-start | bytes 73736 | tf_op jit(solution)/shard_map/ppermute | solution.py:303
  9.5 1.1 %collective-permute-start.4 = (f32[16,384]{1,0:T(8,128)S(1)}, f32[16,384]{1,0:T(8,128)S(1)}, u32[]{:S(2)}, u32[]{:S(2)}) collective-permute-start(f32[16,384]{1,0:T(8,128)S(1)} %get-tuple-element.21), channel_id=1, source_target_pairs={{0,4},{1,5},{2,10},{3,11},{4,0},{5,1},{6,14},{7,15},{8,12},{9,13},... | collective-permute-start | bytes 73736 | tf_op jit(solution)/shard_map/ppermute | solution.py:303
  10.6 1.1 %collective-permute-start.5 = (f32[16,384]{1,0:T(8,128)S(1)}, f32[16,384]{1,0:T(8,128)S(1)}, u32[]{:S(2)}, u32[]{:S(2)}) collective-permute-start(f32[16,384]{1,0:T(8,128)S(1)} %get-tuple-element.22), channel_id=1, source_target_pairs={{0,6},{1,7},{2,0},{3,1},{4,2},{5,3},{6,4},{7,5},{8,14},{9,15},{10,... | collective-permute-start | bytes 73736 | tf_op jit(solution)/shard_map/ppermute | solution.py:303
  11.6 0.2 %collective-permute-start.6 = (f32[16,384]{1,0:T(8,128)S(1)}, f32[16,384]{1,0:T(8,128)S(1)}, u32[]{:S(2)}, u32[]{:S(2)}) collective-permute-start(f32[16,384]{1,0:T(8,128)S(1)} %get-tuple-element.23), channel_id=1, source_target_pairs={{0,8},{1,9},{2,4},{3,5},{4,6},{5,7},{6,2},{7,3},{8,0},{9,1},{10,12... | collective-permute-start | bytes 73736 | tf_op jit(solution)/shard_map/ppermute | solution.py:303
  11.8 0.0 copy-done
  11.8 0.7 %convolution_bitcast_fusion.products = f32[2560,128]{1,0:T(8,128)S(1)} fusion(bf16[2560,320]{1,0:T(8,128)(2,1)S(1)} %bitcast.20, bf16[320,128]{1,0:T(8,128)(2,1)S(1)} %shard_map.134), kind=kOutput, calls=%fused_computation | convolution fusion | flops 209715200 | bytes 3031040 | tf_op jit(solution)/shard_map/dot_general | solution.py:430
  12.5 1.4 %shard_map.135 = (f32[320,128]{1,0:T(8,128)S(1)}, f32[8,128]{1,0:T(8,128)S(1)}) custom-call(s32[4,128]{1,0:T(4,128)} %bitcast.23, s32[4,128]{1,0:T(4,128)} %bitcast.24, f32[320,128]{1,0:T(8,128)} %bitcast.22, f32[1,128]{1,0:T(1,128)} %step_in.1, s32[1]{0:T(128)S(6)} %copy.16.count, f32[320,128]{1,0:T(8,128)S(1)} %get-tuple-element.14.refs_0_.state, ...), custom_call_target="tpu_custom_call" | custom-call | flops 1 | bytes 1 | tf_op jit(solution)/shard_map/pallas_call | solution.py:438
  13.9 0.0 collective-permute-done.3.refs_3_
  13.9 0.3 %collective-permute-done.4.refs_4_ = f32[16,384]{1,0:T(8,128)S(1)} collective-permute-done((f32[16,384]{1,0:T(8,128)S(1)}, f32[16,384]{1,0:T(8,128)S(1)}, u32[]{:S(2)}, u32[]{:S(2)}) %collective-permute-start.4) | collective-permute-done | bytes 24608 | tf_op jit(solution)/shard_map/ppermute | solution.py:303
  14.2 0.3 %collective-permute-done.5.refs_5_ = f32[16,384]{1,0:T(8,128)S(1)} collective-permute-done((f32[16,384]{1,0:T(8,128)S(1)}, f32[16,384]{1,0:T(8,128)S(1)}, u32[]{:S(2)}, u32[]{:S(2)}) %collective-permute-start.5) | collective-permute-done | bytes 24608 | tf_op jit(solution)/shard_map/ppermute | solution.py:303
  14.5 0.0 collective-permute-done.6.refs_6_
  14.5 0.0 collective-permute-done.2.refs_2_
  14.5 1.0 %shard_map.136 = (f32[320,128]{1,0:T(8,128)}, f32[320,128]{1,0:T(8,128)}) custom-call(f32[320,128]{1,0:T(8,128)S(1)} %get-tuple-element.18.base, f32[8,128]{1,0:T(8,128)S(1)} %get-tuple-element.19.rows, f32[320,128]{1,0:T(8,128)S(1)} %get-tuple-element.14.refs_0_.state, f32[320,128]{1,0:T(8,128)S(1)} %collective-permute-done.refs_1_, ...), custom_call_target="tpu_custom_call" | custom-call | tf_op jit(solution)/shard_map/pallas_call | solution.py:462
  (3 shorter events, 0.1 us)
Async XLA Ops:
  0.6 11.2 %copy-start = (bf16[8,320,320]{2,1,0:T(8,128)(2,1)S(1)}, bf16[8,320,320]{2,1,0:T(8,128)(2,1)}, u32[]{:S(2)}) copy-start(bf16[8,320,320]{2,1,0:T(8,128)(2,1)} %param.14) | copy-start | bytes 4915204
  2.1 3.8 %collective-permute-start = (f32[320,128]{1,0:T(8,128)S(1)}, f32[320,128]{1,0:T(8,128)S(1)}, u32[]{:S(2)}, u32[]{:S(2)}) collective-permute-start(f32[320,128]{1,0:T(8,128)S(1)} %get-tuple-element.14.refs_0_.state), channel_id=1, source_target_pairs={{0,8},{8,0},{16,24},{24,16},{1,9},{9,1},{17,25},{25,17},{2,10},{10... | collective-permute-start | bytes 491528 | tf_op jit(solution)/shard_map/ppermute | solution.py:286
  2.7 4.9 %collective-permute-start.1 = (f32[32,384]{1,0:T(8,128)S(1)}, f32[32,384]{1,0:T(8,128)S(1)}, u32[]{:S(2)}, u32[]{:S(2)}) collective-permute-start(f32[32,384]{1,0:T(8,128)S(1)} %get-tuple-element.16), channel_id=1, source_target_pairs={{0,1},{1,0},{2,3},{3,2},{4,5},{5,4},{6,7},{7,6},{8,9},{9,8},{10,11... | collective-permute-start | bytes 147464 | tf_op jit(solution)/shard_map/ppermute | solution.py:303
  6.0 8.5 %collective-permute-start.2 = (f32[320,128]{1,0:T(8,128)S(1)}, f32[320,128]{1,0:T(8,128)S(1)}, u32[]{:S(2)}, u32[]{:S(2)}) collective-permute-start(f32[320,128]{1,0:T(8,128)S(1)} %shard_map.132._), channel_id=1, source_target_pairs={{0,24},{8,16},{16,8},{24,0},{1,25},{9,17},{17,9},{25,1},{2,26},{10... | collective-permute-start | bytes 491528 | tf_op jit(solution)/shard_map/ppermute | solution.py:286
  7.6 6.3 %collective-permute-start.3 = (f32[16,384]{1,0:T(8,128)S(1)}, f32[16,384]{1,0:T(8,128)S(1)}, u32[]{:S(2)}, u32[]{:S(2)}) collective-permute-start(f32[16,384]{1,0:T(8,128)S(1)} %get-tuple-element.20), channel_id=1, source_target_pairs={{0,2},{1,3},{2,6},{3,7},{4,12},{5,13},{6,0},{7,1},{8,10},{9,11},{1... | collective-permute-start | bytes 73736 | tf_op jit(solution)/shard_map/ppermute | solution.py:303
  9.5 4.7 %collective-permute-start.4 = (f32[16,384]{1,0:T(8,128)S(1)}, f32[16,384]{1,0:T(8,128)S(1)}, u32[]{:S(2)}, u32[]{:S(2)}) collective-permute-start(f32[16,384]{1,0:T(8,128)S(1)} %get-tuple-element.21), channel_id=1, source_target_pairs={{0,4},{1,5},{2,10},{3,11},{4,0},{5,1},{6,14},{7,15},{8,12},{9,13},... | collective-permute-start | bytes 73736 | tf_op jit(solution)/shard_map/ppermute | solution.py:303
  10.6 3.9 %collective-permute-start.5 = (f32[16,384]{1,0:T(8,128)S(1)}, f32[16,384]{1,0:T(8,128)S(1)}, u32[]{:S(2)}, u32[]{:S(2)}) collective-permute-start(f32[16,384]{1,0:T(8,128)S(1)} %get-tuple-element.22), channel_id=1, source_target_pairs={{0,6},{1,7},{2,0},{3,1},{4,2},{5,3},{6,4},{7,5},{8,14},{9,15},{10,... | collective-permute-start | bytes 73736 | tf_op jit(solution)/shard_map/ppermute | solution.py:303
  11.6 2.8 %collective-permute-start.6 = (f32[16,384]{1,0:T(8,128)S(1)}, f32[16,384]{1,0:T(8,128)S(1)}, u32[]{:S(2)}, u32[]{:S(2)}) collective-permute-start(f32[16,384]{1,0:T(8,128)S(1)} %get-tuple-element.23), channel_id=1, source_target_pairs={{0,8},{1,9},{2,4},{3,5},{4,6},{5,7},{6,2},{7,3},{8,0},{9,1},{10,12... | collective-permute-start | bytes 73736 | tf_op jit(solution)/shard_map/ppermute | solution.py:303

commit v6 on v5

--- a/solution.py
+++ b/solution.py
@@ -109,6 +109,7 @@
 def outgoing_kernel(
     stages,
     slots_per,
+    width,
     state_in,
     source_in,
     owner_in,
@@ -125,15 +126,15 @@
             (source_in, source),
             (weight_in, weight),
             (dest_in, dest),
-            (state_in, state),
+            (state_in, state.at[pl.ds(0, width), :]),
             (table_in, table),
         ),
         sems,
     )
-    width, clusters = state.shape
+    clusters = state.shape[1]
     links = owner.shape[1]
     sets = table.shape[0]
-    share, lanes = sends[0].shape
+    share, lanes = sends[-1].shape
     slots = share * len(sends)
     for copy in copies[:4]:
         copy.wait()
@@ -160,23 +161,26 @@
     for part in parts_of(table[...]):
         scales = scales + jnp.dot(choose, part, preferred_element_type=jnp.float32)
     copies[4].wait()
-    parts = jnp.concatenate(parts_of(state[...]), axis=1)
+    parts = jnp.concatenate(parts_of(state[pl.ds(0, width), :]), axis=1)
     picked = lax.dot_general(
         jnp.concatenate([pick, pick, pick], axis=1),
         parts,
         (((1,), (1,)), ((), ())),
         preferred_element_type=jnp.float32,
     )
-    blocks = picked * scales
     marks = jnp.broadcast_to(to_cluster, (slots, lanes - width))
+    blocks = jnp.concatenate([picked * scales, marks], axis=1)
     for place, send in enumerate(sends):
-        rows = slice(place * share, (place + 1) * share)
-        send[:, :width] = blocks[rows]
-        send[:, width:] = marks[rows]
+        send[...] = blocks[place * share : place * share + send.shape[0]]
+    trades = share - sends[0].shape[0]
+    if trades:
+        for start in range(0, lanes, clusters):
+            rows = pl.ds(width + start // clusters * trades, trades)
+            state[rows, :] = blocks[share - trades : share, start : start + clusters]
 
 
 def half_kernel(state, _, half):
-    half[...] = state[...].astype(jnp.bfloat16)
+    half[...] = state[pl.ds(0, half.shape[0]), :].astype(jnp.bfloat16)
 
 
 def landed(pieces, width, clusters):
@@ -209,13 +213,13 @@
     source,
     sems,
 ):
-    width, clusters = state.shape
+    width, clusters = base.shape
     kinds = products.shape[0] // width
     step = rows.at[pl.ds(0, 1), :]
     copies = fetched(
         [(column_in, column), (kind_in, kind), (source_in, source), (step_in, step)], sems
     )
-    total = chosen(table, 0) * state[...] - landed([staying], width, clusters)
+    total = chosen(table, 0) * state[pl.ds(0, width), :] - landed([staying], width, clusters)
     high, low = [], []
     for which in range(kinds):
         full = products[pl.ds(which * width, width), :]
@@ -248,15 +252,11 @@
 def combine_kernel(table, held_by, mask, *refs):
     period = len(table)
     me = lax.axis_index("inst")
-    held, rest = refs[: len(held_by)], refs[len(held_by) :]
-    passing = len(rest) // 2
-    out = rest[passing]
-    for origin, target in zip(rest[:passing], rest[passing + 1 :], strict=True):
-        target[...] = origin[...]
+    *held, out = refs
     total = None
     for by, ref in zip(held_by, held, strict=True):
         shift = ((me ^ mask) - (me ^ by) + period) & (period - 1)
-        term = chosen(table, shift) * ref[...]
+        term = chosen(table, shift) * ref[pl.ds(0, out.shape[0]), :]
         total = term if total is None else total + term
     out[...] = total
 
@@ -272,13 +272,13 @@
     total = base[...]
     for mask, ref in zip(held_by[1:], held[1:], strict=True):
         shift = (me - (me ^ mask) + period) & (period - 1)
-        total = total + chosen(table, shift) * ref[...]
+        total = total + chosen(table, shift) * ref[pl.ds(0, width), :]
     for ref in others:
         total = total + ref[...]
     total = total - landed(incoming, width, clusters)
     kept = jnp.where(rows[1:2, :] > 0.0, total, 0.0)
     residual[...] = kept
-    updated[...] = held[0][...] - rows[0:1, :] * kept
+    updated[...] = held[0][pl.ds(0, width), :] - rows[0:1, :] * kept
 
 
 def moved(value, axis, mask):
@@ -286,7 +286,7 @@
     return lax.ppermute(value, axis, [(place, place ^ mask) for place in range(count)])
 
 
-def stage_sent(sends, stage):
+def stage_sent(sends, stage, crossed=False):
     turns, shift = stage
     radix = len(turns[0])
     instances, zones = lax.axis_size("inst"), lax.axis_size("zone")
@@ -297,9 +297,8 @@
             for zone in range(zones):
                 digit = (zone >> shift) & (radix - 1)
                 step = turns[which][digit] - digit
-                place = inst * zones + zone
-                target = place + (step << shift) if step else (inst ^ 1) * zones + zone
-                pairs.append((place, target))
+                beside = inst ^ 1 if crossed or not step else inst
+                pairs.append((inst * zones + zone, beside * zones + zone + (step << shift)))
         held.append(lax.ppermute(sends[which], ("inst", "zone"), pairs))
     return held
 
@@ -331,6 +330,51 @@
                 outs[turn][rows, :] = value
 
 
+def by_digit(values, mine):
+    value = values[0]
+    for digit in range(1, len(values)):
+        if values[digit] is not values[0]:
+            value = jnp.where(mine == digit, values[digit], value)
+    return value
+
+
+def crossing_kernel(stage, block, _, beside, came, own, staying, *outs):
+    staying[...] = own[...]
+    turns, shift = stage
+    radix = len(turns[0])
+    clusters, lanes = beside.shape[1], came.shape[1]
+    mine = (lax.axis_index("zone") >> shift) & (radix - 1)
+    trades = (radix - 1) * block
+    first = beside.shape[0] - lanes // clusters * trades
+    keeps = [jnp.zeros((block, lanes), jnp.float32)]
+    for which in range(radix - 1):
+        tiles = [
+            beside[pl.ds(first + tile * trades + which * block, block), :]
+            for tile in range(lanes // clusters)
+        ]
+        keeps.append(jnp.concatenate(tiles, axis=1))
+    comes = [came[pl.ds(which * block, block), :] for which in range(radix)]
+    for turn, out in enumerate(outs, 1):
+        orders = []
+        for digit in range(radix):
+            used = used_turns(turns, digit)
+            orders.append(used.index(turn) + 1 if turn in used else 0)
+        out[pl.ds(0, block), :] = by_digit([keeps[order] for order in orders], mine)
+        out[pl.ds(block, block), :] = by_digit([comes[order] for order in orders], mine)
+
+
+def crossing(stage, block, after, beside, came, own):
+    turns = stage[0]
+    out = jax.ShapeDtypeStruct((2 * block, came.shape[1]), jnp.float32)
+    return pl.pallas_call(
+        functools.partial(crossing_kernel, stage, block),
+        out_shape=(jax.ShapeDtypeStruct(own.shape, own.dtype), *[out] * (len(turns) - 1)),
+        in_specs=[VMEM] * 4,
+        out_specs=(VMEM,) * len(turns),
+        compiler_params=ROOM,
+    )(after, beside, came, own)
+
+
 def regrouped(held, stage, unit, after):
     turns = stage[0]
     lanes = held[0].shape[1]
@@ -375,10 +419,17 @@
     for turns, _ in stages:
         units.append(units[-1] // len(turns[0]))
     first = len(stages[0][0])
+    crossed = len(stages) == 2 and len(stages[1][0]) == len(stages[1][0][0]) + 1
+    crossed = crossed and instances >= 4 and clusters == LANES
     share = jax.ShapeDtypeStruct((units[1], padded), jnp.float32)
+    shares, bundle = [share] * first, block
+    if crossed:
+        trades = (units[1] - units[2]) * padded // clusters
+        bundle = jax.ShapeDtypeStruct((width + trades, clusters), jnp.float32)
+        shares[0] = jax.ShapeDtypeStruct((units[2], padded), jnp.float32)
     state_t, *sends = pl.pallas_call(
-        functools.partial(outgoing_kernel, stages, slots_per),
-        out_shape=(block, *[share] * first),
+        functools.partial(outgoing_kernel, stages, slots_per, width),
+        out_shape=(bundle, *shares),
         in_specs=[HBM] * 6,
         out_specs=(VMEM,) * (1 + first),
         scratch_shapes=[pltpu.VMEM((1, links), jnp.int32)] * 4
@@ -412,12 +463,17 @@
         )(*held)
         others = [moved(combined, "inst", instances - 1)]
 
-    pieces = sends
-    for place, stage in enumerate(stages):
-        if place:
-            pieces = regrouped(pieces, stage, units[place], combined)
-        pieces = stage_sent(pieces, stage)
-    staying, *incoming = pieces
+    if crossed:
+        staying, came = stage_sent(sends, stages[0], True)
+        pieces = crossing(stages[1], units[2], combined, held[1], came, staying)
+        staying, *incoming = stage_sent(pieces, stages[1], True)
+    else:
+        pieces = sends
+        for place, stage in enumerate(stages):
+            if place:
+                pieces = regrouped(pieces, stage, units[place], combined)
+            pieces = stage_sent(pieces, stage)
+        staying, *incoming = pieces
 
     kinds = jac_table.shape[0]
     half = pl.pallas_call(

time: 15.6 us -> 15.1 us (0.968)
  waiting for transfers between devices: 0.83 us -> 0.32 us
    ppermute x5, waiting for transfers between devices: 0.82 us -> 0.32 us  [stage_sent(): held.append(lax.ppermute(sends[which], ('inst', 'zone'), pairs))]
  transfers between devices with their start and end apart: 7 -> 7, of which waited for: 3 -> 2; matrix products, arithmetic and copies ran while one was open for 4% -> 4% of each run, Pallas kernels for 10% -> 10%
where the time goes in v6:
time: 15.1 us; the launch traced here: 14.9 us
  starting transfers between devices  8.6 us (57%)
  Pallas kernels  3.96 us (26%)
  between operations  1.36 us (9%)
  matrix products  0.67 us (4%)
  waiting for transfers between devices  0.32 us (2%)
    ppermute x5, starting transfers between devices, stage_sent(): held.append(lax.ppermute(sends[which], ('inst', 'zone'), pairs))  6.85 us
    ppermute x2, starting transfers between devices, moved(): lax.ppermute(value, axis, [(place, place ^ mask) for place in range(count)])  1.75 us
    pallas_call x1, Pallas kernels, on_device(): pl.pallas_call(functools.partial(outgoing_kernel, stages, slots_per, widt...  1.48 us
    pallas_call x1, Pallas kernels, on_device(): pl.pallas_call(functools.partial(local_kernel, table), out_shape=(block,...  1.41 us
    pallas_call x1, Pallas kernels, on_device(): pl.pallas_call(functools.partial(final_kernel, table, held_by, len(incomi...  1.01 us
    dot_general x1, matrix products, on_device(): lax.dot_general(jac_table.reshape(kinds * width, width), half, (((1,), (0...  0.67 us
    ppermute x5, waiting for transfers between devices, stage_sent(): held.append(lax.ppermute(sends[which], ('inst', 'zone'), pairs))  0.32 us
  transfers between devices with their start and end apart: 7, of which 2 were waited for; matrix products, arithmetic and copies ran while one was open for 4% of the time, Pallas kernels for 10%

profile of v6, /device:TPU:0, one launch (start us, length us, event | category | flops | bytes accessed | tf_op | source)
XLA Modules:
  0.0 14.9 jit_solution(15446925685093848734)
XLA Ops:
  0.6 0.0 copy-start
  0.6 1.5 %shard_map.131 = (f32[392,128]{1,0:T(8,128)S(1)}, f32[8,384]{1,0:T(8,128)S(1)}, f32[32,384]{1,0:T(8,128)S(1)}) custom-call(f32[320,128]{1,0:T(8,128)} %bitcast.22, s32[1,32]{1,0:T(1,128)} %source_in.1, s32[1,32]{1,0:T(1,128)} %bitcast.25, s32[1,32]{1,0:T(1,128)} %dest_in.1, s32[1,32]{1,0:T(1,128)} %weight_in.1, f32[16,320]{1,0:T(8,128)} %table_in.1), custom_call_target="tpu_custom_call" | custom-call | tf_op jit(solution)/shard_map/pallas_call | solution.py:430
  2.1 0.5 %collective-permute-start = (f32[392,128]{1,0:T(8,128)S(1)}, f32[392,128]{1,0:T(8,128)S(1)}, u32[]{:S(2)}, u32[]{:S(2)}) collective-permute-start(f32[392,128]{1,0:T(8,128)S(1)} %get-tuple-element.14.refs_0_.state), channel_id=1, source_target_pairs={{0,8},{8,0},{16,24},{24,16},{1,9},{9,1},{17,25},{25,17},{2,10},{10... | collective-permute-start | bytes 602120 | tf_op jit(solution)/shard_map/ppermute | solution.py:286
  2.7 2.6 %collective-permute-start.1 = (f32[32,384]{1,0:T(8,128)S(1)}, f32[32,384]{1,0:T(8,128)S(1)}, u32[]{:S(2)}, u32[]{:S(2)}) collective-permute-start(f32[32,384]{1,0:T(8,128)S(1)} %get-tuple-element.15), channel_id=1, source_target_pairs={{0,9},{1,8},{2,11},{3,10},{4,13},{5,12},{6,15},{7,14},{8,1},{9,0},... | collective-permute-start | bytes 147464 | tf_op jit(solution)/shard_map/ppermute | solution.py:302
  5.9 0.0 collective-permute-done.refs_1_.beside
  6.0 1.2 %collective-permute-start.2 = (f32[320,128]{1,0:T(8,128)S(1)}, f32[320,128]{1,0:T(8,128)S(1)}, u32[]{:S(2)}, u32[]{:S(2)}) collective-permute-start(f32[320,128]{1,0:T(8,128)S(1)} %shard_map.132._), channel_id=1, source_target_pairs={{0,24},{8,16},{16,8},{24,0},{1,25},{9,17},{17,9},{25,1},{2,26},{10... | collective-permute-start | bytes 491528 | tf_op jit(solution)/shard_map/ppermute | solution.py:286
  7.2 0.1 collective-permute-done.1.came
  7.3 1.6 %collective-permute-start.3 = (f32[16,384]{1,0:T(8,128)S(1)}, f32[16,384]{1,0:T(8,128)S(1)}, u32[]{:S(2)}, u32[]{:S(2)}) collective-permute-start(f32[16,384]{1,0:T(8,128)S(1)} %get-tuple-element.20), channel_id=1, source_target_pairs={{0,10},{1,11},{2,14},{3,15},{4,12},{5,13},{6,8},{7,9},{8,2},{9,3},... | collective-permute-start | bytes 73736 | tf_op jit(solution)/shard_map/ppermute | solution.py:302
  8.9 1.1 %collective-permute-start.4 = (f32[16,384]{1,0:T(8,128)S(1)}, f32[16,384]{1,0:T(8,128)S(1)}, u32[]{:S(2)}, u32[]{:S(2)}) collective-permute-start(f32[16,384]{1,0:T(8,128)S(1)} %get-tuple-element.21), channel_id=1, source_target_pairs={{0,12},{1,13},{2,10},{3,11},{4,8},{5,9},{6,14},{7,15},{8,4},{9,5},... | collective-permute-start | bytes 73736 | tf_op jit(solution)/shard_map/ppermute | solution.py:302
  10.0 1.3 %collective-permute-start.5 = (f32[16,384]{1,0:T(8,128)S(1)}, f32[16,384]{1,0:T(8,128)S(1)}, u32[]{:S(2)}, u32[]{:S(2)}) collective-permute-start(f32[16,384]{1,0:T(8,128)S(1)} %get-tuple-element.22), channel_id=1, source_target_pairs={{0,14},{1,15},{2,8},{3,9},{4,10},{5,11},{6,12},{7,13},{8,6},{9,7},... | collective-permute-start | bytes 73736 | tf_op jit(solution)/shard_map/ppermute | solution.py:302
  11.3 0.3 %collective-permute-start.6 = (f32[16,384]{1,0:T(8,128)S(1)}, f32[16,384]{1,0:T(8,128)S(1)}, u32[]{:S(2)}, u32[]{:S(2)}) collective-permute-start(f32[16,384]{1,0:T(8,128)S(1)} %get-tuple-element.23), channel_id=1, source_target_pairs={{0,8},{1,9},{2,12},{3,13},{4,14},{5,15},{6,10},{7,11},{8,0},{9,1},... | collective-permute-start | bytes 73736 | tf_op jit(solution)/shard_map/ppermute | solution.py:302
  11.6 0.0 copy-done
  11.6 0.7 %convolution_bitcast_fusion.products = f32[2560,128]{1,0:T(8,128)S(1)} fusion(bf16[2560,320]{1,0:T(8,128)(2,1)S(1)} %bitcast.20, bf16[320,128]{1,0:T(8,128)(2,1)S(1)} %shard_map.134), kind=kOutput, calls=%fused_computation | convolution fusion | flops 209715200 | bytes 3031040 | tf_op jit(solution)/shard_map/dot_general | solution.py:486
  12.2 1.4 %shard_map.135 = (f32[320,128]{1,0:T(8,128)S(1)}, f32[8,128]{1,0:T(8,128)S(1)}) custom-call(s32[4,128]{1,0:T(4,128)} %bitcast.23, s32[4,128]{1,0:T(4,128)} %bitcast.24, f32[320,128]{1,0:T(8,128)} %bitcast.21, f32[1,128]{1,0:T(1,128)} %step_in.1, s32[1]{0:T(128)S(6)} %copy.16.count, f32[392,128]{1,0:T(8,128)S(1)} %get-tuple-element.14.refs_0_.state, ...), custom_call_target="tpu_custom_call" | custom-call | flops 1 | bytes 1 | tf_op jit(solution)/shard_map/pallas_call | solution.py:494
  13.7 0.0 collective-permute-done.3.refs_3_
  13.7 0.0 collective-permute-done.4.refs_4_
  13.7 0.2 %collective-permute-done.5.refs_5_ = f32[16,384]{1,0:T(8,128)S(1)} collective-permute-done((f32[16,384]{1,0:T(8,128)S(1)}, f32[16,384]{1,0:T(8,128)S(1)}, u32[]{:S(2)}, u32[]{:S(2)}) %collective-permute-start.5) | collective-permute-done | bytes 24608 | tf_op jit(solution)/shard_map/ppermute | solution.py:302
  13.9 0.0 collective-permute-done.6.refs_6_
  13.9 0.0 collective-permute-done.2.refs_2_
  13.9 1.0 %shard_map.136 = (f32[320,128]{1,0:T(8,128)}, f32[320,128]{1,0:T(8,128)}) custom-call(f32[320,128]{1,0:T(8,128)S(1)} %get-tuple-element.18.base, f32[8,128]{1,0:T(8,128)S(1)} %get-tuple-element.19.rows, f32[392,128]{1,0:T(8,128)S(1)} %get-tuple-element.14.refs_0_.state, f32[392,128]{1,0:T(8,128)S(1)} %collective-permute-done.refs_1_.beside, ...), custom_call_target="tpu_custom_call" | custom-call | tf_op jit(solution)/shard_map/pallas_call | solution.py:518
  (3 shorter events, 0.1 us)
Async XLA Ops:
  0.6 10.9 %copy-start = (bf16[8,320,320]{2,1,0:T(8,128)(2,1)S(1)}, bf16[8,320,320]{2,1,0:T(8,128)(2,1)}, u32[]{:S(2)}) copy-start(bf16[8,320,320]{2,1,0:T(8,128)(2,1)} %param.14) | copy-start | bytes 4915204
  2.1 3.8 %collective-permute-start = (f32[392,128]{1,0:T(8,128)S(1)}, f32[392,128]{1,0:T(8,128)S(1)}, u32[]{:S(2)}, u32[]{:S(2)}) collective-permute-start(f32[392,128]{1,0:T(8,128)S(1)} %get-tuple-element.14.refs_0_.state), channel_id=1, source_target_pairs={{0,8},{8,0},{16,24},{24,16},{1,9},{9,1},{17,25},{25,17},{2,10},{10... | collective-permute-start | bytes 602120 | tf_op jit(solution)/shard_map/ppermute | solution.py:286
  2.7 4.7 %collective-permute-start.1 = (f32[32,384]{1,0:T(8,128)S(1)}, f32[32,384]{1,0:T(8,128)S(1)}, u32[]{:S(2)}, u32[]{:S(2)}) collective-permute-start(f32[32,384]{1,0:T(8,128)S(1)} %get-tuple-element.15), channel_id=1, source_target_pairs={{0,9},{1,8},{2,11},{3,10},{4,13},{5,12},{6,15},{7,14},{8,1},{9,0},... | collective-permute-start | bytes 147464 | tf_op jit(solution)/shard_map/ppermute | solution.py:302
  6.0 7.9 %collective-permute-start.2 = (f32[320,128]{1,0:T(8,128)S(1)}, f32[320,128]{1,0:T(8,128)S(1)}, u32[]{:S(2)}, u32[]{:S(2)}) collective-permute-start(f32[320,128]{1,0:T(8,128)S(1)} %shard_map.132._), channel_id=1, source_target_pairs={{0,24},{8,16},{16,8},{24,0},{1,25},{9,17},{17,9},{25,1},{2,26},{10... | collective-permute-start | bytes 491528 | tf_op jit(solution)/shard_map/ppermute | solution.py:286
  7.3 6.3 %collective-permute-start.3 = (f32[16,384]{1,0:T(8,128)S(1)}, f32[16,384]{1,0:T(8,128)S(1)}, u32[]{:S(2)}, u32[]{:S(2)}) collective-permute-start(f32[16,384]{1,0:T(8,128)S(1)} %get-tuple-element.20), channel_id=1, source_target_pairs={{0,10},{1,11},{2,14},{3,15},{4,12},{5,13},{6,8},{7,9},{8,2},{9,3},... | collective-permute-start | bytes 73736 | tf_op jit(solution)/shard_map/ppermute | solution.py:302
  8.9 4.7 %collective-permute-start.4 = (f32[16,384]{1,0:T(8,128)S(1)}, f32[16,384]{1,0:T(8,128)S(1)}, u32[]{:S(2)}, u32[]{:S(2)}) collective-permute-start(f32[16,384]{1,0:T(8,128)S(1)} %get-tuple-element.21), channel_id=1, source_target_pairs={{0,12},{1,13},{2,10},{3,11},{4,8},{5,9},{6,14},{7,15},{8,4},{9,5},... | collective-permute-start | bytes 73736 | tf_op jit(solution)/shard_map/ppermute | solution.py:302
  10.0 3.9 %collective-permute-start.5 = (f32[16,384]{1,0:T(8,128)S(1)}, f32[16,384]{1,0:T(8,128)S(1)}, u32[]{:S(2)}, u32[]{:S(2)}) collective-permute-start(f32[16,384]{1,0:T(8,128)S(1)} %get-tuple-element.22), channel_id=1, source_target_pairs={{0,14},{1,15},{2,8},{3,9},{4,10},{5,11},{6,12},{7,13},{8,6},{9,7},... | collective-permute-start | bytes 73736 | tf_op jit(solution)/shard_map/ppermute | solution.py:302
  11.3 2.6 %collective-permute-start.6 = (f32[16,384]{1,0:T(8,128)S(1)}, f32[16,384]{1,0:T(8,128)S(1)}, u32[]{:S(2)}, u32[]{:S(2)}) collective-permute-start(f32[16,384]{1,0:T(8,128)S(1)} %get-tuple-element.23), channel_id=1, source_target_pairs={{0,8},{1,9},{2,12},{3,13},{4,14},{5,15},{6,10},{7,11},{8,0},{9,1},... | collective-permute-start | bytes 73736 | tf_op jit(solution)/shard_map/ppermute | solution.py:302

commit v7 on v6

--- a/solution.py
+++ b/solution.py
@@ -179,8 +179,11 @@
             state[rows, :] = blocks[share - trades : share, start : start + clusters]
 
 
-def half_kernel(state, _, half):
-    half[...] = state[pl.ds(0, half.shape[0]), :].astype(jnp.bfloat16)
+def share_kernel(weight, state, _, half, share, none):
+    value = state[pl.ds(0, half.shape[0]), :]
+    half[...] = value.astype(jnp.bfloat16)
+    share[...] = weight * value
+    none[...] = jnp.zeros_like(none)
 
 
 def landed(pieces, width, clusters):
@@ -196,57 +199,33 @@
     )[:width]
 
 
-def local_kernel(
-    table,
-    column_in,
-    kind_in,
-    source_in,
-    step_in,
-    count,
-    state,
-    products,
-    staying,
-    base,
-    rows,
-    column,
-    kind,
-    source,
-    sems,
-):
+def local_kernel(codes, own, products, staying, base):
     width, clusters = base.shape
     kinds = products.shape[0] // width
-    step = rows.at[pl.ds(0, 1), :]
-    copies = fetched(
-        [(column_in, column), (kind_in, kind), (source_in, source), (step_in, step)], sems
-    )
-    total = chosen(table, 0) * state[pl.ds(0, width), :] - landed([staying], width, clusters)
-    high, low = [], []
+    row = lax.broadcasted_iota(jnp.int32, (clusters, clusters), 0)
+    high, low, counts = [], [], []
     for which in range(kinds):
         full = products[pl.ds(which * width, width), :]
         upper = full.astype(jnp.bfloat16)
         high.append(upper)
         low.append((full - upper.astype(jnp.float32)).astype(jnp.bfloat16))
-    copies[0].wait()
-    copies[1].wait()
-    codes = column[...] + clusters * kind[...]
-    row = lax.broadcasted_iota(jnp.int32, (clusters, clusters), 0)
-    counts = []
-    for which in range(kinds):
-        count_of = jnp.zeros((clusters, clusters), jnp.float32)
+        count = jnp.zeros((clusters, clusters), jnp.float32)
         for entry in range(codes.shape[0]):
             hit = row == codes[entry : entry + 1, :] - which * clusters
-            count_of = count_of + jnp.where(hit, 1.0, 0.0)
-        counts.append(count_of.astype(jnp.bfloat16))
+            count = count + jnp.where(hit, 1.0, 0.0)
+        counts.append(count.astype(jnp.bfloat16))
     counts = jnp.concatenate(counts, axis=0)
+    total = own[...] - landed([staying], width, clusters)
     for part in (high, low):
         total = total + jnp.dot(
             jnp.concatenate(part, axis=1), counts, preferred_element_type=jnp.float32
         )
-    copies[2].wait()
-    copies[3].wait()
-    base[...] = total + source[...]
-    active = lax.broadcasted_iota(jnp.int32, (1, clusters), 1) < count[0]
-    rows[1:2, :] = jnp.where(active, 1.0, 0.0)
+    base[...] = total
+
+
+def early_kernel(before, *refs):
+    *pieces, base = refs
+    base[...] = before[...] - landed(pieces, *base.shape)
 
 
 def combine_kernel(table, held_by, mask, *refs):
@@ -476,11 +455,16 @@
         staying, *incoming = pieces
 
     kinds = jac_table.shape[0]
-    half = pl.pallas_call(
-        half_kernel,
-        out_shape=jax.ShapeDtypeStruct((width, clusters), jnp.bfloat16),
+    codes = pattern_col.T, pattern_type.T
+    half, own, none = pl.pallas_call(
+        functools.partial(share_kernel, table[0]),
+        out_shape=(
+            jax.ShapeDtypeStruct((width, clusters), jnp.bfloat16),
+            block,
+            jax.ShapeDtypeStruct(codes[0].shape, jnp.int32),
+        ),
         in_specs=[VMEM] * 2,
-        out_specs=VMEM,
+        out_specs=(VMEM,) * 3,
         compiler_params=ROOM,
     )(state_t, staying)
     products = lax.dot_general(
@@ -490,30 +474,29 @@
         preferred_element_type=jnp.float32,
     )
 
-    column, kind = pattern_col.T, pattern_type.T
-    base, rows = pl.pallas_call(
-        functools.partial(local_kernel, table),
-        out_shape=(block, jax.ShapeDtypeStruct((8, clusters), jnp.float32)),
-        in_specs=[HBM] * 4 + [SMEM] + [VMEM] * 3,
-        out_specs=(VMEM, VMEM),
-        scratch_shapes=[
-            pltpu.VMEM(column.shape, jnp.int32),
-            pltpu.VMEM(kind.shape, jnp.int32),
-            pltpu.VMEM((width, clusters), jnp.float32),
-            pltpu.SemaphoreType.DMA((4,)),
-        ],
+    codes = codes[0] + clusters * codes[1] + none
+    active = lax.broadcasted_iota(jnp.int32, (1, clusters), 1) + none[:1] < zone_count[0]
+    rows = jnp.concatenate([pseudo_step, active.astype(jnp.float32)], axis=0)
+    base = pl.pallas_call(
+        local_kernel,
+        out_shape=block,
+        in_specs=[VMEM] * 4,
+        out_specs=VMEM,
         compiler_params=ROOM,
         cost_estimate=FREE,
-    )(
-        in_hbm(column),
-        in_hbm(kind),
-        in_hbm(source_t),
-        in_hbm(pseudo_step),
-        zone_count,
-        state_t,
-        products,
-        staying,
-    )
+    )(codes, own, products, staying)
+    base = base + source_t
+    early = len(incoming) // 2
+    if early:
+        base = pl.pallas_call(
+            early_kernel,
+            out_shape=block,
+            in_specs=[VMEM] * (1 + early),
+            out_specs=VMEM,
+            compiler_params=ROOM,
+            cost_estimate=FREE,
+        )(base, *incoming[:early])
+        incoming = incoming[early:]
 
     updated, residual = pl.pallas_call(
         functools.partial(final_kernel, table, held_by, len(incoming)),

time: 15.1 us -> 15 us (level)
  Pallas kernels: 3.96 us -> 3.37 us
  waiting for transfers between devices: 0.32 us -> 0.73 us
    pallas_call x2 -> x3, Pallas kernels: 1.42 us -> 0.87 us  [the longest x1 0.62 us: on_device(): pl.pallas_call(local_kernel, out_shape=block, in_specs=[VMEM] * 4, out_sp...]
    ppermute x5, waiting for transfers between devices: 0.32 us -> 0.73 us  [stage_sent(): held.append(lax.ppermute(sends[which], ('inst', 'zone'), pairs))]
  transfers between devices with their start and end apart: 7 -> 7, of which waited for: 2 -> 3; matrix products, arithmetic and copies ran while one was open for 4% -> 5% of each run, Pallas kernels for 10% -> 6%
where the time goes in v7:
time: 15 us; the launch traced here: 14.9 us
  starting transfers between devices  8.6 us (57%)
  Pallas kernels  3.37 us (22%)
  between operations  1.44 us (10%)
  waiting for transfers between devices  0.73 us (5%)
  matrix products  0.67 us (4%)
    ppermute x5, starting transfers between devices, stage_sent(): held.append(lax.ppermute(sends[which], ('inst', 'zone'), pairs))  6.85 us
    ppermute x2, starting transfers between devices, moved(): lax.ppermute(value, axis, [(place, place ^ mask) for place in range(count)])  1.75 us
    pallas_call x1, Pallas kernels, on_device(): pl.pallas_call(functools.partial(outgoing_kernel, stages, slots_per, widt...  1.48 us
    pallas_call x1, Pallas kernels, on_device(): pl.pallas_call(functools.partial(final_kernel, table, held_by, len(incomi...  0.96 us
    ppermute x5, waiting for transfers between devices, stage_sent(): held.append(lax.ppermute(sends[which], ('inst', 'zone'), pairs))  0.73 us
    dot_general x1, matrix products, on_device(): lax.dot_general(jac_table.reshape(kinds * width, width), half, (((1,), (0...  0.67 us
    pallas_call x1, Pallas kernels, on_device(): pl.pallas_call(local_kernel, out_shape=block, in_specs=[VMEM] * 4, out_sp...  0.62 us
  transfers between devices with their start and end apart: 7, of which 3 were waited for; matrix products, arithmetic and copies ran while one was open for 5% of the time, Pallas kernels for 6%

profile of v7, /device:TPU:0, one launch (start us, length us, event | category | flops | bytes accessed | tf_op | source)
XLA Modules:
  0.0 14.9 jit_solution(9200306701575137188)
XLA Ops:
  0.6 0.0 copy-start
  0.6 1.5 %shard_map.131 = (f32[392,128]{1,0:T(8,128)S(1)}, f32[8,384]{1,0:T(8,128)S(1)}, f32[32,384]{1,0:T(8,128)S(1)}) custom-call(f32[320,128]{1,0:T(8,128)} %bitcast.24, s32[1,32]{1,0:T(1,128)} %source_in.1, s32[1,32]{1,0:T(1,128)} %bitcast.25, s32[1,32]{1,0:T(1,128)} %dest_in.1, s32[1,32]{1,0:T(1,128)} %weight_in.1, f32[16,320]{1,0:T(8,128)} %table_in.1), custom_call_target="tpu_custom_call" | custom-call | tf_op jit(solution)/shard_map/pallas_call | solution.py:409
  2.1 0.5 %collective-permute-start = (f32[392,128]{1,0:T(8,128)S(1)}, f32[392,128]{1,0:T(8,128)S(1)}, u32[]{:S(2)}, u32[]{:S(2)}) collective-permute-start(f32[392,128]{1,0:T(8,128)S(1)} %get-tuple-element.15.refs_0_.state), channel_id=1, source_target_pairs={{0,8},{8,0},{16,24},{24,16},{1,9},{9,1},{17,25},{25,17},{2,10},{10... | collective-permute-start | bytes 602120 | tf_op jit(solution)/shard_map/ppermute | solution.py:265
  2.7 2.6 %collective-permute-start.1 = (f32[32,384]{1,0:T(8,128)S(1)}, f32[32,384]{1,0:T(8,128)S(1)}, u32[]{:S(2)}, u32[]{:S(2)}) collective-permute-start(f32[32,384]{1,0:T(8,128)S(1)} %get-tuple-element.16), channel_id=1, source_target_pairs={{0,9},{1,8},{2,11},{3,10},{4,13},{5,12},{6,15},{7,14},{8,1},{9,0},... | collective-permute-start | bytes 147464 | tf_op jit(solution)/shard_map/ppermute | solution.py:281
  5.9 0.0 collective-permute-done.refs_1_.beside
  6.0 1.2 %collective-permute-start.4 = (f32[320,128]{1,0:T(8,128)S(1)}, f32[320,128]{1,0:T(8,128)S(1)}, u32[]{:S(2)}, u32[]{:S(2)}) collective-permute-start(f32[320,128]{1,0:T(8,128)S(1)} %shard_map.132._), channel_id=1, source_target_pairs={{0,24},{8,16},{16,8},{24,0},{1,25},{9,17},{17,9},{25,1},{2,26},{10... | collective-permute-start | bytes 491528 | tf_op jit(solution)/shard_map/ppermute | solution.py:265
  7.2 0.1 collective-permute-done.1.came
  7.3 1.6 %collective-permute-start.2 = (f32[16,384]{1,0:T(8,128)S(1)}, f32[16,384]{1,0:T(8,128)S(1)}, u32[]{:S(2)}, u32[]{:S(2)}) collective-permute-start(f32[16,384]{1,0:T(8,128)S(1)} %get-tuple-element.22), channel_id=1, source_target_pairs={{0,10},{1,11},{2,14},{3,15},{4,12},{5,13},{6,8},{7,9},{8,2},{9,3},... | collective-permute-start | bytes 73736 | tf_op jit(solution)/shard_map/ppermute | solution.py:281
  8.9 1.1 %collective-permute-start.3 = (f32[16,384]{1,0:T(8,128)S(1)}, f32[16,384]{1,0:T(8,128)S(1)}, u32[]{:S(2)}, u32[]{:S(2)}) collective-permute-start(f32[16,384]{1,0:T(8,128)S(1)} %get-tuple-element.23), channel_id=1, source_target_pairs={{0,12},{1,13},{2,10},{3,11},{4,8},{5,9},{6,14},{7,15},{8,4},{9,5},... | collective-permute-start | bytes 73736 | tf_op jit(solution)/shard_map/ppermute | solution.py:281
  10.0 1.3 %collective-permute-start.5 = (f32[16,384]{1,0:T(8,128)S(1)}, f32[16,384]{1,0:T(8,128)S(1)}, u32[]{:S(2)}, u32[]{:S(2)}) collective-permute-start(f32[16,384]{1,0:T(8,128)S(1)} %get-tuple-element.24), channel_id=1, source_target_pairs={{0,14},{1,15},{2,8},{3,9},{4,10},{5,11},{6,12},{7,13},{8,6},{9,7},... | collective-permute-start | bytes 73736 | tf_op jit(solution)/shard_map/ppermute | solution.py:281
  11.3 0.3 %collective-permute-start.6 = (f32[16,384]{1,0:T(8,128)S(1)}, f32[16,384]{1,0:T(8,128)S(1)}, u32[]{:S(2)}, u32[]{:S(2)}) collective-permute-start(f32[16,384]{1,0:T(8,128)S(1)} %get-tuple-element.25), channel_id=1, source_target_pairs={{0,8},{1,9},{2,12},{3,13},{4,14},{5,15},{6,10},{7,11},{8,0},{9,1},... | collective-permute-start | bytes 73736 | tf_op jit(solution)/shard_map/ppermute | solution.py:281
  11.6 0.0 copy-done
  11.6 0.0 copy-start.1
  11.6 0.0 copy-start.4
  11.6 0.7 %convolution_bitcast_fusion.products = f32[2560,128]{1,0:T(8,128)S(1)} fusion(bf16[2560,320]{1,0:T(8,128)(2,1)S(1)} %bitcast.23, bf16[320,128]{1,0:T(8,128)(2,1)S(1)} %get-tuple-element.21), kind=kOutput, calls=%fused_computation | convolution fusion | flops 209715200 | bytes 3031040 | tf_op jit(solution)/shard_map/dot_general | solution.py:470
  12.3 0.0 copy-done.2
  12.3 0.6 %shard_map.135 = f32[320,128]{1,0:T(8,128)S(1)} custom-call(s32[4,128]{1,0:T(4,128)S(1)} %bitcast_add_fusion.1.codes, f32[320,128]{1,0:T(8,128)S(1)} %get-tuple-element.20.own, f32[2560,128]{1,0:T(8,128)S(1)} %convolution_bitcast_fusion.products, f32[8,384]{1,0:T(8,128)S(1)} %get-tuple-element.18._.staying), custom_call_target="tpu_custom_call" | custom-call | flops 1 | bytes 1 | tf_op jit(solution)/shard_map/pallas_call | solution.py:480
  13.0 0.0 collective-permute-done.2.refs_0_
  13.0 0.4 %collective-permute-done.3.refs_1_ = f32[16,384]{1,0:T(8,128)S(1)} collective-permute-done((f32[16,384]{1,0:T(8,128)S(1)}, f32[16,384]{1,0:T(8,128)S(1)}, u32[]{:S(2)}, u32[]{:S(2)}) %collective-permute-start.3) | collective-permute-done | bytes 24608 | tf_op jit(solution)/shard_map/ppermute | solution.py:281
  13.5 0.2 %shard_map.136.base = f32[320,128]{1,0:T(8,128)S(1)} custom-call(f32[320,128]{1,0:T(8,128)S(1)} %bitcast_add_fusion.before, f32[16,384]{1,0:T(8,128)S(1)} %collective-permute-done.2.refs_0_, f32[16,384]{1,0:T(8,128)S(1)} %collective-permute-done.3.refs_1_), custom_call_target="tpu_custom_call" | custom-call | flops 1 | bytes 1 | tf_op jit(solution)/shard_map/pallas_call | solution.py:491
  13.7 0.2 %collective-permute-done.5.refs_3_ = f32[16,384]{1,0:T(8,128)S(1)} collective-permute-done((f32[16,384]{1,0:T(8,128)S(1)}, f32[16,384]{1,0:T(8,128)S(1)}, u32[]{:S(2)}, u32[]{:S(2)}) %collective-permute-start.5) | collective-permute-done | bytes 24608 | tf_op jit(solution)/shard_map/ppermute | solution.py:281
  13.9 0.0 collective-permute-done.6.refs_4_
  13.9 0.0 collective-permute-done.4.refs_2_
  13.9 1.0 %shard_map.137 = (f32[320,128]{1,0:T(8,128)}, f32[320,128]{1,0:T(8,128)}) custom-call(f32[320,128]{1,0:T(8,128)S(1)} %shard_map.136.base, f32[2,128]{1,0:T(2,128)S(1)} %pad_maximum_fusion.rows, f32[392,128]{1,0:T(8,128)S(1)} %get-tuple-element.15.refs_0_.state, f32[392,128]{1,0:T(8,128)S(1)} %collective-permute-done.refs_1_.beside, ...), custom_call_target="tpu_custom_call" | custom-call | tf_op jit(solution)/shard_map/pallas_call | solution.py:501
  (12 shorter events, 0.1 us)
Async XLA Ops:
  0.6 11.0 %copy-start = (bf16[8,320,320]{2,1,0:T(8,128)(2,1)S(1)}, bf16[8,320,320]{2,1,0:T(8,128)(2,1)}, u32[]{:S(2)}) copy-start(bf16[8,320,320]{2,1,0:T(8,128)(2,1)} %param.14) | copy-start | bytes 4915204
  2.1 3.8 %collective-permute-start = (f32[392,128]{1,0:T(8,128)S(1)}, f32[392,128]{1,0:T(8,128)S(1)}, u32[]{:S(2)}, u32[]{:S(2)}) collective-permute-start(f32[392,128]{1,0:T(8,128)S(1)} %get-tuple-element.15.refs_0_.state), channel_id=1, source_target_pairs={{0,8},{8,0},{16,24},{24,16},{1,9},{9,1},{17,25},{25,17},{2,10},{10... | collective-permute-start | bytes 602120 | tf_op jit(solution)/shard_map/ppermute | solution.py:265
  2.7 4.7 %collective-permute-start.1 = (f32[32,384]{1,0:T(8,128)S(1)}, f32[32,384]{1,0:T(8,128)S(1)}, u32[]{:S(2)}, u32[]{:S(2)}) collective-permute-start(f32[32,384]{1,0:T(8,128)S(1)} %get-tuple-element.16), channel_id=1, source_target_pairs={{0,9},{1,8},{2,11},{3,10},{4,13},{5,12},{6,15},{7,14},{8,1},{9,0},... | collective-permute-start | bytes 147464 | tf_op jit(solution)/shard_map/ppermute | solution.py:281
  6.0 7.9 %collective-permute-start.4 = (f32[320,128]{1,0:T(8,128)S(1)}, f32[320,128]{1,0:T(8,128)S(1)}, u32[]{:S(2)}, u32[]{:S(2)}) collective-permute-start(f32[320,128]{1,0:T(8,128)S(1)} %shard_map.132._), channel_id=1, source_target_pairs={{0,24},{8,16},{16,8},{24,0},{1,25},{9,17},{17,9},{25,1},{2,26},{10... | collective-permute-start | bytes 491528 | tf_op jit(solution)/shard_map/ppermute | solution.py:265
  7.3 5.0 %copy-start.2 = (s32[128,4]{0,1:T(4,128)S(1)}, s32[128,4]{0,1:T(4,128)}, u32[]{:S(2)}) copy-start(s32[128,4]{0,1:T(4,128)} %param.15) | copy-start | bytes 6148
  7.3 5.0 %copy-start.3 = (s32[128,4]{0,1:T(4,128)S(1)}, s32[128,4]{0,1:T(4,128)}, u32[]{:S(2)}) copy-start(s32[128,4]{0,1:T(4,128)} %param.16) | copy-start | bytes 6148
  7.3 5.7 %collective-permute-start.2 = (f32[16,384]{1,0:T(8,128)S(1)}, f32[16,384]{1,0:T(8,128)S(1)}, u32[]{:S(2)}, u32[]{:S(2)}) collective-permute-start(f32[16,384]{1,0:T(8,128)S(1)} %get-tuple-element.22), channel_id=1, source_target_pairs={{0,10},{1,11},{2,14},{3,15},{4,12},{5,13},{6,8},{7,9},{8,2},{9,3},... | collective-permute-start | bytes 73736 | tf_op jit(solution)/shard_map/ppermute | solution.py:281
  8.9 4.5 %collective-permute-start.3 = (f32[16,384]{1,0:T(8,128)S(1)}, f32[16,384]{1,0:T(8,128)S(1)}, u32[]{:S(2)}, u32[]{:S(2)}) collective-permute-start(f32[16,384]{1,0:T(8,128)S(1)} %get-tuple-element.23), channel_id=1, source_target_pairs={{0,12},{1,13},{2,10},{3,11},{4,8},{5,9},{6,14},{7,15},{8,4},{9,5},... | collective-permute-start | bytes 73736 | tf_op jit(solution)/shard_map/ppermute | solution.py:281
  10.0 3.9 %collective-permute-start.5 = (f32[16,384]{1,0:T(8,128)S(1)}, f32[16,384]{1,0:T(8,128)S(1)}, u32[]{:S(2)}, u32[]{:S(2)}) collective-permute-start(f32[16,384]{1,0:T(8,128)S(1)} %get-tuple-element.24), channel_id=1, source_target_pairs={{0,14},{1,15},{2,8},{3,9},{4,10},{5,11},{6,12},{7,13},{8,6},{9,7},... | collective-permute-start | bytes 73736 | tf_op jit(solution)/shard_map/ppermute | solution.py:281
  11.3 2.6 %collective-permute-start.6 = (f32[16,384]{1,0:T(8,128)S(1)}, f32[16,384]{1,0:T(8,128)S(1)}, u32[]{:S(2)}, u32[]{:S(2)}) collective-permute-start(f32[16,384]{1,0:T(8,128)S(1)} %get-tuple-element.25), channel_id=1, source_target_pairs={{0,8},{1,9},{2,12},{3,13},{4,14},{5,15},{6,10},{7,11},{8,0},{9,1},... | collective-permute-start | bytes 73736 | tf_op jit(solution)/shard_map/ppermute | solution.py:281
  11.6 1.4 %copy-start.1 = (f32[1,128,320]{1,2,0:T(8,128)S(1)}, f32[1,128,320]{1,2,0:T(8,128)}, u32[]{:S(2)}) copy-start(f32[1,128,320]{1,2,0:T(8,128)} %param.13) | copy-start | bytes 491524
  11.6 1.4 %copy-start.4 = (f32[1,128]{1,0:T(1,128)S(1)}, f32[1,128]{1,0:T(1,128)}, u32[]{:S(2)}) copy-start(f32[1,128]{1,0:T(1,128)} %param.17) | copy-start | bytes 1540

commit v8 on v7

--- a/solution.py
+++ b/solution.py
@@ -187,7 +187,11 @@
 
 
 def landed(pieces, width, clusters):
-    arrived = jnp.concatenate([piece[...] for piece in pieces], axis=0)
+    arrived = [piece[...] for piece in pieces]
+    short = -sum(piece.shape[0] for piece in arrived) % 16
+    if short:
+        arrived.append(jnp.zeros((short, arrived[0].shape[1]), jnp.float32))
+    arrived = jnp.concatenate(arrived, axis=0)
     target = arrived[:, width : width + 1].astype(jnp.int32)
     landing = lax.broadcasted_iota(jnp.int32, (arrived.shape[0], clusters), 1) == target
     landing = jnp.where(landing, 1.0, 0.0).astype(jnp.bfloat16)
@@ -223,9 +227,22 @@
     base[...] = total
 
 
-def early_kernel(before, *refs):
-    *pieces, base = refs
-    base[...] = before[...] - landed(pieces, *base.shape)
+def early_kernel(table, held_by, pieces, before, *refs):
+    period = len(table)
+    held = refs[: len(held_by)]
+    others = refs[len(held_by) : len(refs) - pieces - 1]
+    base = refs[-1]
+    width, clusters = base.shape
+    me = lax.axis_index("inst")
+    total = before[...]
+    for mask, ref in zip(held_by, held, strict=True):
+        shift = (me - (me ^ mask) + period) & (period - 1)
+        total = total + chosen(table, shift) * ref[pl.ds(0, width), :]
+    for ref in others:
+        total = total + ref[...]
+    if pieces:
+        total = total - landed(refs[len(refs) - pieces - 1 : -1], width, clusters)
+    base[...] = total
 
 
 def combine_kernel(table, held_by, mask, *refs):
@@ -240,24 +257,13 @@
     out[...] = total
 
 
-def final_kernel(table, held_by, pieces, base, rows, *refs):
-    period = len(table)
-    held = refs[: len(held_by)]
-    others = refs[len(held_by) : len(refs) - pieces - 2]
-    incoming = refs[len(refs) - pieces - 2 : len(refs) - 2]
-    updated, residual = refs[-2:]
+def final_kernel(base, rows, state, *refs):
+    *incoming, updated, residual = refs
     width, clusters = base.shape
-    me = lax.axis_index("inst")
-    total = base[...]
-    for mask, ref in zip(held_by[1:], held[1:], strict=True):
-        shift = (me - (me ^ mask) + period) & (period - 1)
-        total = total + chosen(table, shift) * ref[pl.ds(0, width), :]
-    for ref in others:
-        total = total + ref[...]
-    total = total - landed(incoming, width, clusters)
+    total = base[...] - landed(incoming, width, clusters)
     kept = jnp.where(rows[1:2, :] > 0.0, total, 0.0)
     residual[...] = kept
-    updated[...] = held[0][pl.ds(0, width), :] - rows[0:1, :] * kept
+    updated[...] = state[pl.ds(0, width), :] - rows[0:1, :] * kept
 
 
 def moved(value, axis, mask):
@@ -487,24 +493,23 @@
     )(codes, own, products, staying)
     base = base + source_t
     early = len(incoming) // 2
-    if early:
-        base = pl.pallas_call(
-            early_kernel,
-            out_shape=block,
-            in_specs=[VMEM] * (1 + early),
-            out_specs=VMEM,
-            compiler_params=ROOM,
-            cost_estimate=FREE,
-        )(base, *incoming[:early])
-        incoming = incoming[early:]
-
+    sooner = [*held[1:], *others, *incoming[:early]]
+    base = pl.pallas_call(
+        functools.partial(early_kernel, table, held_by[1:], early),
+        out_shape=block,
+        in_specs=[VMEM] * (1 + len(sooner)),
+        out_specs=VMEM,
+        compiler_params=ROOM,
+        cost_estimate=FREE,
+    )(base, *sooner)
+    incoming = incoming[early:]
     updated, residual = pl.pallas_call(
-        functools.partial(final_kernel, table, held_by, len(incoming)),
+        final_kernel,
         out_shape=(block, block),
-        in_specs=[VMEM] * (2 + len(held) + len(others) + len(incoming)),
+        in_specs=[VMEM] * (3 + len(incoming)),
         out_specs=(VMEM, VMEM),
         compiler_params=ROOM,
-    )(base, rows, *held, *others, *incoming)
+    )(base, rows, state_t, *incoming)
     return updated.T[None], residual.T[None]
 
 

time: 15 us -> 15 us (level)
  no operation moved by 1% of the time
where the time goes in v8:
time: 15 us; the launch traced here: 14.9 us
  starting transfers between devices  8.6 us (57%)
  Pallas kernels  3.37 us (22%)
  between operations  1.44 us (10%)
  waiting for transfers between devices  0.72 us (5%)
  matrix products  0.67 us (4%)
    ppermute x5, starting transfers between devices, stage_sent(): held.append(lax.ppermute(sends[which], ('inst', 'zone'), pairs))  6.85 us
    ppermute x2, starting transfers between devices, moved(): lax.ppermute(value, axis, [(place, place ^ mask) for place in range(count)])  1.75 us
    pallas_call x1, Pallas kernels, on_device(): pl.pallas_call(functools.partial(outgoing_kernel, stages, slots_per, widt...  1.48 us
    pallas_call x1, Pallas kernels, on_device(): pl.pallas_call(final_kernel, out_shape=(block, block), in_specs=[VMEM] *...  0.96 us
    ppermute x5, waiting for transfers between devices, stage_sent(): held.append(lax.ppermute(sends[which], ('inst', 'zone'), pairs))  0.72 us
    dot_general x1, matrix products, on_device(): lax.dot_general(jac_table.reshape(kinds * width, width), half, (((1,), (0...  0.67 us
    pallas_call x1, Pallas kernels, on_device(): pl.pallas_call(local_kernel, out_shape=block, in_specs=[VMEM] * 4, out_sp...  0.62 us
  transfers between devices with their start and end apart: 7, of which 3 were waited for; matrix products, arithmetic and copies ran while one was open for 5% of the time, Pallas kernels for 6%

profile of v8, /device:TPU:0, one launch (start us, length us, event | category | flops | bytes accessed | tf_op | source)
XLA Modules:
  0.0 14.9 jit_solution(17361134200469827446)
XLA Ops:
  0.6 0.0 copy-start
  0.6 1.5 %shard_map.131 = (f32[392,128]{1,0:T(8,128)S(1)}, f32[8,384]{1,0:T(8,128)S(1)}, f32[32,384]{1,0:T(8,128)S(1)}) custom-call(f32[320,128]{1,0:T(8,128)} %bitcast.24, s32[1,32]{1,0:T(1,128)} %source_in.1, s32[1,32]{1,0:T(1,128)} %bitcast.25, s32[1,32]{1,0:T(1,128)} %dest_in.1, s32[1,32]{1,0:T(1,128)} %weight_in.1, f32[16,320]{1,0:T(8,128)} %table_in.1), custom_call_target="tpu_custom_call" | custom-call | tf_op jit(solution)/shard_map/pallas_call | solution.py:415
  2.1 0.5 %collective-permute-start = (f32[392,128]{1,0:T(8,128)S(1)}, f32[392,128]{1,0:T(8,128)S(1)}, u32[]{:S(2)}, u32[]{:S(2)}) collective-permute-start(f32[392,128]{1,0:T(8,128)S(1)} %get-tuple-element.15.refs_0_.state), channel_id=1, source_target_pairs={{0,8},{8,0},{16,24},{24,16},{1,9},{9,1},{17,25},{25,17},{2,10},{10... | collective-permute-start | bytes 602120 | tf_op jit(solution)/shard_map/ppermute | solution.py:271
  2.7 2.6 %collective-permute-start.1 = (f32[32,384]{1,0:T(8,128)S(1)}, f32[32,384]{1,0:T(8,128)S(1)}, u32[]{:S(2)}, u32[]{:S(2)}) collective-permute-start(f32[32,384]{1,0:T(8,128)S(1)} %get-tuple-element.16), channel_id=1, source_target_pairs={{0,9},{1,8},{2,11},{3,10},{4,13},{5,12},{6,15},{7,14},{8,1},{9,0},... | collective-permute-start | bytes 147464 | tf_op jit(solution)/shard_map/ppermute | solution.py:287
  5.9 0.0 collective-permute-done.refs_1_.beside.refs_0_
  6.0 1.2 %collective-permute-start.2 = (f32[320,128]{1,0:T(8,128)S(1)}, f32[320,128]{1,0:T(8,128)S(1)}, u32[]{:S(2)}, u32[]{:S(2)}) collective-permute-start(f32[320,128]{1,0:T(8,128)S(1)} %shard_map.132._), channel_id=1, source_target_pairs={{0,24},{8,16},{16,8},{24,0},{1,25},{9,17},{17,9},{25,1},{2,26},{10... | collective-permute-start | bytes 491528 | tf_op jit(solution)/shard_map/ppermute | solution.py:271
  7.2 0.1 collective-permute-done.1.came
  7.3 1.6 %collective-permute-start.3 = (f32[16,384]{1,0:T(8,128)S(1)}, f32[16,384]{1,0:T(8,128)S(1)}, u32[]{:S(2)}, u32[]{:S(2)}) collective-permute-start(f32[16,384]{1,0:T(8,128)S(1)} %get-tuple-element.22), channel_id=1, source_target_pairs={{0,10},{1,11},{2,14},{3,15},{4,12},{5,13},{6,8},{7,9},{8,2},{9,3},... | collective-permute-start | bytes 73736 | tf_op jit(solution)/shard_map/ppermute | solution.py:287
  8.9 1.1 %collective-permute-start.4 = (f32[16,384]{1,0:T(8,128)S(1)}, f32[16,384]{1,0:T(8,128)S(1)}, u32[]{:S(2)}, u32[]{:S(2)}) collective-permute-start(f32[16,384]{1,0:T(8,128)S(1)} %get-tuple-element.23), channel_id=1, source_target_pairs={{0,12},{1,13},{2,10},{3,11},{4,8},{5,9},{6,14},{7,15},{8,4},{9,5},... | collective-permute-start | bytes 73736 | tf_op jit(solution)/shard_map/ppermute | solution.py:287
  10.0 1.3 %collective-permute-start.5 = (f32[16,384]{1,0:T(8,128)S(1)}, f32[16,384]{1,0:T(8,128)S(1)}, u32[]{:S(2)}, u32[]{:S(2)}) collective-permute-start(f32[16,384]{1,0:T(8,128)S(1)} %get-tuple-element.24), channel_id=1, source_target_pairs={{0,14},{1,15},{2,8},{3,9},{4,10},{5,11},{6,12},{7,13},{8,6},{9,7},... | collective-permute-start | bytes 73736 | tf_op jit(solution)/shard_map/ppermute | solution.py:287
  11.3 0.3 %collective-permute-start.6 = (f32[16,384]{1,0:T(8,128)S(1)}, f32[16,384]{1,0:T(8,128)S(1)}, u32[]{:S(2)}, u32[]{:S(2)}) collective-permute-start(f32[16,384]{1,0:T(8,128)S(1)} %get-tuple-element.25), channel_id=1, source_target_pairs={{0,8},{1,9},{2,12},{3,13},{4,14},{5,15},{6,10},{7,11},{8,0},{9,1},... | collective-permute-start | bytes 73736 | tf_op jit(solution)/shard_map/ppermute | solution.py:287
  11.6 0.0 copy-done
  11.6 0.0 copy-start.1
  11.6 0.0 copy-start.4
  11.6 0.7 %convolution_bitcast_fusion.products = f32[2560,128]{1,0:T(8,128)S(1)} fusion(bf16[2560,320]{1,0:T(8,128)(2,1)S(1)} %bitcast.23, bf16[320,128]{1,0:T(8,128)(2,1)S(1)} %get-tuple-element.21), kind=kOutput, calls=%fused_computation | convolution fusion | flops 209715200 | bytes 3031040 | tf_op jit(solution)/shard_map/dot_general | solution.py:476
  12.3 0.0 copy-done.2
  12.3 0.6 %shard_map.135 = f32[320,128]{1,0:T(8,128)S(1)} custom-call(s32[4,128]{1,0:T(4,128)S(1)} %bitcast_add_fusion.1.codes, f32[320,128]{1,0:T(8,128)S(1)} %get-tuple-element.20.own, f32[2560,128]{1,0:T(8,128)S(1)} %convolution_bitcast_fusion.products, f32[8,384]{1,0:T(8,128)S(1)} %get-tuple-element.18._.staying), custom_call_target="tpu_custom_call" | custom-call | flops 1 | bytes 1 | tf_op jit(solution)/shard_map/pallas_call | solution.py:486
  13.0 0.0 collective-permute-done.3.refs_2_
  13.0 0.4 %collective-permute-done.4.refs_3_ = f32[16,384]{1,0:T(8,128)S(1)} collective-permute-done((f32[16,384]{1,0:T(8,128)S(1)}, f32[16,384]{1,0:T(8,128)S(1)}, u32[]{:S(2)}, u32[]{:S(2)}) %collective-permute-start.4) | collective-permute-done | bytes 24608 | tf_op jit(solution)/shard_map/ppermute | solution.py:287
  13.5 0.0 collective-permute-done.2.refs_1_
  13.5 0.2 %shard_map.136.base = f32[320,128]{1,0:T(8,128)S(1)} custom-call(f32[320,128]{1,0:T(8,128)S(1)} %bitcast_add_fusion.before, f32[392,128]{1,0:T(8,128)S(1)} %collective-permute-done.refs_1_.beside.refs_0_, f32[320,128]{1,0:T(8,128)S(1)} %collective-permute-done.2.refs_1_, f32[16,384]{1,0:T(8,128)S(1)} %collective-permute-done.3.refs_2_, ...), custom_call_target="tpu_custom_call" | custom-call | flops 1 | bytes 1 | tf_op jit(solution)/shard_map/pallas_call | solution.py:497
  13.7 0.2 %collective-permute-done.5.refs_0_ = f32[16,384]{1,0:T(8,128)S(1)} collective-permute-done((f32[16,384]{1,0:T(8,128)S(1)}, f32[16,384]{1,0:T(8,128)S(1)}, u32[]{:S(2)}, u32[]{:S(2)}) %collective-permute-start.5) | collective-permute-done | bytes 24608 | tf_op jit(solution)/shard_map/ppermute | solution.py:287
  13.9 0.0 collective-permute-done.6.refs_1_
  13.9 1.0 %shard_map.137 = (f32[320,128]{1,0:T(8,128)}, f32[320,128]{1,0:T(8,128)}) custom-call(f32[320,128]{1,0:T(8,128)S(1)} %shard_map.136.base, f32[2,128]{1,0:T(2,128)S(1)} %pad_maximum_fusion.rows, f32[392,128]{1,0:T(8,128)S(1)} %get-tuple-element.15.refs_0_.state, f32[16,384]{1,0:T(8,128)S(1)} %collective-permute-done.5.refs_0_, ...), custom_call_target="tpu_custom_call" | custom-call | tf_op jit(solution)/shard_map/pallas_call | solution.py:506
  (12 shorter events, 0.1 us)
Async XLA Ops:
  0.6 11.0 %copy-start = (bf16[8,320,320]{2,1,0:T(8,128)(2,1)S(1)}, bf16[8,320,320]{2,1,0:T(8,128)(2,1)}, u32[]{:S(2)}) copy-start(bf16[8,320,320]{2,1,0:T(8,128)(2,1)} %param.14) | copy-start | bytes 4915204
  2.1 3.8 %collective-permute-start = (f32[392,128]{1,0:T(8,128)S(1)}, f32[392,128]{1,0:T(8,128)S(1)}, u32[]{:S(2)}, u32[]{:S(2)}) collective-permute-start(f32[392,128]{1,0:T(8,128)S(1)} %get-tuple-element.15.refs_0_.state), channel_id=1, source_target_pairs={{0,8},{8,0},{16,24},{24,16},{1,9},{9,1},{17,25},{25,17},{2,10},{10... | collective-permute-start | bytes 602120 | tf_op jit(solution)/shard_map/ppermute | solution.py:271
  2.7 4.7 %collective-permute-start.1 = (f32[32,384]{1,0:T(8,128)S(1)}, f32[32,384]{1,0:T(8,128)S(1)}, u32[]{:S(2)}, u32[]{:S(2)}) collective-permute-start(f32[32,384]{1,0:T(8,128)S(1)} %get-tuple-element.16), channel_id=1, source_target_pairs={{0,9},{1,8},{2,11},{3,10},{4,13},{5,12},{6,15},{7,14},{8,1},{9,0},... | collective-permute-start | bytes 147464 | tf_op jit(solution)/shard_map/ppermute | solution.py:287
  6.0 7.5 %collective-permute-start.2 = (f32[320,128]{1,0:T(8,128)S(1)}, f32[320,128]{1,0:T(8,128)S(1)}, u32[]{:S(2)}, u32[]{:S(2)}) collective-permute-start(f32[320,128]{1,0:T(8,128)S(1)} %shard_map.132._), channel_id=1, source_target_pairs={{0,24},{8,16},{16,8},{24,0},{1,25},{9,17},{17,9},{25,1},{2,26},{10... | collective-permute-start | bytes 491528 | tf_op jit(solution)/shard_map/ppermute | solution.py:271
  7.3 5.0 %copy-start.2 = (s32[128,4]{0,1:T(4,128)S(1)}, s32[128,4]{0,1:T(4,128)}, u32[]{:S(2)}) copy-start(s32[128,4]{0,1:T(4,128)} %param.15) | copy-start | bytes 6148
  7.3 5.0 %copy-start.3 = (s32[128,4]{0,1:T(4,128)S(1)}, s32[128,4]{0,1:T(4,128)}, u32[]{:S(2)}) copy-start(s32[128,4]{0,1:T(4,128)} %param.16) | copy-start | bytes 6148
  7.3 5.7 %collective-permute-start.3 = (f32[16,384]{1,0:T(8,128)S(1)}, f32[16,384]{1,0:T(8,128)S(1)}, u32[]{:S(2)}, u32[]{:S(2)}) collective-permute-start(f32[16,384]{1,0:T(8,128)S(1)} %get-tuple-element.22), channel_id=1, source_target_pairs={{0,10},{1,11},{2,14},{3,15},{4,12},{5,13},{6,8},{7,9},{8,2},{9,3},... | collective-permute-start | bytes 73736 | tf_op jit(solution)/shard_map/ppermute | solution.py:287
  8.9 4.5 %collective-permute-start.4 = (f32[16,384]{1,0:T(8,128)S(1)}, f32[16,384]{1,0:T(8,128)S(1)}, u32[]{:S(2)}, u32[]{:S(2)}) collective-permute-start(f32[16,384]{1,0:T(8,128)S(1)} %get-tuple-element.23), channel_id=1, source_target_pairs={{0,12},{1,13},{2,10},{3,11},{4,8},{5,9},{6,14},{7,15},{8,4},{9,5},... | collective-permute-start | bytes 73736 | tf_op jit(solution)/shard_map/ppermute | solution.py:287
  10.0 3.9 %collective-permute-start.5 = (f32[16,384]{1,0:T(8,128)S(1)}, f32[16,384]{1,0:T(8,128)S(1)}, u32[]{:S(2)}, u32[]{:S(2)}) collective-permute-start(f32[16,384]{1,0:T(8,128)S(1)} %get-tuple-element.24), channel_id=1, source_target_pairs={{0,14},{1,15},{2,8},{3,9},{4,10},{5,11},{6,12},{7,13},{8,6},{9,7},... | collective-permute-start | bytes 73736 | tf_op jit(solution)/shard_map/ppermute | solution.py:287
  11.3 2.6 %collective-permute-start.6 = (f32[16,384]{1,0:T(8,128)S(1)}, f32[16,384]{1,0:T(8,128)S(1)}, u32[]{:S(2)}, u32[]{:S(2)}) collective-permute-start(f32[16,384]{1,0:T(8,128)S(1)} %get-tuple-element.25), channel_id=1, source_target_pairs={{0,8},{1,9},{2,12},{3,13},{4,14},{5,15},{6,10},{7,11},{8,0},{9,1},... | collective-permute-start | bytes 73736 | tf_op jit(solution)/shard_map/ppermute | solution.py:287
  11.6 1.4 %copy-start.1 = (f32[1,128,320]{1,2,0:T(8,128)S(1)}, f32[1,128,320]{1,2,0:T(8,128)}, u32[]{:S(2)}) copy-start(f32[1,128,320]{1,2,0:T(8,128)} %param.13) | copy-start | bytes 491524
  11.6 1.4 %copy-start.4 = (f32[1,128]{1,0:T(1,128)S(1)}, f32[1,128]{1,0:T(1,128)}, u32[]{:S(2)}) copy-start(f32[1,128]{1,0:T(1,128)} %param.17) | copy-start | bytes 1540

commit v9 on v8

--- a/solution.py
+++ b/solution.py
@@ -120,15 +120,12 @@
     *refs,
 ):
     *sends, source, owner, dest, weight, table, sems = refs
+    cuts = sems.shape[0] - 5
+    spans = [pl.ds(cut * (width // cuts), width // cuts) for cut in range(cuts)]
     copies = fetched(
-        (
-            (owner_in, owner),
-            (source_in, source),
-            (weight_in, weight),
-            (dest_in, dest),
-            (state_in, state.at[pl.ds(0, width), :]),
-            (table_in, table),
-        ),
+        [(owner_in, owner), (source_in, source), (weight_in, weight), (dest_in, dest)]
+        + [(state_in.at[span, :], state.at[span, :]) for span in spans]
+        + [(table_in, table)],
         sems,
     )
     clusters = state.shape[1]
@@ -156,11 +153,11 @@
     pick = jnp.where(pick, 1.0, 0.0).astype(jnp.bfloat16)
     choose = lax.broadcasted_iota(jnp.int32, (slots, sets), 1) == by_set.astype(jnp.int32)
     choose = jnp.where(choose, 1.0, 0.0).astype(jnp.bfloat16)
-    copies[5].wait()
+    for copy in copies[4:]:
+        copy.wait()
     scales = jnp.zeros((slots, width), jnp.float32)
     for part in parts_of(table[...]):
         scales = scales + jnp.dot(choose, part, preferred_element_type=jnp.float32)
-    copies[4].wait()
     parts = jnp.concatenate(parts_of(state[pl.ds(0, width), :]), axis=1)
     picked = lax.dot_general(
         jnp.concatenate([pick, pick, pick], axis=1),
@@ -408,6 +405,7 @@
     crossed = crossed and instances >= 4 and clusters == LANES
     share = jax.ShapeDtypeStruct((units[1], padded), jnp.float32)
     shares, bundle = [share] * first, block
+    cuts = 5 if width % 40 == 0 else 1
     if crossed:
         trades = (units[1] - units[2]) * padded // clusters
         bundle = jax.ShapeDtypeStruct((width + trades, clusters), jnp.float32)
@@ -418,7 +416,7 @@
         in_specs=[HBM] * 6,
         out_specs=(VMEM,) * (1 + first),
         scratch_shapes=[pltpu.VMEM((1, links), jnp.int32)] * 4
-        + [pltpu.VMEM(iface_table.shape, jnp.float32), pltpu.SemaphoreType.DMA((6,))],
+        + [pltpu.VMEM(iface_table.shape, jnp.float32), pltpu.SemaphoreType.DMA((5 + cuts,))],
         compiler_params=ROOM,
     )(
         in_hbm(state_in),

time: 15 us -> 14.9 us (level)
  no operation moved by 1% of the time
where the time goes in v9:
time: 14.9 us; the launch traced here: 14.8 us
  starting transfers between devices  8.61 us (58%)
  Pallas kernels  3.28 us (22%)
  between operations  1.44 us (10%)
  waiting for transfers between devices  0.7 us (5%)
  matrix products  0.68 us (5%)
    ppermute x5, starting transfers between devices, stage_sent(): held.append(lax.ppermute(sends[which], ('inst', 'zone'), pairs))  6.86 us
    ppermute x2, starting transfers between devices, moved(): lax.ppermute(value, axis, [(place, place ^ mask) for place in range(count)])  1.75 us
    pallas_call x1, Pallas kernels, on_device(): pl.pallas_call(functools.partial(outgoing_kernel, stages, slots_per, widt...  1.38 us
    pallas_call x1, Pallas kernels, on_device(): pl.pallas_call(final_kernel, out_shape=(block, block), in_specs=[VMEM] *...  0.96 us
    ppermute x5, waiting for transfers between devices, stage_sent(): held.append(lax.ppermute(sends[which], ('inst', 'zone'), pairs))  0.69 us
    dot_general x1, matrix products, on_device(): lax.dot_general(jac_table.reshape(kinds * width, width), half, (((1,), (0...  0.68 us
    pallas_call x1, Pallas kernels, on_device(): pl.pallas_call(local_kernel, out_shape=block, in_specs=[VMEM] * 4, out_sp...  0.62 us
  transfers between devices with their start and end apart: 7, of which 3 were waited for; matrix products, arithmetic and copies ran while one was open for 5% of the time, Pallas kernels for 6%

profile of v9, /device:TPU:0, one launch (start us, length us, event | category | flops | bytes accessed | tf_op | source)
XLA Modules:
  0.0 14.8 jit_solution(5344647203446968903)
XLA Ops:
  0.6 0.0 copy-start
  0.6 1.4 %shard_map.131 = (f32[392,128]{1,0:T(8,128)S(1)}, f32[8,384]{1,0:T(8,128)S(1)}, f32[32,384]{1,0:T(8,128)S(1)}) custom-call(f32[320,128]{1,0:T(8,128)} %bitcast.24, s32[1,32]{1,0:T(1,128)} %source_in.1, s32[1,32]{1,0:T(1,128)} %bitcast.25, s32[1,32]{1,0:T(1,128)} %dest_in.1, s32[1,32]{1,0:T(1,128)} %weight_in.1, f32[16,320]{1,0:T(8,128)} %table_in.1), custom_call_target="tpu_custom_call" | custom-call | tf_op jit(solution)/shard_map/pallas_call | solution.py:413
  2.0 0.5 %collective-permute-start = (f32[392,128]{1,0:T(8,128)S(1)}, f32[392,128]{1,0:T(8,128)S(1)}, u32[]{:S(2)}, u32[]{:S(2)}) collective-permute-start(f32[392,128]{1,0:T(8,128)S(1)} %get-tuple-element.15.refs_0_.state), channel_id=1, source_target_pairs={{0,8},{8,0},{16,24},{24,16},{1,9},{9,1},{17,25},{25,17},{2,10},{10... | collective-permute-start | bytes 602120 | tf_op jit(solution)/shard_map/ppermute | solution.py:268
  2.6 2.6 %collective-permute-start.1 = (f32[32,384]{1,0:T(8,128)S(1)}, f32[32,384]{1,0:T(8,128)S(1)}, u32[]{:S(2)}, u32[]{:S(2)}) collective-permute-start(f32[32,384]{1,0:T(8,128)S(1)} %get-tuple-element.16), channel_id=1, source_target_pairs={{0,9},{1,8},{2,11},{3,10},{4,13},{5,12},{6,15},{7,14},{8,1},{9,0},... | collective-permute-start | bytes 147464 | tf_op jit(solution)/shard_map/ppermute | solution.py:284
  5.9 0.0 collective-permute-done.refs_1_.beside.refs_0_
  5.9 1.2 %collective-permute-start.2 = (f32[320,128]{1,0:T(8,128)S(1)}, f32[320,128]{1,0:T(8,128)S(1)}, u32[]{:S(2)}, u32[]{:S(2)}) collective-permute-start(f32[320,128]{1,0:T(8,128)S(1)} %shard_map.132._), channel_id=1, source_target_pairs={{0,24},{8,16},{16,8},{24,0},{1,25},{9,17},{17,9},{25,1},{2,26},{10... | collective-permute-start | bytes 491528 | tf_op jit(solution)/shard_map/ppermute | solution.py:268
  7.1 0.1 collective-permute-done.1.came
  7.2 1.6 %collective-permute-start.3 = (f32[16,384]{1,0:T(8,128)S(1)}, f32[16,384]{1,0:T(8,128)S(1)}, u32[]{:S(2)}, u32[]{:S(2)}) collective-permute-start(f32[16,384]{1,0:T(8,128)S(1)} %get-tuple-element.22), channel_id=1, source_target_pairs={{0,10},{1,11},{2,14},{3,15},{4,12},{5,13},{6,8},{7,9},{8,2},{9,3},... | collective-permute-start | bytes 73736 | tf_op jit(solution)/shard_map/ppermute | solution.py:284
  8.9 1.1 %collective-permute-start.4 = (f32[16,384]{1,0:T(8,128)S(1)}, f32[16,384]{1,0:T(8,128)S(1)}, u32[]{:S(2)}, u32[]{:S(2)}) collective-permute-start(f32[16,384]{1,0:T(8,128)S(1)} %get-tuple-element.23), channel_id=1, source_target_pairs={{0,12},{1,13},{2,10},{3,11},{4,8},{5,9},{6,14},{7,15},{8,4},{9,5},... | collective-permute-start | bytes 73736 | tf_op jit(solution)/shard_map/ppermute | solution.py:284
  9.9 1.3 %collective-permute-start.5 = (f32[16,384]{1,0:T(8,128)S(1)}, f32[16,384]{1,0:T(8,128)S(1)}, u32[]{:S(2)}, u32[]{:S(2)}) collective-permute-start(f32[16,384]{1,0:T(8,128)S(1)} %get-tuple-element.24), channel_id=1, source_target_pairs={{0,14},{1,15},{2,8},{3,9},{4,10},{5,11},{6,12},{7,13},{8,6},{9,7},... | collective-permute-start | bytes 73736 | tf_op jit(solution)/shard_map/ppermute | solution.py:284
  11.2 0.3 %collective-permute-start.6 = (f32[16,384]{1,0:T(8,128)S(1)}, f32[16,384]{1,0:T(8,128)S(1)}, u32[]{:S(2)}, u32[]{:S(2)}) collective-permute-start(f32[16,384]{1,0:T(8,128)S(1)} %get-tuple-element.25), channel_id=1, source_target_pairs={{0,8},{1,9},{2,12},{3,13},{4,14},{5,15},{6,10},{7,11},{8,0},{9,1},... | collective-permute-start | bytes 73736 | tf_op jit(solution)/shard_map/ppermute | solution.py:284
  11.5 0.0 copy-done
  11.5 0.0 copy-start.1
  11.5 0.0 copy-start.4
  11.5 0.7 %convolution_bitcast_fusion.products = f32[2560,128]{1,0:T(8,128)S(1)} fusion(bf16[2560,320]{1,0:T(8,128)(2,1)S(1)} %bitcast.23, bf16[320,128]{1,0:T(8,128)(2,1)S(1)} %get-tuple-element.21), kind=kOutput, calls=%fused_computation | convolution fusion | flops 209715200 | bytes 3031040 | tf_op jit(solution)/shard_map/dot_general | solution.py:474
  12.2 0.6 %shard_map.135 = f32[320,128]{1,0:T(8,128)S(1)} custom-call(s32[4,128]{1,0:T(4,128)S(1)} %bitcast_add_fusion.1.codes, f32[320,128]{1,0:T(8,128)S(1)} %get-tuple-element.20.own, f32[2560,128]{1,0:T(8,128)S(1)} %convolution_bitcast_fusion.products, f32[8,384]{1,0:T(8,128)S(1)} %get-tuple-element.18._.staying), custom_call_target="tpu_custom_call" | custom-call | flops 1 | bytes 1 | tf_op jit(solution)/shard_map/pallas_call | solution.py:484
  12.9 0.0 copy-done.4
  12.9 0.0 collective-permute-done.3.refs_2_
  13.0 0.4 %collective-permute-done.4.refs_3_ = f32[16,384]{1,0:T(8,128)S(1)} collective-permute-done((f32[16,384]{1,0:T(8,128)S(1)}, f32[16,384]{1,0:T(8,128)S(1)}, u32[]{:S(2)}, u32[]{:S(2)}) %collective-permute-start.4) | collective-permute-done | bytes 24608 | tf_op jit(solution)/shard_map/ppermute | solution.py:284
  13.4 0.0 collective-permute-done.2.refs_1_
  13.4 0.2 %shard_map.136.base = f32[320,128]{1,0:T(8,128)S(1)} custom-call(f32[320,128]{1,0:T(8,128)S(1)} %bitcast_add_fusion.before, f32[392,128]{1,0:T(8,128)S(1)} %collective-permute-done.refs_1_.beside.refs_0_, f32[320,128]{1,0:T(8,128)S(1)} %collective-permute-done.2.refs_1_, f32[16,384]{1,0:T(8,128)S(1)} %collective-permute-done.3.refs_2_, ...), custom_call_target="tpu_custom_call" | custom-call | flops 1 | bytes 1 | tf_op jit(solution)/shard_map/pallas_call | solution.py:495
  13.6 0.2 %collective-permute-done.5.refs_0_ = f32[16,384]{1,0:T(8,128)S(1)} collective-permute-done((f32[16,384]{1,0:T(8,128)S(1)}, f32[16,384]{1,0:T(8,128)S(1)}, u32[]{:S(2)}, u32[]{:S(2)}) %collective-permute-start.5) | collective-permute-done | bytes 24608 | tf_op jit(solution)/shard_map/ppermute | solution.py:284
  13.8 0.0 collective-permute-done.6.refs_1_
  13.8 1.0 %shard_map.137 = (f32[320,128]{1,0:T(8,128)}, f32[320,128]{1,0:T(8,128)}) custom-call(f32[320,128]{1,0:T(8,128)S(1)} %shard_map.136.base, f32[2,128]{1,0:T(2,128)S(1)} %pad_maximum_fusion.rows, f32[392,128]{1,0:T(8,128)S(1)} %get-tuple-element.15.refs_0_.state, f32[16,384]{1,0:T(8,128)S(1)} %collective-permute-done.5.refs_0_, ...), custom_call_target="tpu_custom_call" | custom-call | tf_op jit(solution)/shard_map/pallas_call | solution.py:504
  (12 shorter events, 0.1 us)
Async XLA Ops:
  0.6 10.9 %copy-start = (bf16[8,320,320]{2,1,0:T(8,128)(2,1)S(1)}, bf16[8,320,320]{2,1,0:T(8,128)(2,1)}, u32[]{:S(2)}) copy-start(bf16[8,320,320]{2,1,0:T(8,128)(2,1)} %param.14) | copy-start | bytes 4915204
  2.0 3.8 %collective-permute-start = (f32[392,128]{1,0:T(8,128)S(1)}, f32[392,128]{1,0:T(8,128)S(1)}, u32[]{:S(2)}, u32[]{:S(2)}) collective-permute-start(f32[392,128]{1,0:T(8,128)S(1)} %get-tuple-element.15.refs_0_.state), channel_id=1, source_target_pairs={{0,8},{8,0},{16,24},{24,16},{1,9},{9,1},{17,25},{25,17},{2,10},{10... | collective-permute-start | bytes 602120 | tf_op jit(solution)/shard_map/ppermute | solution.py:268
  2.6 4.7 %collective-permute-start.1 = (f32[32,384]{1,0:T(8,128)S(1)}, f32[32,384]{1,0:T(8,128)S(1)}, u32[]{:S(2)}, u32[]{:S(2)}) collective-permute-start(f32[32,384]{1,0:T(8,128)S(1)} %get-tuple-element.16), channel_id=1, source_target_pairs={{0,9},{1,8},{2,11},{3,10},{4,13},{5,12},{6,15},{7,14},{8,1},{9,0},... | collective-permute-start | bytes 147464 | tf_op jit(solution)/shard_map/ppermute | solution.py:284
  5.9 7.5 %collective-permute-start.2 = (f32[320,128]{1,0:T(8,128)S(1)}, f32[320,128]{1,0:T(8,128)S(1)}, u32[]{:S(2)}, u32[]{:S(2)}) collective-permute-start(f32[320,128]{1,0:T(8,128)S(1)} %shard_map.132._), channel_id=1, source_target_pairs={{0,24},{8,16},{16,8},{24,0},{1,25},{9,17},{17,9},{25,1},{2,26},{10... | collective-permute-start | bytes 491528 | tf_op jit(solution)/shard_map/ppermute | solution.py:268
  7.2 5.0 %copy-start.2 = (s32[128,4]{0,1:T(4,128)S(1)}, s32[128,4]{0,1:T(4,128)}, u32[]{:S(2)}) copy-start(s32[128,4]{0,1:T(4,128)} %param.15) | copy-start | bytes 6148
  7.2 5.0 %copy-start.3 = (s32[128,4]{0,1:T(4,128)S(1)}, s32[128,4]{0,1:T(4,128)}, u32[]{:S(2)}) copy-start(s32[128,4]{0,1:T(4,128)} %param.16) | copy-start | bytes 6148
  7.2 5.7 %collective-permute-start.3 = (f32[16,384]{1,0:T(8,128)S(1)}, f32[16,384]{1,0:T(8,128)S(1)}, u32[]{:S(2)}, u32[]{:S(2)}) collective-permute-start(f32[16,384]{1,0:T(8,128)S(1)} %get-tuple-element.22), channel_id=1, source_target_pairs={{0,10},{1,11},{2,14},{3,15},{4,12},{5,13},{6,8},{7,9},{8,2},{9,3},... | collective-permute-start | bytes 73736 | tf_op jit(solution)/shard_map/ppermute | solution.py:284
  8.9 4.5 %collective-permute-start.4 = (f32[16,384]{1,0:T(8,128)S(1)}, f32[16,384]{1,0:T(8,128)S(1)}, u32[]{:S(2)}, u32[]{:S(2)}) collective-permute-start(f32[16,384]{1,0:T(8,128)S(1)} %get-tuple-element.23), channel_id=1, source_target_pairs={{0,12},{1,13},{2,10},{3,11},{4,8},{5,9},{6,14},{7,15},{8,4},{9,5},... | collective-permute-start | bytes 73736 | tf_op jit(solution)/shard_map/ppermute | solution.py:284
  9.9 3.9 %collective-permute-start.5 = (f32[16,384]{1,0:T(8,128)S(1)}, f32[16,384]{1,0:T(8,128)S(1)}, u32[]{:S(2)}, u32[]{:S(2)}) collective-permute-start(f32[16,384]{1,0:T(8,128)S(1)} %get-tuple-element.24), channel_id=1, source_target_pairs={{0,14},{1,15},{2,8},{3,9},{4,10},{5,11},{6,12},{7,13},{8,6},{9,7},... | collective-permute-start | bytes 73736 | tf_op jit(solution)/shard_map/ppermute | solution.py:284
  11.2 2.6 %collective-permute-start.6 = (f32[16,384]{1,0:T(8,128)S(1)}, f32[16,384]{1,0:T(8,128)S(1)}, u32[]{:S(2)}, u32[]{:S(2)}) collective-permute-start(f32[16,384]{1,0:T(8,128)S(1)} %get-tuple-element.25), channel_id=1, source_target_pairs={{0,8},{1,9},{2,12},{3,13},{4,14},{5,15},{6,10},{7,11},{8,0},{9,1},... | collective-permute-start | bytes 73736 | tf_op jit(solution)/shard_map/ppermute | solution.py:284
  11.5 1.4 %copy-start.1 = (f32[1,128,320]{1,2,0:T(8,128)S(1)}, f32[1,128,320]{1,2,0:T(8,128)}, u32[]{:S(2)}) copy-start(f32[1,128,320]{1,2,0:T(8,128)} %param.13) | copy-start | bytes 491524
  11.5 1.4 %copy-start.4 = (f32[1,128]{1,0:T(1,128)S(1)}, f32[1,128]{1,0:T(1,128)}, u32[]{:S(2)}) copy-start(f32[1,128]{1,0:T(1,128)} %param.17) | copy-start | bytes 1540

commit v10 on v9

--- a/solution.py
+++ b/solution.py
@@ -42,10 +42,7 @@
 
 def parts_of(value):
     high = value.astype(jnp.bfloat16)
-    rest = value - high.astype(jnp.float32)
-    middle = rest.astype(jnp.bfloat16)
-    low = (rest - middle.astype(jnp.float32)).astype(jnp.bfloat16)
-    return high, middle, low
+    return high, (value - high.astype(jnp.float32)).astype(jnp.bfloat16)
 
 
 def power_of_two(count):
@@ -160,7 +157,7 @@
         scales = scales + jnp.dot(choose, part, preferred_element_type=jnp.float32)
     parts = jnp.concatenate(parts_of(state[pl.ds(0, width), :]), axis=1)
     picked = lax.dot_general(
-        jnp.concatenate([pick, pick, pick], axis=1),
+        jnp.concatenate([pick, pick], axis=1),
         parts,
         (((1,), (1,)), ((), ())),
         preferred_element_type=jnp.float32,
@@ -194,7 +191,7 @@
     landing = jnp.where(landing, 1.0, 0.0).astype(jnp.bfloat16)
     return lax.dot_general(
         jnp.concatenate(parts_of(arrived), axis=0),
-        jnp.concatenate([landing, landing, landing], axis=0),
+        jnp.concatenate([landing, landing], axis=0),
         (((0,), (0,)), ((), ())),
         preferred_element_type=jnp.float32,
     )[:width]

time: 14.9 us -> 14.9 us (level)
  no operation moved by 1% of the time
where the time goes in v10:
time: 14.9 us; the launch traced here: 14.7 us
  starting transfers between devices  8.6 us (58%)
  Pallas kernels  3.22 us (22%)
  between operations  1.43 us (10%)
  waiting for transfers between devices  0.74 us (5%)
  matrix products  0.67 us (4%)
    ppermute x5, starting transfers between devices, stage_sent(): held.append(lax.ppermute(sends[which], ('inst', 'zone'), pairs))  6.86 us
    ppermute x2, starting transfers between devices, moved(): lax.ppermute(value, axis, [(place, place ^ mask) for place in range(count)])  1.74 us
    pallas_call x1, Pallas kernels, on_device(): pl.pallas_call(functools.partial(outgoing_kernel, stages, slots_per, widt...  1.34 us
    pallas_call x1, Pallas kernels, on_device(): pl.pallas_call(final_kernel, out_shape=(block, block), in_specs=[VMEM] *...  0.96 us
    ppermute x5, waiting for transfers between devices, stage_sent(): held.append(lax.ppermute(sends[which], ('inst', 'zone'), pairs))  0.73 us
    dot_general x1, matrix products, on_device(): lax.dot_general(jac_table.reshape(kinds * width, width), half, (((1,), (0...  0.67 us
    pallas_call x1, Pallas kernels, on_device(): pl.pallas_call(local_kernel, out_shape=block, in_specs=[VMEM] * 4, out_sp...  0.61 us
  transfers between devices with their start and end apart: 7, of which 3 were waited for; matrix products, arithmetic and copies ran while one was open for 5% of the time, Pallas kernels for 6%

profile of v10, /device:TPU:0, one launch (start us, length us, event | category | flops | bytes accessed | tf_op | source)
XLA Modules:
  0.0 14.7 jit_solution(1333621930006025128)
XLA Ops:
  0.6 0.0 copy-start
  0.6 1.3 %shard_map.131 = (f32[392,128]{1,0:T(8,128)S(1)}, f32[8,384]{1,0:T(8,128)S(1)}, f32[32,384]{1,0:T(8,128)S(1)}) custom-call(f32[320,128]{1,0:T(8,128)} %bitcast.24, s32[1,32]{1,0:T(1,128)} %source_in.1, s32[1,32]{1,0:T(1,128)} %bitcast.25, s32[1,32]{1,0:T(1,128)} %dest_in.1, s32[1,32]{1,0:T(1,128)} %weight_in.1, f32[16,320]{1,0:T(8,128)} %table_in.1), custom_call_target="tpu_custom_call" | custom-call | tf_op jit(solution)/shard_map/pallas_call | solution.py:410
  2.0 0.5 %collective-permute-start = (f32[392,128]{1,0:T(8,128)S(1)}, f32[392,128]{1,0:T(8,128)S(1)}, u32[]{:S(2)}, u32[]{:S(2)}) collective-permute-start(f32[392,128]{1,0:T(8,128)S(1)} %get-tuple-element.15.refs_0_.state), channel_id=1, source_target_pairs={{0,8},{8,0},{16,24},{24,16},{1,9},{9,1},{17,25},{25,17},{2,10},{10... | collective-permute-start | bytes 602120 | tf_op jit(solution)/shard_map/ppermute | solution.py:265
  2.5 2.6 %collective-permute-start.1 = (f32[32,384]{1,0:T(8,128)S(1)}, f32[32,384]{1,0:T(8,128)S(1)}, u32[]{:S(2)}, u32[]{:S(2)}) collective-permute-start(f32[32,384]{1,0:T(8,128)S(1)} %get-tuple-element.16), channel_id=1, source_target_pairs={{0,9},{1,8},{2,11},{3,10},{4,13},{5,12},{6,15},{7,14},{8,1},{9,0},... | collective-permute-start | bytes 147464 | tf_op jit(solution)/shard_map/ppermute | solution.py:281
  5.8 0.0 collective-permute-done.refs_1_.beside.refs_0_
  5.9 1.2 %collective-permute-start.2 = (f32[320,128]{1,0:T(8,128)S(1)}, f32[320,128]{1,0:T(8,128)S(1)}, u32[]{:S(2)}, u32[]{:S(2)}) collective-permute-start(f32[320,128]{1,0:T(8,128)S(1)} %shard_map.132._), channel_id=1, source_target_pairs={{0,24},{8,16},{16,8},{24,0},{1,25},{9,17},{17,9},{25,1},{2,26},{10... | collective-permute-start | bytes 491528 | tf_op jit(solution)/shard_map/ppermute | solution.py:265
  7.1 0.1 collective-permute-done.1.came
  7.2 1.6 %collective-permute-start.3 = (f32[16,384]{1,0:T(8,128)S(1)}, f32[16,384]{1,0:T(8,128)S(1)}, u32[]{:S(2)}, u32[]{:S(2)}) collective-permute-start(f32[16,384]{1,0:T(8,128)S(1)} %get-tuple-element.22), channel_id=1, source_target_pairs={{0,10},{1,11},{2,14},{3,15},{4,12},{5,13},{6,8},{7,9},{8,2},{9,3},... | collective-permute-start | bytes 73736 | tf_op jit(solution)/shard_map/ppermute | solution.py:281
  8.8 1.1 %collective-permute-start.4 = (f32[16,384]{1,0:T(8,128)S(1)}, f32[16,384]{1,0:T(8,128)S(1)}, u32[]{:S(2)}, u32[]{:S(2)}) collective-permute-start(f32[16,384]{1,0:T(8,128)S(1)} %get-tuple-element.23), channel_id=1, source_target_pairs={{0,12},{1,13},{2,10},{3,11},{4,8},{5,9},{6,14},{7,15},{8,4},{9,5},... | collective-permute-start | bytes 73736 | tf_op jit(solution)/shard_map/ppermute | solution.py:281
  9.9 1.3 %collective-permute-start.5 = (f32[16,384]{1,0:T(8,128)S(1)}, f32[16,384]{1,0:T(8,128)S(1)}, u32[]{:S(2)}, u32[]{:S(2)}) collective-permute-start(f32[16,384]{1,0:T(8,128)S(1)} %get-tuple-element.24), channel_id=1, source_target_pairs={{0,14},{1,15},{2,8},{3,9},{4,10},{5,11},{6,12},{7,13},{8,6},{9,7},... | collective-permute-start | bytes 73736 | tf_op jit(solution)/shard_map/ppermute | solution.py:281
  11.2 0.3 %collective-permute-start.6 = (f32[16,384]{1,0:T(8,128)S(1)}, f32[16,384]{1,0:T(8,128)S(1)}, u32[]{:S(2)}, u32[]{:S(2)}) collective-permute-start(f32[16,384]{1,0:T(8,128)S(1)} %get-tuple-element.25), channel_id=1, source_target_pairs={{0,8},{1,9},{2,12},{3,13},{4,14},{5,15},{6,10},{7,11},{8,0},{9,1},... | collective-permute-start | bytes 73736 | tf_op jit(solution)/shard_map/ppermute | solution.py:281
  11.4 0.0 copy-done
  11.5 0.0 copy-start.1
  11.5 0.0 copy-start.4
  11.5 0.7 %convolution_bitcast_fusion.products = f32[2560,128]{1,0:T(8,128)S(1)} fusion(bf16[2560,320]{1,0:T(8,128)(2,1)S(1)} %bitcast.23, bf16[320,128]{1,0:T(8,128)(2,1)S(1)} %get-tuple-element.21), kind=kOutput, calls=%fused_computation | convolution fusion | flops 209715200 | bytes 3031040 | tf_op jit(solution)/shard_map/dot_general | solution.py:471
  12.2 0.0 copy-done.2
  12.2 0.6 %shard_map.135 = f32[320,128]{1,0:T(8,128)S(1)} custom-call(s32[4,128]{1,0:T(4,128)S(1)} %bitcast_add_fusion.1.codes, f32[320,128]{1,0:T(8,128)S(1)} %get-tuple-element.20.own, f32[2560,128]{1,0:T(8,128)S(1)} %convolution_bitcast_fusion.products, f32[8,384]{1,0:T(8,128)S(1)} %get-tuple-element.18._.staying), custom_call_target="tpu_custom_call" | custom-call | flops 1 | bytes 1 | tf_op jit(solution)/shard_map/pallas_call | solution.py:481
  12.9 0.0 collective-permute-done.3.refs_2_
  12.9 0.4 %collective-permute-done.4.refs_3_ = f32[16,384]{1,0:T(8,128)S(1)} collective-permute-done((f32[16,384]{1,0:T(8,128)S(1)}, f32[16,384]{1,0:T(8,128)S(1)}, u32[]{:S(2)}, u32[]{:S(2)}) %collective-permute-start.4) | collective-permute-done | bytes 24608 | tf_op jit(solution)/shard_map/ppermute | solution.py:281
  13.3 0.0 collective-permute-done.2.refs_1_
  13.3 0.2 %shard_map.136.base = f32[320,128]{1,0:T(8,128)S(1)} custom-call(f32[320,128]{1,0:T(8,128)S(1)} %bitcast_add_fusion.before, f32[392,128]{1,0:T(8,128)S(1)} %collective-permute-done.refs_1_.beside.refs_0_, f32[320,128]{1,0:T(8,128)S(1)} %collective-permute-done.2.refs_1_, f32[16,384]{1,0:T(8,128)S(1)} %collective-permute-done.3.refs_2_, ...), custom_call_target="tpu_custom_call" | custom-call | flops 1 | bytes 1 | tf_op jit(solution)/shard_map/pallas_call | solution.py:492
  13.6 0.2 %collective-permute-done.5.refs_0_ = f32[16,384]{1,0:T(8,128)S(1)} collective-permute-done((f32[16,384]{1,0:T(8,128)S(1)}, f32[16,384]{1,0:T(8,128)S(1)}, u32[]{:S(2)}, u32[]{:S(2)}) %collective-permute-start.5) | collective-permute-done | bytes 24608 | tf_op jit(solution)/shard_map/ppermute | solution.py:281
  13.8 0.0 collective-permute-done.6.refs_1_
  13.8 1.0 %shard_map.137 = (f32[320,128]{1,0:T(8,128)}, f32[320,128]{1,0:T(8,128)}) custom-call(f32[320,128]{1,0:T(8,128)S(1)} %shard_map.136.base, f32[2,128]{1,0:T(2,128)S(1)} %pad_maximum_fusion.rows, f32[392,128]{1,0:T(8,128)S(1)} %get-tuple-element.15.refs_0_.state, f32[16,384]{1,0:T(8,128)S(1)} %collective-permute-done.5.refs_0_, ...), custom_call_target="tpu_custom_call" | custom-call | tf_op jit(solution)/shard_map/pallas_call | solution.py:501
  (12 shorter events, 0.1 us)
Async XLA Ops:
  0.6 10.8 %copy-start = (bf16[8,320,320]{2,1,0:T(8,128)(2,1)S(1)}, bf16[8,320,320]{2,1,0:T(8,128)(2,1)}, u32[]{:S(2)}) copy-start(bf16[8,320,320]{2,1,0:T(8,128)(2,1)} %param.14) | copy-start | bytes 4915204
  2.0 3.8 %collective-permute-start = (f32[392,128]{1,0:T(8,128)S(1)}, f32[392,128]{1,0:T(8,128)S(1)}, u32[]{:S(2)}, u32[]{:S(2)}) collective-permute-start(f32[392,128]{1,0:T(8,128)S(1)} %get-tuple-element.15.refs_0_.state), channel_id=1, source_target_pairs={{0,8},{8,0},{16,24},{24,16},{1,9},{9,1},{17,25},{25,17},{2,10},{10... | collective-permute-start | bytes 602120 | tf_op jit(solution)/shard_map/ppermute | solution.py:265
  2.5 4.7 %collective-permute-start.1 = (f32[32,384]{1,0:T(8,128)S(1)}, f32[32,384]{1,0:T(8,128)S(1)}, u32[]{:S(2)}, u32[]{:S(2)}) collective-permute-start(f32[32,384]{1,0:T(8,128)S(1)} %get-tuple-element.16), channel_id=1, source_target_pairs={{0,9},{1,8},{2,11},{3,10},{4,13},{5,12},{6,15},{7,14},{8,1},{9,0},... | collective-permute-start | bytes 147464 | tf_op jit(solution)/shard_map/ppermute | solution.py:281
  5.9 7.5 %collective-permute-start.2 = (f32[320,128]{1,0:T(8,128)S(1)}, f32[320,128]{1,0:T(8,128)S(1)}, u32[]{:S(2)}, u32[]{:S(2)}) collective-permute-start(f32[320,128]{1,0:T(8,128)S(1)} %shard_map.132._), channel_id=1, source_target_pairs={{0,24},{8,16},{16,8},{24,0},{1,25},{9,17},{17,9},{25,1},{2,26},{10... | collective-permute-start | bytes 491528 | tf_op jit(solution)/shard_map/ppermute | solution.py:265
  7.2 5.0 %copy-start.2 = (s32[128,4]{0,1:T(4,128)S(1)}, s32[128,4]{0,1:T(4,128)}, u32[]{:S(2)}) copy-start(s32[128,4]{0,1:T(4,128)} %param.15) | copy-start | bytes 6148
  7.2 5.0 %copy-start.3 = (s32[128,4]{0,1:T(4,128)S(1)}, s32[128,4]{0,1:T(4,128)}, u32[]{:S(2)}) copy-start(s32[128,4]{0,1:T(4,128)} %param.16) | copy-start | bytes 6148
  7.2 5.7 %collective-permute-start.3 = (f32[16,384]{1,0:T(8,128)S(1)}, f32[16,384]{1,0:T(8,128)S(1)}, u32[]{:S(2)}, u32[]{:S(2)}) collective-permute-start(f32[16,384]{1,0:T(8,128)S(1)} %get-tuple-element.22), channel_id=1, source_target_pairs={{0,10},{1,11},{2,14},{3,15},{4,12},{5,13},{6,8},{7,9},{8,2},{9,3},... | collective-permute-start | bytes 73736 | tf_op jit(solution)/shard_map/ppermute | solution.py:281
  8.8 4.5 %collective-permute-start.4 = (f32[16,384]{1,0:T(8,128)S(1)}, f32[16,384]{1,0:T(8,128)S(1)}, u32[]{:S(2)}, u32[]{:S(2)}) collective-permute-start(f32[16,384]{1,0:T(8,128)S(1)} %get-tuple-element.23), channel_id=1, source_target_pairs={{0,12},{1,13},{2,10},{3,11},{4,8},{5,9},{6,14},{7,15},{8,4},{9,5},... | collective-permute-start | bytes 73736 | tf_op jit(solution)/shard_map/ppermute | solution.py:281
  9.9 3.9 %collective-permute-start.5 = (f32[16,384]{1,0:T(8,128)S(1)}, f32[16,384]{1,0:T(8,128)S(1)}, u32[]{:S(2)}, u32[]{:S(2)}) collective-permute-start(f32[16,384]{1,0:T(8,128)S(1)} %get-tuple-element.24), channel_id=1, source_target_pairs={{0,14},{1,15},{2,8},{3,9},{4,10},{5,11},{6,12},{7,13},{8,6},{9,7},... | collective-permute-start | bytes 73736 | tf_op jit(solution)/shard_map/ppermute | solution.py:281
  11.2 2.6 %collective-permute-start.6 = (f32[16,384]{1,0:T(8,128)S(1)}, f32[16,384]{1,0:T(8,128)S(1)}, u32[]{:S(2)}, u32[]{:S(2)}) collective-permute-start(f32[16,384]{1,0:T(8,128)S(1)} %get-tuple-element.25), channel_id=1, source_target_pairs={{0,8},{1,9},{2,12},{3,13},{4,14},{5,15},{6,10},{7,11},{8,0},{9,1},... | collective-permute-start | bytes 73736 | tf_op jit(solution)/shard_map/ppermute | solution.py:281
  11.5 1.4 %copy-start.1 = (f32[1,128,320]{1,2,0:T(8,128)S(1)}, f32[1,128,320]{1,2,0:T(8,128)}, u32[]{:S(2)}) copy-start(f32[1,128,320]{1,2,0:T(8,128)} %param.13) | copy-start | bytes 491524
  11.5 1.4 %copy-start.4 = (f32[1,128]{1,0:T(1,128)S(1)}, f32[1,128]{1,0:T(1,128)}, u32[]{:S(2)}) copy-start(f32[1,128]{1,0:T(1,128)} %param.17) | copy-start | bytes 1540

commit v11 on v10

--- a/solution.py
+++ b/solution.py
@@ -186,8 +186,9 @@
     if short:
         arrived.append(jnp.zeros((short, arrived[0].shape[1]), jnp.float32))
     arrived = jnp.concatenate(arrived, axis=0)
-    target = arrived[:, width : width + 1].astype(jnp.int32)
-    landing = lax.broadcasted_iota(jnp.int32, (arrived.shape[0], clusters), 1) == target
+    target = arrived[:, width : width + 1]
+    cluster = lax.broadcasted_iota(jnp.int32, (arrived.shape[0], clusters), 1)
+    landing = cluster.astype(jnp.float32) == target
     landing = jnp.where(landing, 1.0, 0.0).astype(jnp.bfloat16)
     return lax.dot_general(
         jnp.concatenate(parts_of(arrived), axis=0),

time: 14.9 us -> 14.9 us (level)
  no operation moved by 1% of the time
where the time goes in v11:
time: 14.9 us; the launch traced here: 14.7 us
  starting transfers between devices  8.6 us (58%)
  Pallas kernels  3.21 us (22%)
  between operations  1.44 us (10%)
  waiting for transfers between devices  0.74 us (5%)
  matrix products  0.67 us (4%)
    ppermute x5, starting transfers between devices, stage_sent(): held.append(lax.ppermute(sends[which], ('inst', 'zone'), pairs))  6.86 us
    ppermute x2, starting transfers between devices, moved(): lax.ppermute(value, axis, [(place, place ^ mask) for place in range(count)])  1.74 us
    pallas_call x1, Pallas kernels, on_device(): pl.pallas_call(functools.partial(outgoing_kernel, stages, slots_per, widt...  1.34 us
    pallas_call x1, Pallas kernels, on_device(): pl.pallas_call(final_kernel, out_shape=(block, block), in_specs=[VMEM] *...  0.95 us
    ppermute x5, waiting for transfers between devices, stage_sent(): held.append(lax.ppermute(sends[which], ('inst', 'zone'), pairs))  0.74 us
    dot_general x1, matrix products, on_device(): lax.dot_general(jac_table.reshape(kinds * width, width), half, (((1,), (0...  0.67 us
    pallas_call x1, Pallas kernels, on_device(): pl.pallas_call(local_kernel, out_shape=block, in_specs=[VMEM] * 4, out_sp...  0.61 us
  transfers between devices with their start and end apart: 7, of which 3 were waited for; matrix products, arithmetic and copies ran while one was open for 5% of the time, Pallas kernels for 6%

profile of v11, /device:TPU:0, one launch (start us, length us, event | category | flops | bytes accessed | tf_op | source)
XLA Modules:
  0.0 14.7 jit_solution(16218479703591524661)
XLA Ops:
  0.6 0.0 copy-start
  0.6 1.3 %shard_map.131 = (f32[392,128]{1,0:T(8,128)S(1)}, f32[8,384]{1,0:T(8,128)S(1)}, f32[32,384]{1,0:T(8,128)S(1)}) custom-call(f32[320,128]{1,0:T(8,128)} %bitcast.24, s32[1,32]{1,0:T(1,128)} %source_in.1, s32[1,32]{1,0:T(1,128)} %bitcast.25, s32[1,32]{1,0:T(1,128)} %dest_in.1, s32[1,32]{1,0:T(1,128)} %weight_in.1, f32[16,320]{1,0:T(8,128)} %table_in.1), custom_call_target="tpu_custom_call" | custom-call | tf_op jit(solution)/shard_map/pallas_call | solution.py:411
  2.0 0.5 %collective-permute-start = (f32[392,128]{1,0:T(8,128)S(1)}, f32[392,128]{1,0:T(8,128)S(1)}, u32[]{:S(2)}, u32[]{:S(2)}) collective-permute-start(f32[392,128]{1,0:T(8,128)S(1)} %get-tuple-element.15.refs_0_.state), channel_id=1, source_target_pairs={{0,8},{8,0},{16,24},{24,16},{1,9},{9,1},{17,25},{25,17},{2,10},{10... | collective-permute-start | bytes 602120 | tf_op jit(solution)/shard_map/ppermute | solution.py:266
  2.5 2.6 %collective-permute-start.1 = (f32[32,384]{1,0:T(8,128)S(1)}, f32[32,384]{1,0:T(8,128)S(1)}, u32[]{:S(2)}, u32[]{:S(2)}) collective-permute-start(f32[32,384]{1,0:T(8,128)S(1)} %get-tuple-element.16), channel_id=1, source_target_pairs={{0,9},{1,8},{2,11},{3,10},{4,13},{5,12},{6,15},{7,14},{8,1},{9,0},... | collective-permute-start | bytes 147464 | tf_op jit(solution)/shard_map/ppermute | solution.py:282
  5.8 0.0 collective-permute-done.refs_1_.beside.refs_0_
  5.9 1.2 %collective-permute-start.2 = (f32[320,128]{1,0:T(8,128)S(1)}, f32[320,128]{1,0:T(8,128)S(1)}, u32[]{:S(2)}, u32[]{:S(2)}) collective-permute-start(f32[320,128]{1,0:T(8,128)S(1)} %shard_map.132._), channel_id=1, source_target_pairs={{0,24},{8,16},{16,8},{24,0},{1,25},{9,17},{17,9},{25,1},{2,26},{10... | collective-permute-start | bytes 491528 | tf_op jit(solution)/shard_map/ppermute | solution.py:266
  7.1 0.1 collective-permute-done.1.came
  7.2 1.6 %collective-permute-start.3 = (f32[16,384]{1,0:T(8,128)S(1)}, f32[16,384]{1,0:T(8,128)S(1)}, u32[]{:S(2)}, u32[]{:S(2)}) collective-permute-start(f32[16,384]{1,0:T(8,128)S(1)} %get-tuple-element.22), channel_id=1, source_target_pairs={{0,10},{1,11},{2,14},{3,15},{4,12},{5,13},{6,8},{7,9},{8,2},{9,3},... | collective-permute-start | bytes 73736 | tf_op jit(solution)/shard_map/ppermute | solution.py:282
  8.8 1.1 %collective-permute-start.4 = (f32[16,384]{1,0:T(8,128)S(1)}, f32[16,384]{1,0:T(8,128)S(1)}, u32[]{:S(2)}, u32[]{:S(2)}) collective-permute-start(f32[16,384]{1,0:T(8,128)S(1)} %get-tuple-element.23), channel_id=1, source_target_pairs={{0,12},{1,13},{2,10},{3,11},{4,8},{5,9},{6,14},{7,15},{8,4},{9,5},... | collective-permute-start | bytes 73736 | tf_op jit(solution)/shard_map/ppermute | solution.py:282
  9.9 1.3 %collective-permute-start.5 = (f32[16,384]{1,0:T(8,128)S(1)}, f32[16,384]{1,0:T(8,128)S(1)}, u32[]{:S(2)}, u32[]{:S(2)}) collective-permute-start(f32[16,384]{1,0:T(8,128)S(1)} %get-tuple-element.24), channel_id=1, source_target_pairs={{0,14},{1,15},{2,8},{3,9},{4,10},{5,11},{6,12},{7,13},{8,6},{9,7},... | collective-permute-start | bytes 73736 | tf_op jit(solution)/shard_map/ppermute | solution.py:282
  11.2 0.3 %collective-permute-start.6 = (f32[16,384]{1,0:T(8,128)S(1)}, f32[16,384]{1,0:T(8,128)S(1)}, u32[]{:S(2)}, u32[]{:S(2)}) collective-permute-start(f32[16,384]{1,0:T(8,128)S(1)} %get-tuple-element.25), channel_id=1, source_target_pairs={{0,8},{1,9},{2,12},{3,13},{4,14},{5,15},{6,10},{7,11},{8,0},{9,1},... | collective-permute-start | bytes 73736 | tf_op jit(solution)/shard_map/ppermute | solution.py:282
  11.4 0.0 copy-done
  11.5 0.0 copy-start.1
  11.5 0.0 copy-start.4
  11.5 0.7 %convolution_bitcast_fusion.products = f32[2560,128]{1,0:T(8,128)S(1)} fusion(bf16[2560,320]{1,0:T(8,128)(2,1)S(1)} %bitcast.23, bf16[320,128]{1,0:T(8,128)(2,1)S(1)} %get-tuple-element.21), kind=kOutput, calls=%fused_computation | convolution fusion | flops 209715200 | bytes 3031040 | tf_op jit(solution)/shard_map/dot_general | solution.py:472
  12.2 0.6 %shard_map.135 = f32[320,128]{1,0:T(8,128)S(1)} custom-call(s32[4,128]{1,0:T(4,128)S(1)} %bitcast_add_fusion.1.codes, f32[320,128]{1,0:T(8,128)S(1)} %get-tuple-element.20.own, f32[2560,128]{1,0:T(8,128)S(1)} %convolution_bitcast_fusion.products, f32[8,384]{1,0:T(8,128)S(1)} %get-tuple-element.18._.staying), custom_call_target="tpu_custom_call" | custom-call | flops 1 | bytes 1 | tf_op jit(solution)/shard_map/pallas_call | solution.py:482
  12.8 0.0 copy-done.4
  12.9 0.0 collective-permute-done.3.refs_2_
  12.9 0.4 %collective-permute-done.4.refs_3_ = f32[16,384]{1,0:T(8,128)S(1)} collective-permute-done((f32[16,384]{1,0:T(8,128)S(1)}, f32[16,384]{1,0:T(8,128)S(1)}, u32[]{:S(2)}, u32[]{:S(2)}) %collective-permute-start.4) | collective-permute-done | bytes 24608 | tf_op jit(solution)/shard_map/ppermute | solution.py:282
  13.3 0.0 collective-permute-done.2.refs_1_
  13.3 0.2 %shard_map.136.base = f32[320,128]{1,0:T(8,128)S(1)} custom-call(f32[320,128]{1,0:T(8,128)S(1)} %bitcast_add_fusion.before, f32[392,128]{1,0:T(8,128)S(1)} %collective-permute-done.refs_1_.beside.refs_0_, f32[320,128]{1,0:T(8,128)S(1)} %collective-permute-done.2.refs_1_, f32[16,384]{1,0:T(8,128)S(1)} %collective-permute-done.3.refs_2_, ...), custom_call_target="tpu_custom_call" | custom-call | flops 1 | bytes 1 | tf_op jit(solution)/shard_map/pallas_call | solution.py:493
  13.6 0.2 %collective-permute-done.5.refs_0_ = f32[16,384]{1,0:T(8,128)S(1)} collective-permute-done((f32[16,384]{1,0:T(8,128)S(1)}, f32[16,384]{1,0:T(8,128)S(1)}, u32[]{:S(2)}, u32[]{:S(2)}) %collective-permute-start.5) | collective-permute-done | bytes 24608 | tf_op jit(solution)/shard_map/ppermute | solution.py:282
  13.8 0.0 collective-permute-done.6.refs_1_
  13.8 1.0 %shard_map.137 = (f32[320,128]{1,0:T(8,128)}, f32[320,128]{1,0:T(8,128)}) custom-call(f32[320,128]{1,0:T(8,128)S(1)} %shard_map.136.base, f32[2,128]{1,0:T(2,128)S(1)} %pad_maximum_fusion.rows, f32[392,128]{1,0:T(8,128)S(1)} %get-tuple-element.15.refs_0_.state, f32[16,384]{1,0:T(8,128)S(1)} %collective-permute-done.5.refs_0_, ...), custom_call_target="tpu_custom_call" | custom-call | tf_op jit(solution)/shard_map/pallas_call | solution.py:502
  (12 shorter events, 0.1 us)
Async XLA Ops:
  0.6 10.8 %copy-start = (bf16[8,320,320]{2,1,0:T(8,128)(2,1)S(1)}, bf16[8,320,320]{2,1,0:T(8,128)(2,1)}, u32[]{:S(2)}) copy-start(bf16[8,320,320]{2,1,0:T(8,128)(2,1)} %param.14) | copy-start | bytes 4915204
  2.0 3.8 %collective-permute-start = (f32[392,128]{1,0:T(8,128)S(1)}, f32[392,128]{1,0:T(8,128)S(1)}, u32[]{:S(2)}, u32[]{:S(2)}) collective-permute-start(f32[392,128]{1,0:T(8,128)S(1)} %get-tuple-element.15.refs_0_.state), channel_id=1, source_target_pairs={{0,8},{8,0},{16,24},{24,16},{1,9},{9,1},{17,25},{25,17},{2,10},{10... | collective-permute-start | bytes 602120 | tf_op jit(solution)/shard_map/ppermute | solution.py:266
  2.5 4.7 %collective-permute-start.1 = (f32[32,384]{1,0:T(8,128)S(1)}, f32[32,384]{1,0:T(8,128)S(1)}, u32[]{:S(2)}, u32[]{:S(2)}) collective-permute-start(f32[32,384]{1,0:T(8,128)S(1)} %get-tuple-element.16), channel_id=1, source_target_pairs={{0,9},{1,8},{2,11},{3,10},{4,13},{5,12},{6,15},{7,14},{8,1},{9,0},... | collective-permute-start | bytes 147464 | tf_op jit(solution)/shard_map/ppermute | solution.py:282
  5.9 7.5 %collective-permute-start.2 = (f32[320,128]{1,0:T(8,128)S(1)}, f32[320,128]{1,0:T(8,128)S(1)}, u32[]{:S(2)}, u32[]{:S(2)}) collective-permute-start(f32[320,128]{1,0:T(8,128)S(1)} %shard_map.132._), channel_id=1, source_target_pairs={{0,24},{8,16},{16,8},{24,0},{1,25},{9,17},{17,9},{25,1},{2,26},{10... | collective-permute-start | bytes 491528 | tf_op jit(solution)/shard_map/ppermute | solution.py:266
  7.2 5.0 %copy-start.2 = (s32[128,4]{0,1:T(4,128)S(1)}, s32[128,4]{0,1:T(4,128)}, u32[]{:S(2)}) copy-start(s32[128,4]{0,1:T(4,128)} %param.15) | copy-start | bytes 6148
  7.2 5.0 %copy-start.3 = (s32[128,4]{0,1:T(4,128)S(1)}, s32[128,4]{0,1:T(4,128)}, u32[]{:S(2)}) copy-start(s32[128,4]{0,1:T(4,128)} %param.16) | copy-start | bytes 6148
  7.2 5.7 %collective-permute-start.3 = (f32[16,384]{1,0:T(8,128)S(1)}, f32[16,384]{1,0:T(8,128)S(1)}, u32[]{:S(2)}, u32[]{:S(2)}) collective-permute-start(f32[16,384]{1,0:T(8,128)S(1)} %get-tuple-element.22), channel_id=1, source_target_pairs={{0,10},{1,11},{2,14},{3,15},{4,12},{5,13},{6,8},{7,9},{8,2},{9,3},... | collective-permute-start | bytes 73736 | tf_op jit(solution)/shard_map/ppermute | solution.py:282
  8.8 4.5 %collective-permute-start.4 = (f32[16,384]{1,0:T(8,128)S(1)}, f32[16,384]{1,0:T(8,128)S(1)}, u32[]{:S(2)}, u32[]{:S(2)}) collective-permute-start(f32[16,384]{1,0:T(8,128)S(1)} %get-tuple-element.23), channel_id=1, source_target_pairs={{0,12},{1,13},{2,10},{3,11},{4,8},{5,9},{6,14},{7,15},{8,4},{9,5},... | collective-permute-start | bytes 73736 | tf_op jit(solution)/shard_map/ppermute | solution.py:282
  9.9 3.9 %collective-permute-start.5 = (f32[16,384]{1,0:T(8,128)S(1)}, f32[16,384]{1,0:T(8,128)S(1)}, u32[]{:S(2)}, u32[]{:S(2)}) collective-permute-start(f32[16,384]{1,0:T(8,128)S(1)} %get-tuple-element.24), channel_id=1, source_target_pairs={{0,14},{1,15},{2,8},{3,9},{4,10},{5,11},{6,12},{7,13},{8,6},{9,7},... | collective-permute-start | bytes 73736 | tf_op jit(solution)/shard_map/ppermute | solution.py:282
  11.2 2.6 %collective-permute-start.6 = (f32[16,384]{1,0:T(8,128)S(1)}, f32[16,384]{1,0:T(8,128)S(1)}, u32[]{:S(2)}, u32[]{:S(2)}) collective-permute-start(f32[16,384]{1,0:T(8,128)S(1)} %get-tuple-element.25), channel_id=1, source_target_pairs={{0,8},{1,9},{2,12},{3,13},{4,14},{5,15},{6,10},{7,11},{8,0},{9,1},... | collective-permute-start | bytes 73736 | tf_op jit(solution)/shard_map/ppermute | solution.py:282
  11.5 1.3 %copy-start.1 = (f32[1,128,320]{1,2,0:T(8,128)S(1)}, f32[1,128,320]{1,2,0:T(8,128)}, u32[]{:S(2)}) copy-start(f32[1,128,320]{1,2,0:T(8,128)} %param.13) | copy-start | bytes 491524
  11.5 1.4 %copy-start.4 = (f32[1,128]{1,0:T(1,128)S(1)}, f32[1,128]{1,0:T(1,128)}, u32[]{:S(2)}) copy-start(f32[1,128]{1,0:T(1,128)} %param.17) | copy-start | bytes 1540
